TPU v7x, 512 devices: a whole 4x8x8 slice. The times are simulated.
512 devices in a mesh: dp: 32 (over x_lo, z, core), tensor: 16 (over y, x_hi).
Axes of the slice: x: 4 (x_hi: 2, x_lo: 2; x = x_hi * 2 + x_lo), y: 8, z: 8, core: 2. Of those that a mesh axis runs over, the one named last changes fastest.
Arguments:
- teacher_hidden: bfloat16 [65536, 8192], P('dp', 'tensor'), may hold values from -6 to 6
- teacher_gain: bfloat16 [8192], P('tensor'), may hold values from 0.5 to 1.5
- student_hidden: bfloat16 [65536, 2048], P(('dp', 'tensor')), may hold values from -6 to 6
- student_gain: float32 [2048], replicated, may hold values from 0.5 to 1.5
- projection: bfloat16 [2048, 8192], P('dp', 'tensor'), may hold values from -0.125 to 0.125
- lengths: int32 [32], P('dp'), may hold values from 1 to 2048, as said below
Outputs:
- loss: float32 [], replicated
- grad_gain: float32 [2048], replicated
- grad_proj: float32 [2048, 8192], P('dp', 'tensor')
Inputs may be any that keep to these rules, and one draw needn't show every extreme that they name: `lengths`: one sequence has exactly 2048 valid positions.
All inputs are finite; a program needn't handle non-finite values.
Results may differ from a plain program's by a relative error of at most 0.002.
Values may be sent and summed in bfloat16 or wider, within the bound.
No kernel may reach another device: no remote copies, remote signals or barrier semaphores. Data moves between devices by JAX's collectives and lax.ppermute only.
A program may use at most 64 MiB of HBM per device.

v0:
```python
import jax
import jax.numpy as jnp
from jax import lax
from jax.sharding import PartitionSpec as P

TW = 8192


epsilon = 1e-06


def on_device(teacher_hidden, teacher_gain, student_hidden, student_gain, projection, lengths):
    hidden_f = teacher_hidden.astype(jnp.float32)
    row_squares = lax.psum(jnp.sum(hidden_f * hidden_f, axis=1), "tensor")
    target = (
        hidden_f * lax.rsqrt(row_squares[:, None] / TW + epsilon) * teacher_gain.astype(jnp.float32)
    )
    count = lax.psum(lengths.astype(jnp.float32), "dp")[0]
    student_f = student_hidden.astype(jnp.float32)
    normed = student_f * lax.rsqrt(jnp.mean(student_f * student_f, axis=1, keepdims=True) + epsilon)
    scaled = (normed * student_gain).astype(jnp.bfloat16)
    proj_full = lax.all_gather(projection, "dp", axis=0, tiled=True)
    length_here = lengths[0]
    factor = 2.0 / count
    block_rows = lax.all_gather(scaled, "tensor", axis=0, tiled=True)
    row_count = block_rows.shape[0]
    predicted = jnp.dot(block_rows, proj_full, preferred_element_type=jnp.float32)
    positions = jnp.arange(row_count, dtype=jnp.int32)
    valid = positions < length_here
    diff = jnp.where(valid[:, None], predicted - target, jnp.float32(0.0))
    slope = (diff * factor).astype(jnp.bfloat16)
    grad_total = jnp.dot(block_rows.T, slope, preferred_element_type=jnp.float32)
    loss_part = jnp.sum(diff * diff)
    grad_proj = lax.psum_scatter(grad_total, "dp", scatter_dimension=0, tiled=True)
    gain_part = jnp.sum(proj_full.astype(jnp.float32) * grad_total, axis=1)
    loss_all, gain_all = lax.psum((loss_part, gain_part), ("dp", "tensor"))
    loss = loss_all / (count * TW)
    grad_gain = gain_all / student_gain
    return (loss, grad_gain, grad_proj)


def solution(mesh):
    return jax.shard_map(
        on_device,
        mesh=mesh,
        in_specs=(
            P("dp", "tensor"),
            P("tensor"),
            P(("dp", "tensor"), None),
            P(),
            P("dp", "tensor"),
            P("dp"),
        ),
        out_specs=(P(), P(), P("dp", "tensor")),
        check_vma=False,
    )
```

profile of v0, /device:TPU:1, one launch (start us, length us, event | category | flops | bytes accessed | tf_op | source)
XLA Modules:
  0.0 375.4 jit_solution(16109726886987439591)
XLA Ops:
  7.2 0.0 all-gather.5.cloned.1.call-start
  7.2 0.7 all-gather.5.cloned.1.call-update
  7.9 0.0 copy-start
  7.9 0.0 all-gather.3.cloned.1.call-start
  8.0 1.4 fusion.6
  9.3 2.1 fusion.8
  11.4 0.0 all-gather.3.cloned.1.call-update
  11.4 0.0 reduce-scatter.4.cloned.1.call-start
  12.1 60.7 %psum.30 = f32[1]{0:T(128)} all-reduce(f32[1]{0:T(128)S(6)} %convert_element_type.25), channel_id=1, replica_groups=mesh['dp'=32,'tensor'=16] {'dp'}, use_global_device_ids=true, to_apply=%region_5.6 | all-reduce | flops 1 | bytes 8 | tf_op jit(solution)/shard_map/psum | solution.py:18
  72.8 0.7 convert_element_type.24
  74.2 2.1 fusion
  76.2 35.9 %psum.28 = f32[2048]{0:T(1024)S(1)} all-reduce(f32[2048]{0:T(1024)S(1)} %fusion), channel_id=1, replica_groups=mesh['dp'=32,'tensor'=16] {'tensor'}, use_global_device_ids=true, to_apply=%region_2.0 | all-reduce | flops 2048 | bytes 16384 | tf_op jit(solution)/shard_map/psum | solution.py:14
  112.2 0.0 all-gather.5.cloned.1.call-done
  112.2 4.0 %copy.11 = bf16[2048,512]{0,1:T(8,128)(2,1)} copy(bf16[2048,512]{1,0:T(8,128)(2,1)} %all-gather.5.cloned.1.call-done) | data formatting | bytes 4194304 | tf_op jit(solution)/shard_map/all_gather | solution.py:22
  116.2 110.3 %all-gather.3.cloned.1.call-done = bf16[2048,2048]{1,0:T(8,128)(2,1)} async-done(((bf16[128,2048]{1,0:T(8,128)(2,1)}), bf16[2048,2048]{1,0:T(8,128)(2,1)}) %all-gather.3.cloned.1.call-update) | async-done | bytes 8388624 | tf_op jit(solution)/shard_map/all_gather | solution.py:25
  226.5 0.0 copy-done
  226.5 9.7 %multiply_reduce_fusion.1 = (f32[]{:T(128)}, f32[2048,512]{1,0:T(8,128)S(1)}) fusion(f32[512]{0:T(512)S(1)} %convert_element_type.24, f32[2048]{0:T(1024)S(1)} %add_rsqrt_fusion, bf16[2048,512]{1,0:T(8,128)(2,1)S(1)} %copy-done, bf16[2048,2048]{1,0:T(8,128)(2,1)} %all-gather.3.cloned.1.call-done, bf16[2048,512]{1,0:T(8,128)(2,1)} %all-gather.5.cloned.1.call-done, ...), kind=kOutput, calls=%fused_computation.8 | convolution fusion | flops 4302307328 | bytes 16789508 | tf_op jit(solution)/shard_map/dot_general | solution.py:27
  236.1 0.0 copy-done.1
  236.1 6.2 %multiply_reduce_fusion = (f32[2048]{0:T(1024)S(1)}, f32[2048,512]{0,1:T(8,128)}) fusion(bf16[2048,512]{0,1:T(8,128)(2,1)S(1)} %copy-done.1, bf16[2048,2048]{1,0:T(8,128)(2,1)S(1)} %copy-done.3, f32[2048,512]{1,0:T(8,128)S(1)} %get-tuple-element.12, f32[]{:T(128)} %bitcast.2), kind=kOutput, calls=%fused_computation.6 | convolution fusion | flops 4300208128 | bytes 18882564 | tf_op jit(solution)/shard_map/dot_general | solution.py:32
  242.4 5.3 %copy.13 = f32[2048,512]{1,0:T(8,128)} copy(f32[2048,512]{0,1:T(8,128)} %get-tuple-element.14) | data formatting | bytes 8388608
  247.7 0.0 reduce-scatter.4.cloned.1.call-update
  248.4 98.6 %all-reduce = (f32[]{:T(128)}, f32[2048]{0:T(1024)S(1)}) all-reduce(f32[]{:T(128)} %get-tuple-element.11, f32[2048]{0:T(1024)S(1)} %get-tuple-element.13), channel_id=1, replica_groups=mesh['dp'=32,'tensor'=16] {'dp','tensor'}, use_global_device_ids=true, to_apply=%region_4.5 | all-reduce | flops 2049 | bytes 16392 | tf_op jit(solution)/shard_map/psum | solution.py:36
  347.0 0.6 div.31
  348.3 19.4 %reduce-scatter.4.cloned.1.call-done = f32[64,512]{1,0:T(8,128)} async-done(((f32[2048,512]{1,0:T(8,128)}), f32[64,512]{1,0:T(8,128)}) %reduce-scatter.4.cloned.1.call-update) | async-done | bytes 131088
  (8 shorter events, 0.0 us)
Async XLA Ops:
  7.2 105.0 %all-gather.5.cloned.1.call-start = ((), (), s32[]{:S(2)}) async-start(), calls=%async_computation.2 | async-start | bytes 2162688 | tf_op jit(solution)/shard_map/all_gather | solution.py:22
  7.9 218.6 %copy-start = (bf16[2048,512]{1,0:T(8,128)(2,1)S(1)}, bf16[2048,512]{1,0:T(8,128)(2,1)}, u32[]{:S(2)}) copy-start(bf16[2048,512]{1,0:T(8,128)(2,1)} %param.6) | copy-start | bytes 6291460
  7.9 218.6 %all-gather.3.cloned.1.call-start = ((), (), s32[]{:S(2)}) async-start(), calls=%async_computation.1 | async-start | bytes 8912896 | tf_op jit(solution)/shard_map/all_gather | solution.py:25
  11.4 356.3 %reduce-scatter.4.cloned.1.call-start = ((), (), s32[]{:S(2)}) async-start(), calls=%async_computation.3 | async-start | bytes 4325376
  226.5 9.7 %copy-start.1 = (bf16[2048,512]{0,1:T(8,128)(2,1)S(1)}, bf16[2048,512]{0,1:T(8,128)(2,1)}, u32[]{:S(2)}) copy-start(bf16[2048,512]{0,1:T(8,128)(2,1)} %copy.11) | copy-start | bytes 6291460
  226.5 9.7 %copy-start.3 = (bf16[2048,2048]{1,0:T(8,128)(2,1)S(1)}, bf16[2048,2048]{1,0:T(8,128)(2,1)}, u32[]{:S(2)}) copy-start(bf16[2048,2048]{1,0:T(8,128)(2,1)} %all-gather.3.cloned.1.call-done) | copy-start | bytes 25165828
  247.7 99.3 %copy-start.2 = (f32[2048]{0:T(1024)S(1)}, f32[2048]{0:T(1024)}, u32[]{:S(2)}) copy-start(f32[2048]{0:T(1024)} %param.9) | copy-start | bytes 24580
Sparse Core Ops, SparseCore 0:
  10.1 73.7 all-gather.4
  87.1 139.3 all-gather.2
  247.9 119.7 reduce-scatter.3
where the time goes:
time: 379 us; the launch traced here: 375 us
  blocking collectives  195 us (51%)
  waiting for transfers between devices  130 us (34%)
  between operations  17.6 us (5%)
  matrix products  15.9 us (4%)
  local copies, waits for them, and re-layouts  9.33 us (2%)
  other arithmetic  6.81 us (2%)
    all_gather x1, waiting for transfers between devices, on_device(): block_rows = lax.all_gather(scaled, 'tensor', axis=0, tiled=True)  110 us
    psum x1, blocking collectives, on_device(): loss_all, gain_all = lax.psum((loss_part, gain_part), ('dp', 'tensor'))  98.6 us
    psum x1, blocking collectives, on_device(): count = lax.psum(lengths.astype(jnp.float32), 'dp')[0]  60.7 us
    psum x1, blocking collectives, on_device(): row_squares = lax.psum(jnp.sum(hidden_f * hidden_f, axis=1), 'tensor')  35.9 us
    unnamed x4, waiting for transfers between devices  20.1 us
    dot_general x1, matrix products, on_device(): jnp.dot(block_rows, proj_full, preferred_element_type=jnp.float32)  9.66 us
  transfers between devices with their start and end apart: 3, of which 2 were waited for; matrix products, arithmetic and copies ran while one was open for 3% of the time, Pallas kernels for 0%

commit v1 on v0

v1 whole, which is shorter than its diff:
```python
import jax
import jax.numpy as jnp
from jax import lax
from jax.sharding import Mesh, PartitionSpec as P

TW = 8192
EPS = 1e-06
F32, BF16 = jnp.float32, jnp.bfloat16
DP = ("xl", "z", "c")
TENSOR = ("y", "xh")


SWAP = [(0, 0), (1, 2), (2, 1), (3, 3)]
CROSS = [(c * 2 + xh, (1 - xh) * 2 + c) for c in (0, 1) for xh in (0, 1)]


def flip(x, axis, size, bit):
    return lax.ppermute(x, axis, [(i, i ^ bit) for i in range(size)])


def shift(x, axis, size, by):
    return lax.ppermute(x, axis, [(i, (i + by) % size) for i in range(size)])


def corner(flip_xl, flip_c, flip_xh):
    return [
        (xl * 4 + c * 2 + xh, (xl ^ flip_xl) * 4 + (xh ^ flip_c) * 2 + (c ^ flip_xh))
        for xl in (0, 1)
        for c in (0, 1)
        for xh in (0, 1)
    ]


def gather_projection(projection, lengths):
    xl, xh, z = lax.axis_index("xl"), lax.axis_index("xh"), lax.axis_index("z")
    length = lengths[0]
    lane = lax.broadcasted_iota(jnp.int32, (16, 512), 1)
    digits = jnp.where(lane == 0, length // 16, jnp.where(lane == 1, length % 16, 0)).astype(BF16)
    own = jnp.concatenate([projection, digits], axis=0)
    got = {}
    for fx in (0, 1):
        for fc in (0, 1):
            got[fx, fc] = lax.ppermute(own, ("xl", "c", "xh"), corner(fx, 0, fc))
    by_xl = []
    for x in (0, 1):
        for k in (0, 1):
            a = jnp.where(xh == k, got[0, 0], got[0, 1])
            b = jnp.where(xh == k, got[1, 0], got[1, 1])
            by_xl.append(jnp.where(xl == x, a, b))
    block = jnp.concatenate([b[:64] for b in by_xl] + [b[64:68] for b in by_xl], axis=0)
    shards = {0: block}
    up = down = block
    for step in (1, 2, 3):
        up = shift(up, "z", 8, 1)
        down = shift(down, "z", 8, -1)
        shards[-step], shards[step] = up, down
    first = shift(up[:128], "z", 8, 1)
    last = shift(down[128:], "z", 8, -1)
    shards[4] = jnp.concatenate([first, last], axis=0)
    full = jnp.zeros((2, 8, 128, 512), BF16)
    total = jnp.zeros((), F32)
    for offset, shard in shards.items():
        rows = shard[:256].reshape(2, 1, 128, 512)
        full = lax.dynamic_update_slice(full, rows, (0, (z + offset) % 8, 0, 0))
        tail = shard[256:].astype(F32)
        total += jnp.sum(tail.reshape(4, 4, 512)[:, 0, 0] * 16 + tail.reshape(4, 4, 512)[:, 0, 1])
    return full.reshape(2048, 512), total


def row_scale(teacher_hidden, teacher_gain, lengths):
    hidden_f = teacher_hidden.astype(F32)
    squares = jnp.sum(hidden_f * hidden_f, axis=1).reshape(16, 128)
    for bit in (1, 2, 4):
        squares = squares + flip(squares, "y", 8, bit)
    packed = jnp.concatenate(
        [
            squares,
            teacher_gain.astype(F32).reshape(4, 128),
            jnp.broadcast_to(lengths.astype(F32), (4, 128)),
        ],
        axis=0,
    )
    mine = lax.ppermute(packed, ("c", "xh"), SWAP)
    other = lax.ppermute(squares, ("c", "xh"), CROSS)
    scale = lax.rsqrt((mine[:16] + other).reshape(2048) / TW + EPS)
    return scale, mine[16:20].reshape(512), mine[20, 0].astype(jnp.int32)


def on_device(teacher_hidden, teacher_gain, student_hidden, student_gain, projection, lengths):
    c, xl, xh = lax.axis_index("c"), lax.axis_index("xl"), lax.axis_index("xh")
    student_f = student_hidden.astype(F32)
    normed = student_f * lax.rsqrt(jnp.mean(student_f * student_f, axis=1, keepdims=True) + EPS)
    scaled = (normed * student_gain).astype(BF16)
    scaled = lax.ppermute(scaled, ("c", "xh"), SWAP)
    near = lax.all_gather(scaled, "y", axis=0, tiled=True)

    proj_full, count = gather_projection(projection, lengths)
    scale, gain, length = row_scale(teacher_hidden, teacher_gain, lengths)
    teacher = lax.ppermute(teacher_hidden, ("c", "xh"), SWAP).reshape(8, 2, 128, 512)
    far = flip(near, "c", 2, 1)

    factor = 2.0 / count
    scale = scale.reshape(8, 2, 128)
    grad_total = None
    loss_part = jnp.zeros((), F32)
    for rows, half in ((near, c), (far, 1 - c)):
        hidden = lax.dynamic_index_in_dim(teacher, half, 1, keepdims=False).reshape(1024, 512)
        rs = lax.dynamic_index_in_dim(scale, half, 1, keepdims=False).reshape(1024, 1)
        target = hidden.astype(F32) * rs * gain
        predicted = jnp.dot(rows, proj_full, preferred_element_type=F32)
        i = jnp.arange(1024, dtype=jnp.int32)
        positions = (i // 128) * 256 + half * 128 + i % 128
        diff = jnp.where((positions < length)[:, None], predicted - target, F32(0.0))
        slope = (diff * factor).astype(BF16)
        part = jnp.dot(rows.T, slope, preferred_element_type=F32)
        grad_total = part if grad_total is None else grad_total + part
        loss_part += jnp.sum(diff * diff)

    gain_part = jnp.sum(proj_full.astype(F32) * grad_total, axis=1)
    by_z = grad_total.reshape(2, 8, 128, 512).transpose(1, 2, 0, 3).reshape(1024, 1024)
    mine = lax.psum_scatter(by_z, "z", scatter_dimension=0, tiled=True).reshape(2, 64, 2, 512)

    sums = jnp.concatenate(
        [gain_part.reshape(16, 128), jnp.broadcast_to(loss_part, (8, 128))], axis=0
    )
    for axis, size, bit in (
        ("c", 2, 1),
        ("z", 8, 1),
        ("z", 8, 2),
        ("z", 8, 4),
        ("y", 8, 1),
        ("y", 8, 2),
        ("y", 8, 4),
        ("xl", 2, 1),
        ("xh", 2, 1),
    ):
        sums = sums + flip(sums, axis, size, bit)
    grad_proj = jnp.zeros((64, 512), F32)
    for fx in (0, 1):
        for fc in (0, 1):
            send = lax.dynamic_slice(mine, (xh ^ fc, 0, xl ^ fx, 0), (1, 64, 1, 512)).reshape(64, 512)
            grad_proj += lax.ppermute(send, ("xl", "c", "xh"), corner(fx, fc, 0))
    loss = sums[16, 0] / (count * TW)
    grad_gain = sums[:16].reshape(2048) / student_gain
    return (loss, grad_gain, grad_proj)


def solution(mesh):
    parts = Mesh(mesh.devices.reshape(2, 8, 2, 8, 2), DP + TENSOR)
    return jax.shard_map(
        on_device,
        mesh=parts,
        in_specs=(P(DP, TENSOR), P(TENSOR), P(DP + TENSOR, None), P(), P(DP, TENSOR), P(DP)),
        out_specs=(P(), P(), P(DP, TENSOR)),
        check_vma=False,
    )
```

time: 379 us -> 258 us (0.68)
  blocking collectives: 195 us -> 0 us
  starting transfers between devices: 0.12 us -> 140 us
  waiting for transfers between devices: 130 us -> 35.5 us
  local copies, waits for them, and re-layouts: 9.33 us -> 24.5 us
  between operations: 17.6 us -> 24.7 us
  matrix products: 15.9 us -> 21.9 us
    psum x3 -> x0, blocking collectives: 195 us -> none  [the longest x1 98.6 us: on_device(): loss_all, gain_all = lax.psum((loss_part, gain_part), ('dp', 'tensor'))]
    ppermute x0 -> x33, starting transfers between devices: none -> 139 us  [the longest x13 56.5 us: flip(): return lax.ppermute(x, axis, [(i, i ^ bit) for i in range(size)])]
    all_gather x2 -> x1, waiting for transfers between devices: 110 us -> 0.01 us  [on_device(): near = lax.all_gather(scaled, 'y', axis=0, tiled=True)]
    ppermute x0 -> x33, waiting for transfers between devices: none -> 32.9 us  [the longest x13 21.6 us: flip(): return lax.ppermute(x, axis, [(i, i ^ bit) for i in range(size)])]
    unnamed x4 -> x2, waiting for transfers between devices: 20.1 us -> 0.03 us
    dot_general x2 -> x4, matrix products: 15.9 us -> 21.9 us  [the longest x2 11.1 us: on_device(): part = jnp.dot(rows.T, slope, preferred_element_type=F32)]
    reshape x0 -> x9, local copies, waits for them, and re-layouts: none -> 5.83 us  [the longest x1 5.28 us: on_device(): grad_total.reshape(2, 8, 128, 512).transpose(1, 2, 0, 3).reshape(1024, 1024)]
    dynamic_update_slice x0 -> x8, local copies, waits for them, and re-layouts: none -> 5.82 us  [gather_projection(): full = lax.dynamic_update_slice(full, rows, (0, (z + offset) % 8, 0, 0))]
  transfers between devices with their start and end apart: 3 -> 35, of which waited for: 2 -> 17; matrix products, arithmetic and copies ran while one was open for 3% -> 8% of each run, Pallas kernels for 0% -> 0%
where the time goes in v1:
time: 258 us; the launch traced here: 256 us
  starting transfers between devices  140 us (54%)
  waiting for transfers between devices  35.5 us (14%)
  between operations  24.7 us (10%)
  local copies, waits for them, and re-layouts  24.5 us (9%)
  matrix products  21.9 us (8%)
  other arithmetic  9.44 us (4%)
    ppermute x13, starting transfers between devices, flip(): return lax.ppermute(x, axis, [(i, i ^ bit) for i in range(size)])  56.5 us
    ppermute x8, starting transfers between devices, shift(): return lax.ppermute(x, axis, [(i, (i + by) % size) for i in range(size)])  33.5 us
    ppermute x13, waiting for transfers between devices, flip(): return lax.ppermute(x, axis, [(i, i ^ bit) for i in range(size)])  21.6 us
    ppermute x4, starting transfers between devices, on_device(): grad_proj += lax.ppermute(send, ('xl', 'c', 'xh'), corner(fx, fc, 0))  16.4 us
    ppermute x4, starting transfers between devices, gather_projection(): got[fx, fc] = lax.ppermute(own, ('xl', 'c', 'xh'), corner(fx, 0, fc))  12.9 us
    dot_general x2, matrix products, on_device(): part = jnp.dot(rows.T, slope, preferred_element_type=F32)  11.1 us
    dot_general x2, matrix products, on_device(): predicted = jnp.dot(rows, proj_full, preferred_element_type=F32)  10.8 us
    ppermute x1, starting transfers between devices, row_scale(): mine = lax.ppermute(packed, ('c', 'xh'), SWAP)  8.1 us
  transfers between devices with their start and end apart: 35, of which 17 were waited for; matrix products, arithmetic and copies ran while one was open for 8% of the time, Pallas kernels for 0%

profile of v1, /device:TPU:1, one launch (start us, length us, event | category | flops | bytes accessed | tf_op | source)
XLA Modules:
  0.0 255.6 jit_solution(7067624869239449193)
XLA Ops:
  9.9 6.0 %collective-permute-start.12 = (bf16[128,2048]{1,0:T(8,128)(2,1)S(1)}, bf16[128,2048]{1,0:T(8,128)(2,1)S(1)}, u32[]{:S(2)}, u32[]{:S(2)}) collective-permute-start(bf16[128,2048]{1,0:T(8,128)(2,1)S(1)} %fusion.8), channel_id=1, source_target_pairs={{0,0},{1,16},{16,1},{17,17},{2,2},{3,18},{18,3},{19,19},{4,4},{5,2... | collective-permute-start | bytes 1572872 | tf_op jit(solution)/shard_map/ppermute | solution.py:94
  15.9 6.8 %collective-permute-done.12 = bf16[128,2048]{1,0:T(8,128)(2,1)S(1)} collective-permute-done((bf16[128,2048]{1,0:T(8,128)(2,1)S(1)}, bf16[128,2048]{1,0:T(8,128)(2,1)S(1)}, u32[]{:S(2)}, u32[]{:S(2)}) %collective-permute-start.12) | collective-permute-done | bytes 524320 | tf_op jit(solution)/shard_map/ppermute | solution.py:94
  28.5 4.2 %collective-permute-start.14 = (f32[16,128]{1,0:T(8,128)S(1)}, f32[16,128]{1,0:T(8,128)S(1)}, u32[]{:S(2)}, u32[]{:S(2)}) collective-permute-start(f32[16,128]{1,0:T(8,128)S(1)} %bitcast_add_fusion), channel_id=1, source_target_pairs={{0,4},{2,6},{4,0},{6,2},{8,12},{10,14},{12,8},{14,10},{1,5},{3,7},... | collective-permute-start | bytes 24584 | tf_op jit(solution)/shard_map/ppermute | solution.py:18
  33.8 7.7 %collective-permute-start.15 = (f32[16,128]{1,0:T(8,128)S(1)}, f32[16,128]{1,0:T(8,128)S(1)}, u32[]{:S(2)}, u32[]{:S(2)}) collective-permute-start(f32[16,128]{1,0:T(8,128)S(1)} %fusion.45), channel_id=1, source_target_pairs={{0,8},{2,10},{4,12},{6,14},{8,0},{10,2},{12,4},{14,6},{1,9},{3,11}... | collective-permute-start | bytes 24584 | tf_op jit(solution)/shard_map/ppermute | solution.py:18
  42.7 8.1 %collective-permute-start.16 = (f32[24,128]{1,0:T(8,128)S(1)}, f32[24,128]{1,0:T(8,128)S(1)}, u32[]{:S(2)}, u32[]{:S(2)}) collective-permute-start(f32[24,128]{1,0:T(8,128)S(1)} %maximum_maximum_fusion), channel_id=1, source_target_pairs={{0,0},{1,16},{16,1},{17,17},{2,2},{3,18},{18,3},{19,19},{4,4},{5,2... | collective-permute-start | bytes 36872 | tf_op jit(solution)/shard_map/ppermute | solution.py:83
  54.7 4.9 %collective-permute-start.2 = (bf16[80,512]{1,0:T(8,128)(2,1)S(1)}, bf16[80,512]{1,0:T(8,128)(2,1)S(1)}, u32[]{:S(2)}, u32[]{:S(2)}) collective-permute-start(bf16[80,512]{1,0:T(8,128)(2,1)S(1)} %pad_maximum_fusion.2), channel_id=1, source_target_pairs={{0,256},{1,272},{16,257},{17,273},{256,0},{257,16},{272,1},{273,17... | collective-permute-start | bytes 245768 | tf_op jit(solution)/shard_map/ppermute | solution.py:43
  59.5 4.2 %collective-permute-start.3 = (bf16[80,512]{1,0:T(8,128)(2,1)S(1)}, bf16[80,512]{1,0:T(8,128)(2,1)S(1)}, u32[]{:S(2)}, u32[]{:S(2)}) collective-permute-start(bf16[80,512]{1,0:T(8,128)(2,1)S(1)} %pad_maximum_fusion.2), channel_id=1, source_target_pairs={{0,257},{1,273},{16,256},{17,272},{256,1},{257,17},{272,0},{273,16... | collective-permute-start | bytes 245768 | tf_op jit(solution)/shard_map/ppermute | solution.py:43
  67.0 4.1 %collective-permute-start.17 = (bf16[2048,512]{1,0:T(8,128)(2,1)}, bf16[2048,512]{1,0:T(8,128)(2,1)S(1)}, u32[]{:S(2)}, u32[]{:S(2)}) collective-permute-start(bf16[2048,512]{1,0:T(8,128)(2,1)} %param.6), channel_id=1, source_target_pairs={{0,0},{1,16},{16,1},{17,17},{2,2},{3,18},{18,3},{19,19},{4,4},{5,2... | collective-permute-start | bytes 6291464 | tf_op jit(solution)/shard_map/ppermute | solution.py:99
  75.6 8.6 %collective-permute-start.5 = (bf16[272,512]{1,0:T(8,128)(2,1)S(1)}, bf16[272,512]{1,0:T(8,128)(2,1)S(1)}, u32[]{:S(2)}, u32[]{:S(2)}) collective-permute-start(bf16[272,512]{1,0:T(8,128)(2,1)S(1)} %concatenate.23), channel_id=1, source_target_pairs={{0,224},{32,0},{64,32},{96,64},{128,96},{160,128},{192,160},{224,1... | collective-permute-start | bytes 835592 | tf_op jit(solution)/shard_map/ppermute | solution.py:22
  95.1 4.7 %collective-permute-start.7 = (bf16[272,512]{1,0:T(8,128)(2,1)S(1)}, bf16[272,512]{1,0:T(8,128)(2,1)S(1)}, u32[]{:S(2)}, u32[]{:S(2)}) collective-permute-start(bf16[272,512]{1,0:T(8,128)(2,1)S(1)} %collective-permute-done.5), channel_id=1, source_target_pairs={{0,224},{32,0},{64,32},{96,64},{128,96},{160,128},{192,160},{224,1... | collective-permute-start | bytes 835592 | tf_op jit(solution)/shard_map/ppermute | solution.py:22
  104.7 5.1 %collective-permute-start.9 = (bf16[272,512]{1,0:T(8,128)(2,1)S(1)}, bf16[272,512]{1,0:T(8,128)(2,1)S(1)}, u32[]{:S(2)}, u32[]{:S(2)}) collective-permute-start(bf16[272,512]{1,0:T(8,128)(2,1)S(1)} %collective-permute-done.7), channel_id=1, source_target_pairs={{0,224},{32,0},{64,32},{96,64},{128,96},{160,128},{192,160},{224,1... | collective-permute-start | bytes 835592 | tf_op jit(solution)/shard_map/ppermute | solution.py:22
  113.3 5.0 %collective-permute-start.11 = (bf16[144,512]{1,0:T(8,128)(2,1)S(1)}, bf16[144,512]{1,0:T(8,128)(2,1)S(1)}, u32[]{:S(2)}, u32[]{:S(2)}) collective-permute-start(bf16[144,512]{1,0:T(8,128)(2,1)S(1)} %slice.199), channel_id=1, source_target_pairs={{0,224},{32,0},{64,32},{96,64},{128,96},{160,128},{192,160},{224,1... | collective-permute-start | bytes 442376 | tf_op jit(solution)/shard_map/ppermute | solution.py:22
  129.0 4.9 %multiply_reduce_fusion.3 = (f32[]{:T(128)}, f32[1024,512]{1,0:T(8,128)S(1)}) fusion(f32[512]{0:T(512)S(1)} %slice_bitcast_fusion.1, f32[1024]{0:T(1024)S(1)} %bitcast.110, bf16[1024,512]{1,0:T(8,128)(2,1)S(1)} %bitcast.92, bf16[1024,2048]{1,0:T(8,128)(2,1)S(1)} %copy-done.5, bf16[2048,512]{1,0:T(8,128)(2,1)} %bitcast.17, pred[1024]{0:T(1024)(128)(4,1)S(1)} %fusion.25), kind=kOutput, calls=%fused_computation.13 | convolution fusion | flops 2151153664 | bytes 9444356 | tf_op jit(solution)/shard_map/dot_general | solution.py:110
  134.0 5.9 %multiply_reduce_fusion.2 = (f32[]{:T(128)}, f32[1024,512]{1,0:T(8,128)S(1)}) fusion(f32[512]{0:T(512)S(1)} %slice_bitcast_fusion.1, f32[1024]{0:T(1024)S(1)} %bitcast.109, bf16[1024,512]{1,0:T(8,128)(2,1)S(1)} %bitcast.91, bf16[1024,2048]{1,0:T(8,128)(2,1)} %collective-permute-done.19, bf16[2048,512]{1,0:T(8,128)(2,1)} %bitcast.17, ...), kind=kOutput, calls=%fused_computation.12 | convolution fusion | flops 2151153664 | bytes 9444356 | tf_op jit(solution)/shard_map/dot_general | solution.py:110
  139.8 4.7 %fusion.9 = f32[2048,512]{1,0:T(8,128)S(1)} fusion(bf16[1024,2048]{1,0:T(8,128)(2,1)} %collective-permute-done.19, f32[1024,512]{1,0:T(8,128)S(1)} %get-tuple-element.20, f32[]{:T(128)S(6)} %div.50), kind=kOutput, calls=%fused_computation.21 | convolution fusion | flops 2148532224 | bytes 10485764 | tf_op jit(solution)/shard_map/dot_general | solution.py:115
  144.5 6.4 %multiply_reduce_fusion = (f32[2048]{0:T(1024)S(1)}, f32[2048,512]{1,0:T(8,128)}) fusion(bf16[2,8,128,512]{3,2,1,0:T(8,128)(2,1)} %constant_dynamic-update-slice_fusion, f32[2048,512]{1,0:T(8,128)S(1)} %fusion.9, bf16[1024,2048]{1,0:T(8,128)(2,1)S(1)} %copy-done.5, f32[1024,512]{1,0:T(8,128)S(1)} %get-tuple-element.18, f32[]{:T(128)S(6)} %div.50), kind=kOutput, calls=%fused_computation.1 | convolution fusion | flops 2152724480 | bytes 16785412 | tf_op jit(solution)/shard_map/dot_general | solution.py:115
  150.9 5.3 %copy.29 = f32[2,8,128,512]{2,1,3,0:T(8,128)} copy(f32[2,8,128,512]{3,2,1,0:T(8,128)} %bitcast.89) | data formatting | bytes 8388608 | tf_op jit(solution)/shard_map/reshape | solution.py:120
  156.2 5.1 %copy.43 = f32[128,8,8,128]{3,1,2,0:T(8,128)} copy(f32[128,8,8,128]{3,2,1,0:T(8,128)} %bitcast.88) | data formatting | bytes 8388608
  162.7 6.5 %collective-permute-start.20 = (f32[24,128]{1,0:T(8,128)S(1)}, f32[24,128]{1,0:T(8,128)S(1)}, u32[]{:S(2)}, u32[]{:S(2)}) collective-permute-start(f32[24,128]{1,0:T(8,128)S(1)} %concatenate.27), channel_id=1, source_target_pairs={{0,16},{16,0},{1,17},{17,1},{2,18},{18,2},{3,19},{19,3},{4,20},{20... | collective-permute-start | bytes 36872 | tf_op jit(solution)/shard_map/ppermute | solution.py:18
  174.5 6.0 %collective-permute-start.22 = (f32[24,128]{1,0:T(8,128)S(1)}, f32[24,128]{1,0:T(8,128)S(1)}, u32[]{:S(2)}, u32[]{:S(2)}) collective-permute-start(f32[24,128]{1,0:T(8,128)S(1)} %add.349), channel_id=1, source_target_pairs={{0,64},{32,96},{64,0},{96,32},{128,192},{160,224},{192,128},{224,1... | collective-permute-start | bytes 36872 | tf_op jit(solution)/shard_map/ppermute | solution.py:18
  181.7 5.2 %collective-permute-start.23 = (f32[24,128]{1,0:T(8,128)S(1)}, f32[24,128]{1,0:T(8,128)S(1)}, u32[]{:S(2)}, u32[]{:S(2)}) collective-permute-start(f32[24,128]{1,0:T(8,128)S(1)} %add.350), channel_id=1, source_target_pairs={{0,128},{32,160},{64,192},{96,224},{128,0},{160,32},{192,64},{224,... | collective-permute-start | bytes 36872 | tf_op jit(solution)/shard_map/ppermute | solution.py:18
  201.0 5.4 %collective-permute-start.26 = (f32[24,128]{1,0:T(8,128)S(1)}, f32[24,128]{1,0:T(8,128)S(1)}, u32[]{:S(2)}, u32[]{:S(2)}) collective-permute-start(f32[24,128]{1,0:T(8,128)S(1)} %add.353), channel_id=1, source_target_pairs={{0,8},{2,10},{4,12},{6,14},{8,0},{10,2},{12,4},{14,6},{1,9},{3,11}... | collective-permute-start | bytes 36872 | tf_op jit(solution)/shard_map/ppermute | solution.py:18
  214.1 5.0 %collective-permute-start.28 = (f32[24,128]{1,0:T(8,128)S(1)}, f32[24,128]{1,0:T(8,128)S(1)}, u32[]{:S(2)}, u32[]{:S(2)}) collective-permute-start(f32[24,128]{1,0:T(8,128)S(1)} %add.355), channel_id=1, source_target_pairs={{0,1},{1,0},{2,3},{3,2},{4,5},{5,4},{6,7},{7,6},{8,9},{9,8},{10,11... | collective-permute-start | bytes 36872 | tf_op jit(solution)/shard_map/ppermute | solution.py:18
  226.1 10.2 %collective-permute-start.29 = (f32[64,512]{1,0:T(8,128)S(1)}, f32[64,512]{1,0:T(8,128)S(1)}, u32[]{:S(2)}, u32[]{:S(2)}) collective-permute-start(f32[64,512]{1,0:T(8,128)S(1)} %bitcast.101), channel_id=1, source_target_pairs={{0,0},{1,16},{16,1},{17,17},{256,256},{257,272},{272,257},{273,273... | collective-permute-start | bytes 393224 | tf_op jit(solution)/shard_map/ppermute | solution.py:142
  (160 shorter events, 90.6 us)
Async XLA Ops:
  7.2 79.4 %all-gather.2.cloned.1.call-start = ((), (), s32[]{:S(2)}) async-start(), calls=%async_computation.1 | async-start | bytes 4718592 | tf_op jit(solution)/shard_map/all_gather | solution.py:95
  9.9 12.9 %collective-permute-start.12 = (bf16[128,2048]{1,0:T(8,128)(2,1)S(1)}, bf16[128,2048]{1,0:T(8,128)(2,1)S(1)}, u32[]{:S(2)}, u32[]{:S(2)}) collective-permute-start(bf16[128,2048]{1,0:T(8,128)(2,1)S(1)} %fusion.8), channel_id=1, source_target_pairs={{0,0},{1,16},{16,1},{17,17},{2,2},{3,18},{18,3},{19,19},{4,4},{5,2... | collective-permute-start | bytes 1572872 | tf_op jit(solution)/shard_map/ppermute | solution.py:94
  23.6 200.3 %reduce-scatter.2.cloned.1.call-start = ((), (), s32[]{:S(2)}) async-start(), calls=%async_computation.2 | async-start | bytes 4718592 | tf_op jit(solution)/shard_map/reduce_scatter | solution.py:121
  33.8 8.8 %collective-permute-start.15 = (f32[16,128]{1,0:T(8,128)S(1)}, f32[16,128]{1,0:T(8,128)S(1)}, u32[]{:S(2)}, u32[]{:S(2)}) collective-permute-start(f32[16,128]{1,0:T(8,128)S(1)} %fusion.45), channel_id=1, source_target_pairs={{0,8},{2,10},{4,12},{6,14},{8,0},{10,2},{12,4},{14,6},{1,9},{3,11}... | collective-permute-start | bytes 24584 | tf_op jit(solution)/shard_map/ppermute | solution.py:18
  42.7 21.2 %collective-permute-start.16 = (f32[24,128]{1,0:T(8,128)S(1)}, f32[24,128]{1,0:T(8,128)S(1)}, u32[]{:S(2)}, u32[]{:S(2)}) collective-permute-start(f32[24,128]{1,0:T(8,128)S(1)} %maximum_maximum_fusion), channel_id=1, source_target_pairs={{0,0},{1,16},{16,1},{17,17},{2,2},{3,18},{18,3},{19,19},{4,4},{5,2... | collective-permute-start | bytes 36872 | tf_op jit(solution)/shard_map/ppermute | solution.py:83
  50.8 20.4 %collective-permute-start = (bf16[80,512]{1,0:T(8,128)(2,1)S(1)}, bf16[80,512]{1,0:T(8,128)(2,1)S(1)}, u32[]{:S(2)}, u32[]{:S(2)}) collective-permute-start(bf16[80,512]{1,0:T(8,128)(2,1)S(1)} %pad_maximum_fusion.2), channel_id=1, source_target_pairs={{0,0},{1,16},{16,1},{17,17},{256,256},{257,272},{272,257},{273,273... | collective-permute-start | bytes 245768 | tf_op jit(solution)/shard_map/ppermute | solution.py:43
  52.7 18.5 %collective-permute-start.1 = (bf16[80,512]{1,0:T(8,128)(2,1)S(1)}, bf16[80,512]{1,0:T(8,128)(2,1)S(1)}, u32[]{:S(2)}, u32[]{:S(2)}) collective-permute-start(bf16[80,512]{1,0:T(8,128)(2,1)S(1)} %pad_maximum_fusion.2), channel_id=1, source_target_pairs={{0,1},{1,17},{16,0},{17,16},{256,257},{257,273},{272,256},{273,272... | collective-permute-start | bytes 245768 | tf_op jit(solution)/shard_map/ppermute | solution.py:43
  54.7 16.6 %collective-permute-start.2 = (bf16[80,512]{1,0:T(8,128)(2,1)S(1)}, bf16[80,512]{1,0:T(8,128)(2,1)S(1)}, u32[]{:S(2)}, u32[]{:S(2)}) collective-permute-start(bf16[80,512]{1,0:T(8,128)(2,1)S(1)} %pad_maximum_fusion.2), channel_id=1, source_target_pairs={{0,256},{1,272},{16,257},{17,273},{256,0},{257,16},{272,1},{273,17... | collective-permute-start | bytes 245768 | tf_op jit(solution)/shard_map/ppermute | solution.py:43
  59.5 11.7 %collective-permute-start.3 = (bf16[80,512]{1,0:T(8,128)(2,1)S(1)}, bf16[80,512]{1,0:T(8,128)(2,1)S(1)}, u32[]{:S(2)}, u32[]{:S(2)}) collective-permute-start(bf16[80,512]{1,0:T(8,128)(2,1)S(1)} %pad_maximum_fusion.2), channel_id=1, source_target_pairs={{0,257},{1,273},{16,256},{17,272},{256,1},{257,17},{272,0},{273,16... | collective-permute-start | bytes 245768 | tf_op jit(solution)/shard_map/ppermute | solution.py:43
  67.0 59.8 %collective-permute-start.17 = (bf16[2048,512]{1,0:T(8,128)(2,1)}, bf16[2048,512]{1,0:T(8,128)(2,1)S(1)}, u32[]{:S(2)}, u32[]{:S(2)}) collective-permute-start(bf16[2048,512]{1,0:T(8,128)(2,1)} %param.6), channel_id=1, source_target_pairs={{0,0},{1,16},{16,1},{17,17},{2,2},{3,18},{18,3},{19,19},{4,4},{5,2... | collective-permute-start | bytes 6291464 | tf_op jit(solution)/shard_map/ppermute | solution.py:99
  71.5 18.3 %collective-permute-start.4 = (bf16[272,512]{1,0:T(8,128)(2,1)S(1)}, bf16[272,512]{1,0:T(8,128)(2,1)S(1)}, u32[]{:S(2)}, u32[]{:S(2)}) collective-permute-start(bf16[272,512]{1,0:T(8,128)(2,1)S(1)} %concatenate.23), channel_id=1, source_target_pairs={{0,32},{32,64},{64,96},{96,128},{128,160},{160,192},{192,224},{224... | collective-permute-start | bytes 835592 | tf_op jit(solution)/shard_map/ppermute | solution.py:22
  75.6 14.2 %collective-permute-start.5 = (bf16[272,512]{1,0:T(8,128)(2,1)S(1)}, bf16[272,512]{1,0:T(8,128)(2,1)S(1)}, u32[]{:S(2)}, u32[]{:S(2)}) collective-permute-start(bf16[272,512]{1,0:T(8,128)(2,1)S(1)} %concatenate.23), channel_id=1, source_target_pairs={{0,224},{32,0},{64,32},{96,64},{128,96},{160,128},{192,160},{224,1... | collective-permute-start | bytes 835592 | tf_op jit(solution)/shard_map/ppermute | solution.py:22
  86.6 47.4 %collective-permute-start.19 = (bf16[1024,2048]{1,0:T(8,128)(2,1)}, bf16[1024,2048]{1,0:T(8,128)(2,1)}, u32[]{:S(2)}, u32[]{:S(2)}) collective-permute-start(bf16[1024,2048]{1,0:T(8,128)(2,1)} %all-gather.2.cloned.1.call-done), channel_id=1, source_target_pairs={{0,16},{16,0},{1,17},{17,1},{2,18},{18,2},{3,19},{19,3},{4,20},{20... | collective-permute-start | bytes 12582920 | tf_op jit(solution)/shard_map/ppermute | solution.py:18
  89.9 11.4 %collective-permute-start.6 = (bf16[272,512]{1,0:T(8,128)(2,1)S(1)}, bf16[272,512]{1,0:T(8,128)(2,1)S(1)}, u32[]{:S(2)}, u32[]{:S(2)}) collective-permute-start(bf16[272,512]{1,0:T(8,128)(2,1)S(1)} %collective-permute-done.4), channel_id=1, source_target_pairs={{0,32},{32,64},{64,96},{96,128},{128,160},{160,192},{192,224},{224... | collective-permute-start | bytes 835592 | tf_op jit(solution)/shard_map/ppermute | solution.py:22
  95.1 8.9 %collective-permute-start.7 = (bf16[272,512]{1,0:T(8,128)(2,1)S(1)}, bf16[272,512]{1,0:T(8,128)(2,1)S(1)}, u32[]{:S(2)}, u32[]{:S(2)}) collective-permute-start(bf16[272,512]{1,0:T(8,128)(2,1)S(1)} %collective-permute-done.5), channel_id=1, source_target_pairs={{0,224},{32,0},{64,32},{96,64},{128,96},{160,128},{192,160},{224,1... | collective-permute-start | bytes 835592 | tf_op jit(solution)/shard_map/ppermute | solution.py:22
  102.0 10.5 %collective-permute-start.8 = (bf16[272,512]{1,0:T(8,128)(2,1)S(1)}, bf16[272,512]{1,0:T(8,128)(2,1)S(1)}, u32[]{:S(2)}, u32[]{:S(2)}) collective-permute-start(bf16[272,512]{1,0:T(8,128)(2,1)S(1)} %collective-permute-done.6), channel_id=1, source_target_pairs={{0,32},{32,64},{64,96},{96,128},{128,160},{160,192},{192,224},{224... | collective-permute-start | bytes 835592 | tf_op jit(solution)/shard_map/ppermute | solution.py:22
  104.7 8.6 %collective-permute-start.9 = (bf16[272,512]{1,0:T(8,128)(2,1)S(1)}, bf16[272,512]{1,0:T(8,128)(2,1)S(1)}, u32[]{:S(2)}, u32[]{:S(2)}) collective-permute-start(bf16[272,512]{1,0:T(8,128)(2,1)S(1)} %collective-permute-done.7), channel_id=1, source_target_pairs={{0,224},{32,0},{64,32},{96,64},{128,96},{160,128},{192,160},{224,1... | collective-permute-start | bytes 835592 | tf_op jit(solution)/shard_map/ppermute | solution.py:22
  113.3 11.3 %collective-permute-start.11 = (bf16[144,512]{1,0:T(8,128)(2,1)S(1)}, bf16[144,512]{1,0:T(8,128)(2,1)S(1)}, u32[]{:S(2)}, u32[]{:S(2)}) collective-permute-start(bf16[144,512]{1,0:T(8,128)(2,1)S(1)} %slice.199), channel_id=1, source_target_pairs={{0,224},{32,0},{64,32},{96,64},{128,96},{160,128},{192,160},{224,1... | collective-permute-start | bytes 442376 | tf_op jit(solution)/shard_map/ppermute | solution.py:22
  118.4 7.7 %collective-permute-start.10 = (bf16[128,512]{1,0:T(8,128)(2,1)S(1)}, bf16[128,512]{1,0:T(8,128)(2,1)S(1)}, u32[]{:S(2)}, u32[]{:S(2)}) collective-permute-start(bf16[128,512]{1,0:T(8,128)(2,1)S(1)} %slice.198), channel_id=1, source_target_pairs={{0,32},{32,64},{64,96},{96,128},{128,160},{160,192},{192,224},{224... | collective-permute-start | bytes 393224 | tf_op jit(solution)/shard_map/ppermute | solution.py:22
  162.7 7.4 %collective-permute-start.20 = (f32[24,128]{1,0:T(8,128)S(1)}, f32[24,128]{1,0:T(8,128)S(1)}, u32[]{:S(2)}, u32[]{:S(2)}) collective-permute-start(f32[24,128]{1,0:T(8,128)S(1)} %concatenate.27), channel_id=1, source_target_pairs={{0,16},{16,0},{1,17},{17,1},{2,18},{18,2},{3,19},{19,3},{4,20},{20... | collective-permute-start | bytes 36872 | tf_op jit(solution)/shard_map/ppermute | solution.py:18
  181.7 8.6 %collective-permute-start.23 = (f32[24,128]{1,0:T(8,128)S(1)}, f32[24,128]{1,0:T(8,128)S(1)}, u32[]{:S(2)}, u32[]{:S(2)}) collective-permute-start(f32[24,128]{1,0:T(8,128)S(1)} %add.350), channel_id=1, source_target_pairs={{0,128},{32,160},{64,192},{96,224},{128,0},{160,32},{192,64},{224,... | collective-permute-start | bytes 36872 | tf_op jit(solution)/shard_map/ppermute | solution.py:18
  201.0 8.3 %collective-permute-start.26 = (f32[24,128]{1,0:T(8,128)S(1)}, f32[24,128]{1,0:T(8,128)S(1)}, u32[]{:S(2)}, u32[]{:S(2)}) collective-permute-start(f32[24,128]{1,0:T(8,128)S(1)} %add.353), channel_id=1, source_target_pairs={{0,8},{2,10},{4,12},{6,14},{8,0},{10,2},{12,4},{14,6},{1,9},{3,11}... | collective-permute-start | bytes 36872 | tf_op jit(solution)/shard_map/ppermute | solution.py:18
  226.1 17.1 %collective-permute-start.29 = (f32[64,512]{1,0:T(8,128)S(1)}, f32[64,512]{1,0:T(8,128)S(1)}, u32[]{:S(2)}, u32[]{:S(2)}) collective-permute-start(f32[64,512]{1,0:T(8,128)S(1)} %bitcast.101), channel_id=1, source_target_pairs={{0,0},{1,16},{16,1},{17,17},{256,256},{257,272},{272,257},{273,273... | collective-permute-start | bytes 393224 | tf_op jit(solution)/shard_map/ppermute | solution.py:142
  238.3 7.5 %collective-permute-start.31 = (f32[64,512]{1,0:T(8,128)S(1)}, f32[64,512]{1,0:T(8,128)S(1)}, u32[]{:S(2)}, u32[]{:S(2)}) collective-permute-start(f32[64,512]{1,0:T(8,128)S(1)} %bitcast.103), channel_id=1, source_target_pairs={{0,256},{1,272},{16,257},{17,273},{256,0},{257,16},{272,1},{273,17... | collective-permute-start | bytes 393224 | tf_op jit(solution)/shard_map/ppermute | solution.py:142
  (17 other events, 178.1 us)
Sparse Core Ops, SparseCore 0:
  23.7 61.7 all-gather.1
  161.5 62.3 reduce-scatter.1

commit v2 on v1

v2 whole, which is shorter than its diff:
```python
import functools

import jax
import jax.numpy as jnp
from jax import lax
from jax.experimental import pallas as pl
from jax.experimental.pallas import tpu as pltpu
from jax.sharding import Mesh, PartitionSpec as P

TW = 8192
EPS = 1e-06
F32, BF16 = jnp.float32, jnp.bfloat16
DP = ("xl", "z", "c")
TENSOR = ("y", "xh")


SWAP = [(0, 0), (1, 2), (2, 1), (3, 3)]
CROSS = [(c * 2 + xh, (1 - xh) * 2 + c) for c in (0, 1) for xh in (0, 1)]


def flip(x, axis, size, bit):
    return lax.ppermute(x, axis, [(i, i ^ bit) for i in range(size)])


def shift(x, axis, size, by):
    return lax.ppermute(x, axis, [(i, (i + by) % size) for i in range(size)])


def corner(flip_xl, flip_c):
    return [
        (xl * 4 + c * 2 + xh, (xl ^ flip_xl) * 4 + (xh ^ flip_c) * 2 + c)
        for xl in (0, 1)
        for c in (0, 1)
        for xh in (0, 1)
    ]


def tie(*arrays):
    return lax.optimization_barrier(arrays)


def rows_step(ints, half, factor, rows, proj_ref, teacher_lo, teacher_hi, scale_ref, gain_ref, grad_ref, loss_ref, blocks):
    step = pl.program_id(0)
    length = ints[1]
    predicted = jnp.dot(rows, proj_ref[...], preferred_element_type=F32)
    scale = jnp.concatenate([scale_ref[...], jnp.zeros((112, 128), F32)], axis=0).T
    lane = lax.broadcasted_iota(jnp.int32, (128, 128), 1)
    row = lax.broadcasted_iota(jnp.int32, (128, 1), 0)
    gain = gain_ref[...]
    loss = jnp.zeros((8, 512), F32)
    slopes = []
    for b in range(blocks):
        place = (step * blocks + b) * 2 + half
        s = jnp.sum(jnp.where(lane == place, scale, 0.0), axis=1, keepdims=True)
        hidden = jnp.where(step == 0, teacher_lo[b, 0], teacher_hi[b, 0])
        target = hidden.astype(F32) * s * gain
        valid = (place * 128 + row) < length
        diff = jnp.where(valid, predicted[b * 128 : (b + 1) * 128] - target, 0.0)
        slopes.append((diff * factor).astype(BF16))
        loss += jnp.sum((diff * diff).reshape(16, 8, 512), axis=0)
    slope = jnp.concatenate(slopes, axis=0)
    loss_ref[...] += loss[:, :128] + loss[:, 128:256] + loss[:, 256:384] + loss[:, 384:]
    for x in range(2):
        grad_ref[:, x * 512 : (x + 1) * 512] += lax.dot_general(
            rows[:, x * 1024 : (x + 1) * 1024],
            slope,
            (((0,), (0,)), ((), ())),
            preferred_element_type=F32,
        )


def near_kernel(ints, rows_ref, teacher_lo, teacher_hi, scale_ref, gain_ref, *rest, blocks):
    shards, (grad_ref, loss_ref, proj_ref, count_ref) = rest[:9], rest[9:]

    @pl.when(pl.program_id(0) == 0)
    def _():
        z = ints[2]
        tails = jnp.zeros((16, 512), F32)
        for offset, shard in zip((0, 1, 2, 3, -1, -2, -3), shards):
            place = lax.rem(z + (offset + 8), 8) * 128
            for x in range(2):
                proj_ref[pl.ds(pl.multiple_of(x * 1024 + place, 128), 128), :] = shard[x * 128 : (x + 1) * 128, :]
            tails += shard[256:272, :].astype(F32)
        place = lax.rem(z + 4, 8) * 128
        proj_ref[pl.ds(pl.multiple_of(place, 128), 128), :] = shards[7][...]
        proj_ref[pl.ds(pl.multiple_of(1024 + place, 128), 128), :] = shards[8][:128, :]
        tails += shards[8][128:144, :].astype(F32)
        lane = lax.broadcasted_iota(jnp.int32, (16, 512), 1)
        weight = jnp.where(lane == 0, 4.0, jnp.where(lane == 1, 0.25, 0.0))
        count_ref[...] = jnp.full((8, 128), jnp.sum(tails * weight), F32)
        grad_ref[...] = jnp.zeros_like(grad_ref)
        loss_ref[...] = jnp.zeros_like(loss_ref)

    factor = 2.0 / count_ref[0:1, 0:1]
    rows_step(
        ints, ints[0], factor, rows_ref[...], proj_ref, teacher_lo, teacher_hi, scale_ref, gain_ref, grad_ref, loss_ref, blocks
    )


def far_kernel(ints, rows_ref, teacher_lo, teacher_hi, scale_ref, gain_ref, *rest, blocks):
    proj_ref, count_ref, grad_in, loss_in, grad_ref, loss_ref, sums_ref = rest

    @pl.when(pl.program_id(0) == 0)
    def _():
        grad_ref[...] = grad_in[...]
        loss_ref[...] = loss_in[...]

    factor = 2.0 / count_ref[0:1, 0:1]
    rows_step(
        ints, 1 - ints[0], factor, rows_ref[...], proj_ref, teacher_lo, teacher_hi, scale_ref, gain_ref, grad_ref, loss_ref, blocks
    )

    @pl.when(pl.program_id(0) == pl.num_programs(0) - 1)
    def _():
        for x in range(2):
            g = grad_ref[:, x * 512 : (x + 1) * 512] * proj_ref[x * 1024 : (x + 1) * 1024, :].astype(F32)
            g = g[:, :128] + g[:, 128:256] + g[:, 256:384] + g[:, 384:]
            sums_ref[x * 8 : (x + 1) * 8, :] = jnp.sum(g.reshape(8, 128, 128), axis=2)
        sums_ref[16:24, :] = loss_ref[...]


def whole(shape):
    return pl.BlockSpec(shape, lambda i, ints: (0,) * len(shape), pipeline_mode=pl.Buffered(1))


def rows_call(kernel, name, flipped, ints, rows, teacher, scale, gain, extra, outs, blocks=4):
    half = (lambda i, ints: (0, 1 - ints[0], 0, 0)) if flipped else (lambda i, ints: (0, ints[0], 0, 0))
    return pl.pallas_call(
        functools.partial(kernel, blocks=blocks),
        grid_spec=pltpu.PrefetchScalarGridSpec(
            num_scalar_prefetch=1,
            grid=(8 // blocks,),
            in_specs=[
                pl.BlockSpec((blocks * 128, 2048), lambda i, ints: (i, 0)),
                pl.BlockSpec((4, 1, 128, 512), half, pipeline_mode=pl.Buffered(1)),
                pl.BlockSpec((4, 1, 128, 512), half, pipeline_mode=pl.Buffered(1)),
                whole((16, 128)),
                whole((1, 512)),
            ]
            + [whole(a.shape) for a in extra],
            out_specs=[whole(shape) for shape, _ in outs],
        ),
        out_shape=[jax.ShapeDtypeStruct(shape, dtype) for shape, dtype in outs],
        compiler_params=pltpu.CompilerParams(vmem_limit_bytes=28 * 2**20),
        cost_estimate=pl.CostEstimate(flops=4 * 1024 * 2048 * 512, bytes_accessed=12 * 2**20, transcendentals=0),
        name=name,
    )(ints, rows, *teacher, scale, gain, *extra)


def own_rows(projection, lengths):
    length = lengths[0]
    lane = lax.broadcasted_iota(jnp.int32, (16, 512), 1)
    digits = jnp.where(lane == 0, length >> 4, jnp.where(lane == 1, length & 15, 0)).astype(BF16)
    return jnp.concatenate([projection, digits], axis=0)


def projection_block(rows_of_x, c):
    rows_of_x = rows_of_x.reshape(2, 2, 80, 512)
    kept = lax.dynamic_index_in_dim(rows_of_x, c, 1, keepdims=False)
    given = lax.dynamic_index_in_dim(rows_of_x, 1 - c, 1, keepdims=False)
    taken = flip(given, "c", 2, 1)
    low, high = jnp.where(c == 0, kept, taken), jnp.where(c == 0, taken, kept)
    parts = [low[0], high[0], low[1], high[1]]
    return jnp.concatenate([p[:64] for p in parts] + [p[64:68] for p in parts], axis=0)


def on_device(teacher_hidden, teacher_gain, student_hidden, student_gain, projection, lengths):
    c, xl, xh, z = (lax.axis_index(a) for a in ("c", "xl", "xh", "z"))
    student_f = student_hidden.astype(F32)
    normed = student_f * lax.rsqrt(jnp.mean(student_f * student_f, axis=1, keepdims=True) + EPS)
    scaled = (normed * student_gain).astype(BF16)
    scaled = lax.ppermute(scaled, ("c", "xh"), SWAP)
    rows_of_x = lax.all_gather(own_rows(projection, lengths), ("xl", "xh"), axis=0, tiled=True)
    scaled, rows_of_x = tie(scaled, rows_of_x)
    near = lax.all_gather(scaled, "y", axis=0, tiled=True)

    block = projection_block(rows_of_x, c)
    up1, down1 = shift(block, "z", 8, 1), shift(block, "z", 8, -1)

    hidden_f = teacher_hidden.astype(F32)
    squares = jnp.sum(hidden_f * hidden_f, axis=1).reshape(16, 128)
    squares, _ = tie(squares, block)
    squares = lax.psum(squares, "y")
    packed = jnp.concatenate(
        [
            squares,
            teacher_gain.astype(F32).reshape(4, 128),
            jnp.broadcast_to(lengths.astype(F32), (4, 128)),
        ],
        axis=0,
    )
    mine = lax.ppermute(packed, ("c", "xh"), SWAP)
    other = lax.ppermute(squares, ("c", "xh"), CROSS)
    teacher, _ = tie(teacher_hidden, block)
    lo = lax.ppermute(teacher[:1024], ("c", "xh"), SWAP)

    up1, down1, squares, lo = tie(up1, down1, squares, lo)
    hi = lax.ppermute(teacher[1024:], ("c", "xh"), SWAP)
    up2, down2 = shift(up1, "z", 8, 1), shift(down1, "z", 8, -1)
    up2, down2, mine, other = tie(up2, down2, mine, other)
    up3, down3 = shift(up2, "z", 8, 1), shift(down2, "z", 8, -1)
    up3, down3, hi = tie(up3, down3, hi)
    teacher = [lo.reshape(4, 2, 128, 512), hi.reshape(4, 2, 128, 512)]
    up4 = shift(up3[:128], "z", 8, 1)
    down4 = shift(down3[128:], "z", 8, -1)
    near, up4, down4 = tie(near, up4, down4)
    far = flip(near, "c", 2, 1)

    scale = lax.rsqrt((mine[:16] + other) / TW + EPS)
    gain = mine[16:20].reshape(1, 512)
    ints = jnp.stack([c, mine[20, 0].astype(jnp.int32), z]).astype(jnp.int32)
    grad, loss_part, proj_full, count = rows_call(
        near_kernel,
        "near_rows",
        False,
        ints,
        near,
        teacher,
        scale,
        gain,
        [block, down1, down2, down3, up1, up2, up3, up4, down4],
        [((1024, 1024), F32), ((8, 128), F32), ((2048, 512), BF16), ((8, 128), F32)],
    )
    grad, _, sums = rows_call(
        far_kernel,
        "far_rows",
        True,
        ints,
        far,
        teacher,
        scale,
        gain,
        [proj_full, count, grad, loss_part],
        [((1024, 1024), F32), ((8, 128), F32), ((24, 128), F32)],
    )
    mine = lax.psum_scatter(grad, "z", scatter_dimension=0, tiled=True).reshape(2, 64, 2, 512)

    for axis, size, bit in (
        ("c", 2, 1),
        ("z", 8, 1),
        ("z", 8, 2),
        ("z", 8, 4),
        ("y", 8, 1),
        ("y", 8, 2),
        ("y", 8, 4),
        ("xl", 2, 1),
        ("xh", 2, 1),
    ):
        sums = sums + flip(sums, axis, size, bit)
    grad_proj = jnp.zeros((64, 512), F32)
    for fx in (0, 1):
        for fc in (0, 1):
            send = lax.dynamic_slice(mine, (xh ^ fc, 0, xl ^ fx, 0), (1, 64, 1, 512)).reshape(64, 512)
            grad_proj += lax.ppermute(send, ("xl", "c", "xh"), corner(fx, fc))
    loss = jnp.sum(sums[16:]) / (count[0, 0] * TW)
    grad_gain = sums[:16].reshape(2048) / student_gain
    return (loss, grad_gain, grad_proj)


def solution(mesh):
    parts = Mesh(mesh.devices.reshape(2, 8, 2, 8, 2), DP + TENSOR)
    return jax.shard_map(
        on_device,
        mesh=parts,
        in_specs=(P(DP, TENSOR), P(TENSOR), P(DP + TENSOR, None), P(), P(DP, TENSOR), P(DP)),
        out_specs=(P(), P(), P(DP, TENSOR)),
        check_vma=False,
    )
```

time: 258 us -> 233 us (0.903)
  starting transfers between devices: 140 us -> 104 us
  blocking collectives: 0 us -> 29 us
  matrix products: 21.9 us -> 0 us
  Pallas kernels: 0 us -> 15.1 us
  local copies, waits for them, and re-layouts: 24.5 us -> 16.2 us
  waiting for transfers between devices: 35.5 us -> 42.3 us
  between operations: 24.7 us -> 18.3 us
  other arithmetic: 9.44 us -> 6.09 us
    dot_general x4 -> x0, matrix products: 21.9 us -> none  [the longest x2 11.1 us: on_device(): part = jnp.dot(rows.T, slope, preferred_element_type=F32)]
    ppermute x13 -> x11, starting transfers between devices: 56.5 us -> 35.9 us  [flip(): return lax.ppermute(x, axis, [(i, i ^ bit) for i in range(size)])]
    psum x0 -> x1, blocking collectives: none -> 16.1 us  [on_device(): squares = lax.psum(squares, 'y')]
    pallas_call x0 -> x2, Pallas kernels: none -> 15.1 us  [rows_call(): pl.pallas_call(functools.partial(kernel, blocks=blocks), grid_spec=pltpu....]
    all_gather x0 -> x1, blocking collectives: none -> 12.9 us  [on_device(): lax.all_gather(own_rows(projection, lengths), ('xl', 'xh'), axis=0, tiled...]
    ppermute x11 -> x8, starting transfers between devices: 43.4 us -> 32.5 us  [the longest x4 16.3 us: on_device(): grad_proj += lax.ppermute(send, ('xl', 'c', 'xh'), corner(fx, fc))]
    ppermute x8, waiting for transfers between devices: 0.71 us -> 10 us  [shift(): return lax.ppermute(x, axis, [(i, (i + by) % size) for i in range(size)])]
    ppermute x1, waiting for transfers between devices: 6.85 us -> 0.01 us  [on_device(): scaled = lax.ppermute(scaled, ('c', 'xh'), SWAP)]
  transfers between devices with their start and end apart: 35 -> 30, of which waited for: 17 -> 16; matrix products, arithmetic and copies ran while one was open for 8% -> 2% of each run, Pallas kernels for 0% -> 3%
where the time goes in v2:
time: 233 us; the launch traced here: 231 us
  starting transfers between devices  104 us (45%)
  waiting for transfers between devices  42.3 us (18%)
  blocking collectives  29 us (12%)
  between operations  18.3 us (8%)
  local copies, waits for them, and re-layouts  16.2 us (7%)
  Pallas kernels  15.1 us (6%)
  other arithmetic  6.09 us (3%)
    ppermute x11, starting transfers between devices, flip(): return lax.ppermute(x, axis, [(i, i ^ bit) for i in range(size)])  35.9 us
    ppermute x8, starting transfers between devices, shift(): return lax.ppermute(x, axis, [(i, (i + by) % size) for i in range(size)])  29.8 us
    ppermute x11, waiting for transfers between devices, flip(): return lax.ppermute(x, axis, [(i, i ^ bit) for i in range(size)])  24.5 us
    ppermute x4, starting transfers between devices, on_device(): grad_proj += lax.ppermute(send, ('xl', 'c', 'xh'), corner(fx, fc))  16.3 us
    psum x1, blocking collectives, on_device(): squares = lax.psum(squares, 'y')  16.1 us
    pallas_call x2, Pallas kernels, rows_call(): pl.pallas_call(functools.partial(kernel, blocks=blocks), grid_spec=pltpu....  15.1 us
    all_gather x1, blocking collectives, on_device(): lax.all_gather(own_rows(projection, lengths), ('xl', 'xh'), axis=0, tiled...  12.9 us
    unnamed x34, local copies, waits for them, and re-layouts  11.5 us
  transfers between devices with their start and end apart: 30, of which 16 were waited for; matrix products, arithmetic and copies ran while one was open for 2% of the time, Pallas kernels for 3%

profile of v2, /device:TPU:1, one launch (start us, length us, event | category | flops | bytes accessed | tf_op | source)
XLA Modules:
  0.0 231.3 jit_solution(703076757409088926)
XLA Ops:
  9.8 6.0 %collective-permute-start = (bf16[128,2048]{1,0:T(8,128)(2,1)S(1)}, bf16[128,2048]{1,0:T(8,128)(2,1)S(1)}, u32[]{:S(2)}, u32[]{:S(2)}) collective-permute-start(bf16[128,2048]{1,0:T(8,128)(2,1)S(1)} %fusion.2), channel_id=1, source_target_pairs={{0,0},{1,16},{16,1},{17,17},{2,2},{3,18},{18,3},{19,19},{4,4},{5,2... | collective-permute-start | bytes 1572872 | tf_op jit(solution)/shard_map/ppermute | solution.py:172
  17.4 12.9 %all_gather.6 = bf16[320,512]{1,0:T(8,128)(2,1)S(1)} all-gather(bf16[80,512]{1,0:T(8,128)(2,1)S(1)} %pad_maximum_fusion), channel_id=1, replica_groups=mesh['xl'=2,'z'=8,'c'=2,'y'=8,'xh'=2] {'xl','xh'}, dimensions={0}, use_global_device_ids=true | all-gather | bytes 409600 | tf_op jit(solution)/shard_map/all_gather | solution.py:173
  31.3 4.1 %collective-permute-start.1 = (bf16[2,80,512]{2,1,0:T(8,128)(2,1)S(1)}, bf16[2,80,512]{2,1,0:T(8,128)(2,1)S(1)}, u32[]{:S(2)}, u32[]{:S(2)}) collective-permute-start(bf16[2,80,512]{2,1,0:T(8,128)(2,1)S(1)} %dynamic-slice_bitcast_fusion), channel_id=1, source_target_pairs={{0,16},{16,0},{1,17},{17,1},{2,18},{18,2},{3,19},{19,3},{4,20},{20... | collective-permute-start | bytes 491528 | tf_op jit(solution)/shard_map/ppermute | solution.py:22
  38.1 4.7 %collective-permute-start.4 = (bf16[1024,512]{1,0:T(8,128)(2,1)}, bf16[1024,512]{1,0:T(8,128)(2,1)S(1)}, u32[]{:S(2)}, u32[]{:S(2)}) collective-permute-start(bf16[1024,512]{1,0:T(8,128)(2,1)} %get-tuple-element.50), channel_id=1, source_target_pairs={{0,0},{1,16},{16,1},{17,17},{2,2},{3,18},{18,3},{19,19},{4,4},{5,2... | collective-permute-start | bytes 3145736 | tf_op jit(solution)/shard_map/ppermute | solution.py:195
  45.2 4.1 %collective-permute-start.2 = (bf16[272,512]{1,0:T(8,128)(2,1)S(1)}, bf16[272,512]{1,0:T(8,128)(2,1)S(1)}, u32[]{:S(2)}, u32[]{:S(2)}) collective-permute-start(bf16[272,512]{1,0:T(8,128)(2,1)S(1)} %concatenate.10.rest_0_), channel_id=1, source_target_pairs={{0,32},{32,64},{64,96},{96,128},{128,160},{160,192},{192,224},{224... | collective-permute-start | bytes 835592 | tf_op jit(solution)/shard_map/ppermute | solution.py:26
  49.3 8.6 %collective-permute-start.3 = (bf16[272,512]{1,0:T(8,128)(2,1)S(1)}, bf16[272,512]{1,0:T(8,128)(2,1)S(1)}, u32[]{:S(2)}, u32[]{:S(2)}) collective-permute-start(bf16[272,512]{1,0:T(8,128)(2,1)S(1)} %concatenate.10.rest_0_), channel_id=1, source_target_pairs={{0,224},{32,0},{64,32},{96,64},{128,96},{160,128},{192,160},{224,1... | collective-permute-start | bytes 835592 | tf_op jit(solution)/shard_map/ppermute | solution.py:26
  58.4 16.1 %psum.7 = f32[16,128]{1,0:T(8,128)S(1)} all-reduce(f32[16,128]{1,0:T(8,128)S(1)} %bitcast.68), channel_id=1, replica_groups=mesh['xl'=2,'z'=8,'c'=2,'y'=8,'xh'=2] {'y'}, use_global_device_ids=true, to_apply=%region_2.3 | all-reduce | flops 2048 | bytes 16384 | tf_op jit(solution)/shard_map/psum | solution.py:183
  76.5 4.6 %collective-permute-start.6 = (bf16[272,512]{1,0:T(8,128)(2,1)S(1)}, bf16[272,512]{1,0:T(8,128)(2,1)S(1)}, u32[]{:S(2)}, u32[]{:S(2)}) collective-permute-start(bf16[272,512]{1,0:T(8,128)(2,1)S(1)} %collective-permute-done.3.rest_1_), channel_id=1, source_target_pairs={{0,224},{32,0},{64,32},{96,64},{128,96},{160,128},{192,160},{224,1... | collective-permute-start | bytes 835592 | tf_op jit(solution)/shard_map/ppermute | solution.py:26
  81.2 7.3 %collective-permute-start.7 = (f32[24,128]{1,0:T(8,128)S(1)}, f32[24,128]{1,0:T(8,128)S(1)}, u32[]{:S(2)}, u32[]{:S(2)}) collective-permute-start(f32[24,128]{1,0:T(8,128)S(1)} %maximum_maximum_fusion), channel_id=1, source_target_pairs={{0,0},{1,16},{16,1},{17,17},{2,2},{3,18},{18,3},{19,19},{4,4},{5,2... | collective-permute-start | bytes 36872 | tf_op jit(solution)/shard_map/ppermute | solution.py:192
  94.7 2.9 %collective-permute-start.9 = (bf16[272,512]{1,0:T(8,128)(2,1)S(1)}, bf16[272,512]{1,0:T(8,128)(2,1)S(1)}, u32[]{:S(2)}, u32[]{:S(2)}) collective-permute-start(bf16[272,512]{1,0:T(8,128)(2,1)S(1)} %collective-permute-done.5.rest_5_), channel_id=1, source_target_pairs={{0,32},{32,64},{64,96},{96,128},{128,160},{160,192},{192,224},{224... | collective-permute-start | bytes 835592 | tf_op jit(solution)/shard_map/ppermute | solution.py:26
  100.8 4.0 %collective-permute-done.9.rest_6_ = bf16[272,512]{1,0:T(8,128)(2,1)S(1)} collective-permute-done((bf16[272,512]{1,0:T(8,128)(2,1)S(1)}, bf16[272,512]{1,0:T(8,128)(2,1)S(1)}, u32[]{:S(2)}, u32[]{:S(2)}) %collective-permute-start.9) | collective-permute-done | bytes 278560 | tf_op jit(solution)/shard_map/ppermute | solution.py:26
  106.7 3.4 %collective-permute-start.12 = (bf16[128,512]{1,0:T(8,128)(2,1)S(1)}, bf16[128,512]{1,0:T(8,128)(2,1)S(1)}, u32[]{:S(2)}, u32[]{:S(2)}) collective-permute-start(bf16[128,512]{1,0:T(8,128)(2,1)S(1)} %slice.109), channel_id=1, source_target_pairs={{0,32},{32,64},{64,96},{96,128},{128,160},{160,192},{192,224},{224... | collective-permute-start | bytes 393224 | tf_op jit(solution)/shard_map/ppermute | solution.py:26
  110.1 3.6 %collective-permute-done.12.rest_7_ = bf16[128,512]{1,0:T(8,128)(2,1)S(1)} collective-permute-done((bf16[128,512]{1,0:T(8,128)(2,1)S(1)}, bf16[128,512]{1,0:T(8,128)(2,1)S(1)}, u32[]{:S(2)}, u32[]{:S(2)}) %collective-permute-start.12) | collective-permute-done | bytes 131104 | tf_op jit(solution)/shard_map/ppermute | solution.py:26
  115.0 5.1 %collective-permute-start.14 = (bf16[1024,2048]{1,0:T(8,128)(2,1)}, bf16[1024,2048]{1,0:T(8,128)(2,1)}, u32[]{:S(2)}, u32[]{:S(2)}) collective-permute-start(bf16[1024,2048]{1,0:T(8,128)(2,1)} %all-gather.2.cloned.1.call-done.rows_ref), channel_id=1, source_target_pairs={{0,16},{16,0},{1,17},{17,1},{2,18},{18,2},{3,19},{19,3},{4,20},{20... | collective-permute-start | bytes 12582920 | tf_op jit(solution)/shard_map/ppermute | solution.py:22
  127.3 6.4 %near_rows.1 = (f32[1024,1024]{1,0:T(8,128)S(1)}, f32[8,128]{1,0:T(8,128)S(1)}, bf16[2048,512]{1,0:T(8,128)(2,1)S(1)}, f32[8,128]{1,0:T(8,128)S(1)}) custom-call(s32[3]{0:T(128)S(1)} %pad_add_fusion.ints, bf16[1024,2048]{1,0:T(8,128)(2,1)S(1)} %copy-done.1, bf16[4,2,128,512]{3,2,1,0:T(8,128)(2,1)S(1)} %bitcast.58, bf16[4,2,128,512]{3,2,1,0:T(8,128)(2,1)S(1)} %bitcast.60, ...), custom_call_target="tpu_custom_call" | custom-call | flops 4294967296 | bytes 12582912 | tf_op jit(solution)/shard_map/near_rows/pallas_call | solution.py:128
  133.7 8.7 %far_rows.1 = (f32[1024,1024]{1,0:T(8,128)S(1)}, f32[8,128]{1,0:T(8,128)}, f32[24,128]{1,0:T(8,128)S(1)}) custom-call(s32[3]{0:T(128)S(1)} %pad_add_fusion.ints, bf16[1024,2048]{1,0:T(8,128)(2,1)} %collective-permute-done.14.rows_ref, bf16[4,2,128,512]{3,2,1,0:T(8,128)(2,1)S(1)} %bitcast.59, bf16[4,2,128,512]{3,2,1,0:T(8,128)(2,1)S(1)} %bitcast.61, ...), custom_call_target="tpu_custom_call" | custom-call | flops 4294967296 | bytes 12582912 | tf_op jit(solution)/shard_map/far_rows/pallas_call | solution.py:128
  153.9 3.5 %collective-permute-done.17 = f32[24,128]{1,0:T(8,128)S(1)} collective-permute-done((f32[24,128]{1,0:T(8,128)S(1)}, f32[24,128]{1,0:T(8,128)S(1)}, u32[]{:S(2)}, u32[]{:S(2)}) %collective-permute-start.17) | collective-permute-done | bytes 12320 | tf_op jit(solution)/shard_map/ppermute | solution.py:22
  157.3 4.2 %collective-permute-start.18 = (f32[24,128]{1,0:T(8,128)S(1)}, f32[24,128]{1,0:T(8,128)S(1)}, u32[]{:S(2)}, u32[]{:S(2)}) collective-permute-start(f32[24,128]{1,0:T(8,128)S(1)} %add.93), channel_id=1, source_target_pairs={{0,128},{32,160},{64,192},{96,224},{128,0},{160,32},{192,64},{224,... | collective-permute-start | bytes 36872 | tf_op jit(solution)/shard_map/ppermute | solution.py:22
  161.5 4.4 %collective-permute-done.18 = f32[24,128]{1,0:T(8,128)S(1)} collective-permute-done((f32[24,128]{1,0:T(8,128)S(1)}, f32[24,128]{1,0:T(8,128)S(1)}, u32[]{:S(2)}, u32[]{:S(2)}) %collective-permute-start.18) | collective-permute-done | bytes 12320 | tf_op jit(solution)/shard_map/ppermute | solution.py:22
  173.0 3.5 %collective-permute-done.20 = f32[24,128]{1,0:T(8,128)S(1)} collective-permute-done((f32[24,128]{1,0:T(8,128)S(1)}, f32[24,128]{1,0:T(8,128)S(1)}, u32[]{:S(2)}, u32[]{:S(2)}) %collective-permute-start.20) | collective-permute-done | bytes 12320 | tf_op jit(solution)/shard_map/ppermute | solution.py:22
  176.5 4.9 %collective-permute-start.21 = (f32[24,128]{1,0:T(8,128)S(1)}, f32[24,128]{1,0:T(8,128)S(1)}, u32[]{:S(2)}, u32[]{:S(2)}) collective-permute-start(f32[24,128]{1,0:T(8,128)S(1)} %add.96), channel_id=1, source_target_pairs={{0,8},{2,10},{4,12},{6,14},{8,0},{10,2},{12,4},{14,6},{1,9},{3,11}... | collective-permute-start | bytes 36872 | tf_op jit(solution)/shard_map/ppermute | solution.py:22
  181.3 3.5 %collective-permute-done.21 = f32[24,128]{1,0:T(8,128)S(1)} collective-permute-done((f32[24,128]{1,0:T(8,128)S(1)}, f32[24,128]{1,0:T(8,128)S(1)}, u32[]{:S(2)}, u32[]{:S(2)}) %collective-permute-start.21) | collective-permute-done | bytes 12320 | tf_op jit(solution)/shard_map/ppermute | solution.py:22
  189.6 4.9 %collective-permute-start.23 = (f32[24,128]{1,0:T(8,128)S(1)}, f32[24,128]{1,0:T(8,128)S(1)}, u32[]{:S(2)}, u32[]{:S(2)}) collective-permute-start(f32[24,128]{1,0:T(8,128)S(1)} %add.98), channel_id=1, source_target_pairs={{0,1},{1,0},{2,3},{3,2},{4,5},{5,4},{6,7},{7,6},{8,9},{9,8},{10,11... | collective-permute-start | bytes 36872 | tf_op jit(solution)/shard_map/ppermute | solution.py:22
  201.9 10.1 %collective-permute-start.24 = (f32[64,512]{1,0:T(8,128)S(1)}, f32[64,512]{1,0:T(8,128)S(1)}, u32[]{:S(2)}, u32[]{:S(2)}) collective-permute-start(f32[64,512]{1,0:T(8,128)S(1)} %bitcast.64), channel_id=1, source_target_pairs={{0,0},{1,16},{16,1},{17,17},{256,256},{257,272},{272,257},{273,273... | collective-permute-start | bytes 393224 | tf_op jit(solution)/shard_map/ppermute | solution.py:254
  (115 shorter events, 71.5 us)
Async XLA Ops:
  7.2 107.8 %all-gather.2.cloned.1.call-start = ((), (), s32[]{:S(2)}) async-start(), calls=%async_computation.1 | async-start | bytes 4718592 | tf_op jit(solution)/shard_map/all_gather | solution.py:175
  9.8 20.5 %collective-permute-start = (bf16[128,2048]{1,0:T(8,128)(2,1)S(1)}, bf16[128,2048]{1,0:T(8,128)(2,1)S(1)}, u32[]{:S(2)}, u32[]{:S(2)}) collective-permute-start(bf16[128,2048]{1,0:T(8,128)(2,1)S(1)} %fusion.2), channel_id=1, source_target_pairs={{0,0},{1,16},{16,1},{17,17},{2,2},{3,18},{18,3},{19,19},{4,4},{5,2... | collective-permute-start | bytes 1572872 | tf_op jit(solution)/shard_map/ppermute | solution.py:172
  31.2 168.7 %reduce-scatter.2.cloned.1.call-start = ((), (), s32[]{:S(2)}) async-start(), calls=%async_computation.2 | async-start | bytes 4718592 | tf_op jit(solution)/shard_map/reduce_scatter | solution.py:236
  38.1 36.4 %collective-permute-start.4 = (bf16[1024,512]{1,0:T(8,128)(2,1)}, bf16[1024,512]{1,0:T(8,128)(2,1)S(1)}, u32[]{:S(2)}, u32[]{:S(2)}) collective-permute-start(bf16[1024,512]{1,0:T(8,128)(2,1)} %get-tuple-element.50), channel_id=1, source_target_pairs={{0,0},{1,16},{16,1},{17,17},{2,2},{3,18},{18,3},{19,19},{4,4},{5,2... | collective-permute-start | bytes 3145736 | tf_op jit(solution)/shard_map/ppermute | solution.py:195
  42.8 55.5 %collective-permute-start.11 = (bf16[1024,512]{1,0:T(8,128)(2,1)}, bf16[1024,512]{1,0:T(8,128)(2,1)S(1)}, u32[]{:S(2)}, u32[]{:S(2)}) collective-permute-start(bf16[1024,512]{1,0:T(8,128)(2,1)} %get-tuple-element.49), channel_id=1, source_target_pairs={{0,0},{1,16},{16,1},{17,17},{2,2},{3,18},{18,3},{19,19},{4,4},{5,2... | collective-permute-start | bytes 3145736 | tf_op jit(solution)/shard_map/ppermute | solution.py:198
  45.2 29.3 %collective-permute-start.2 = (bf16[272,512]{1,0:T(8,128)(2,1)S(1)}, bf16[272,512]{1,0:T(8,128)(2,1)S(1)}, u32[]{:S(2)}, u32[]{:S(2)}) collective-permute-start(bf16[272,512]{1,0:T(8,128)(2,1)S(1)} %concatenate.10.rest_0_), channel_id=1, source_target_pairs={{0,32},{32,64},{64,96},{96,128},{128,160},{160,192},{192,224},{224... | collective-permute-start | bytes 835592 | tf_op jit(solution)/shard_map/ppermute | solution.py:26
  49.3 25.2 %collective-permute-start.3 = (bf16[272,512]{1,0:T(8,128)(2,1)S(1)}, bf16[272,512]{1,0:T(8,128)(2,1)S(1)}, u32[]{:S(2)}, u32[]{:S(2)}) collective-permute-start(bf16[272,512]{1,0:T(8,128)(2,1)S(1)} %concatenate.10.rest_0_), channel_id=1, source_target_pairs={{0,224},{32,0},{64,32},{96,64},{128,96},{160,128},{192,160},{224,1... | collective-permute-start | bytes 835592 | tf_op jit(solution)/shard_map/ppermute | solution.py:26
  74.5 17.1 %collective-permute-start.5 = (bf16[272,512]{1,0:T(8,128)(2,1)S(1)}, bf16[272,512]{1,0:T(8,128)(2,1)S(1)}, u32[]{:S(2)}, u32[]{:S(2)}) collective-permute-start(bf16[272,512]{1,0:T(8,128)(2,1)S(1)} %collective-permute-done.2.rest_4_), channel_id=1, source_target_pairs={{0,32},{32,64},{64,96},{96,128},{128,160},{160,192},{192,224},{224... | collective-permute-start | bytes 835592 | tf_op jit(solution)/shard_map/ppermute | solution.py:26
  76.5 15.1 %collective-permute-start.6 = (bf16[272,512]{1,0:T(8,128)(2,1)S(1)}, bf16[272,512]{1,0:T(8,128)(2,1)S(1)}, u32[]{:S(2)}, u32[]{:S(2)}) collective-permute-start(bf16[272,512]{1,0:T(8,128)(2,1)S(1)} %collective-permute-done.3.rest_1_), channel_id=1, source_target_pairs={{0,224},{32,0},{64,32},{96,64},{128,96},{160,128},{192,160},{224,1... | collective-permute-start | bytes 835592 | tf_op jit(solution)/shard_map/ppermute | solution.py:26
  81.2 10.4 %collective-permute-start.7 = (f32[24,128]{1,0:T(8,128)S(1)}, f32[24,128]{1,0:T(8,128)S(1)}, u32[]{:S(2)}, u32[]{:S(2)}) collective-permute-start(f32[24,128]{1,0:T(8,128)S(1)} %maximum_maximum_fusion), channel_id=1, source_target_pairs={{0,0},{1,16},{16,1},{17,17},{2,2},{3,18},{18,3},{19,19},{4,4},{5,2... | collective-permute-start | bytes 36872 | tf_op jit(solution)/shard_map/ppermute | solution.py:192
  91.6 9.2 %collective-permute-start.10 = (bf16[272,512]{1,0:T(8,128)(2,1)S(1)}, bf16[272,512]{1,0:T(8,128)(2,1)S(1)}, u32[]{:S(2)}, u32[]{:S(2)}) collective-permute-start(bf16[272,512]{1,0:T(8,128)(2,1)S(1)} %collective-permute-done.6.rest_2_), channel_id=1, source_target_pairs={{0,224},{32,0},{64,32},{96,64},{128,96},{160,128},{192,160},{224,1... | collective-permute-start | bytes 835592 | tf_op jit(solution)/shard_map/ppermute | solution.py:26
  94.7 10.1 %collective-permute-start.9 = (bf16[272,512]{1,0:T(8,128)(2,1)S(1)}, bf16[272,512]{1,0:T(8,128)(2,1)S(1)}, u32[]{:S(2)}, u32[]{:S(2)}) collective-permute-start(bf16[272,512]{1,0:T(8,128)(2,1)S(1)} %collective-permute-done.5.rest_5_), channel_id=1, source_target_pairs={{0,32},{32,64},{64,96},{96,128},{128,160},{160,192},{192,224},{224... | collective-permute-start | bytes 835592 | tf_op jit(solution)/shard_map/ppermute | solution.py:26
  104.8 9.5 %collective-permute-start.13 = (bf16[144,512]{1,0:T(8,128)(2,1)S(1)}, bf16[144,512]{1,0:T(8,128)(2,1)S(1)}, u32[]{:S(2)}, u32[]{:S(2)}) collective-permute-start(bf16[144,512]{1,0:T(8,128)(2,1)S(1)} %slice.110), channel_id=1, source_target_pairs={{0,224},{32,0},{64,32},{96,64},{128,96},{160,128},{192,160},{224,1... | collective-permute-start | bytes 442376 | tf_op jit(solution)/shard_map/ppermute | solution.py:26
  106.7 6.9 %collective-permute-start.12 = (bf16[128,512]{1,0:T(8,128)(2,1)S(1)}, bf16[128,512]{1,0:T(8,128)(2,1)S(1)}, u32[]{:S(2)}, u32[]{:S(2)}) collective-permute-start(bf16[128,512]{1,0:T(8,128)(2,1)S(1)} %slice.109), channel_id=1, source_target_pairs={{0,32},{32,64},{64,96},{96,128},{128,160},{160,192},{192,224},{224... | collective-permute-start | bytes 393224 | tf_op jit(solution)/shard_map/ppermute | solution.py:26
  115.0 18.7 %collective-permute-start.14 = (bf16[1024,2048]{1,0:T(8,128)(2,1)}, bf16[1024,2048]{1,0:T(8,128)(2,1)}, u32[]{:S(2)}, u32[]{:S(2)}) collective-permute-start(bf16[1024,2048]{1,0:T(8,128)(2,1)} %all-gather.2.cloned.1.call-done.rows_ref), channel_id=1, source_target_pairs={{0,16},{16,0},{1,17},{17,1},{2,18},{18,2},{3,19},{19,3},{4,20},{20... | collective-permute-start | bytes 12582920 | tf_op jit(solution)/shard_map/ppermute | solution.py:22
  151.9 5.4 %collective-permute-start.17 = (f32[24,128]{1,0:T(8,128)S(1)}, f32[24,128]{1,0:T(8,128)S(1)}, u32[]{:S(2)}, u32[]{:S(2)}) collective-permute-start(f32[24,128]{1,0:T(8,128)S(1)} %add.92), channel_id=1, source_target_pairs={{0,64},{32,96},{64,0},{96,32},{128,192},{160,224},{192,128},{224,1... | collective-permute-start | bytes 36872 | tf_op jit(solution)/shard_map/ppermute | solution.py:22
  157.3 8.6 %collective-permute-start.18 = (f32[24,128]{1,0:T(8,128)S(1)}, f32[24,128]{1,0:T(8,128)S(1)}, u32[]{:S(2)}, u32[]{:S(2)}) collective-permute-start(f32[24,128]{1,0:T(8,128)S(1)} %add.93), channel_id=1, source_target_pairs={{0,128},{32,160},{64,192},{96,224},{128,0},{160,32},{192,64},{224,... | collective-permute-start | bytes 36872 | tf_op jit(solution)/shard_map/ppermute | solution.py:22
  170.7 5.7 %collective-permute-start.20 = (f32[24,128]{1,0:T(8,128)S(1)}, f32[24,128]{1,0:T(8,128)S(1)}, u32[]{:S(2)}, u32[]{:S(2)}) collective-permute-start(f32[24,128]{1,0:T(8,128)S(1)} %add.95), channel_id=1, source_target_pairs={{0,4},{2,6},{4,0},{6,2},{8,12},{10,14},{12,8},{14,10},{1,5},{3,7},... | collective-permute-start | bytes 36872 | tf_op jit(solution)/shard_map/ppermute | solution.py:22
  176.5 8.3 %collective-permute-start.21 = (f32[24,128]{1,0:T(8,128)S(1)}, f32[24,128]{1,0:T(8,128)S(1)}, u32[]{:S(2)}, u32[]{:S(2)}) collective-permute-start(f32[24,128]{1,0:T(8,128)S(1)} %add.96), channel_id=1, source_target_pairs={{0,8},{2,10},{4,12},{6,14},{8,0},{10,2},{12,4},{14,6},{1,9},{3,11}... | collective-permute-start | bytes 36872 | tf_op jit(solution)/shard_map/ppermute | solution.py:22
  189.6 6.1 %collective-permute-start.23 = (f32[24,128]{1,0:T(8,128)S(1)}, f32[24,128]{1,0:T(8,128)S(1)}, u32[]{:S(2)}, u32[]{:S(2)}) collective-permute-start(f32[24,128]{1,0:T(8,128)S(1)} %add.98), channel_id=1, source_target_pairs={{0,1},{1,0},{2,3},{3,2},{4,5},{5,4},{6,7},{7,6},{8,9},{9,8},{10,11... | collective-permute-start | bytes 36872 | tf_op jit(solution)/shard_map/ppermute | solution.py:22
  201.9 17.0 %collective-permute-start.24 = (f32[64,512]{1,0:T(8,128)S(1)}, f32[64,512]{1,0:T(8,128)S(1)}, u32[]{:S(2)}, u32[]{:S(2)}) collective-permute-start(f32[64,512]{1,0:T(8,128)S(1)} %bitcast.64), channel_id=1, source_target_pairs={{0,0},{1,16},{16,1},{17,17},{256,256},{257,272},{272,257},{273,273... | collective-permute-start | bytes 393224 | tf_op jit(solution)/shard_map/ppermute | solution.py:254
  212.1 6.8 %collective-permute-start.25 = (f32[64,512]{1,0:T(8,128)S(1)}, f32[64,512]{1,0:T(8,128)S(1)}, u32[]{:S(2)}, u32[]{:S(2)}) collective-permute-start(f32[64,512]{1,0:T(8,128)S(1)} %bitcast.65), channel_id=1, source_target_pairs={{0,16},{1,0},{16,17},{17,1},{256,272},{257,256},{272,273},{273,257... | collective-permute-start | bytes 393224 | tf_op jit(solution)/shard_map/ppermute | solution.py:254
  214.0 7.5 %collective-permute-start.26 = (f32[64,512]{1,0:T(8,128)S(1)}, f32[64,512]{1,0:T(8,128)S(1)}, u32[]{:S(2)}, u32[]{:S(2)}) collective-permute-start(f32[64,512]{1,0:T(8,128)S(1)} %bitcast.66), channel_id=1, source_target_pairs={{0,256},{1,272},{16,257},{17,273},{256,0},{257,16},{272,1},{273,17... | collective-permute-start | bytes 393224 | tf_op jit(solution)/shard_map/ppermute | solution.py:254
  215.9 6.7 %collective-permute-start.27 = (f32[64,512]{1,0:T(8,128)S(1)}, f32[64,512]{1,0:T(8,128)S(1)}, u32[]{:S(2)}, u32[]{:S(2)}) collective-permute-start(f32[64,512]{1,0:T(8,128)S(1)} %bitcast.67), channel_id=1, source_target_pairs={{0,272},{1,256},{16,273},{17,257},{256,16},{257,0},{272,17},{273,1... | collective-permute-start | bytes 393224 | tf_op jit(solution)/shard_map/ppermute | solution.py:254
  (21 other events, 211.3 us)
Sparse Core Ops, SparseCore 0:
  31.3 63.5 all-gather.1
  144.5 55.3 reduce-scatter.1

commit v3 on v0

v3 whole, which is shorter than its diff:
```python
import jax
import jax.numpy as jnp
from jax import lax
from jax.experimental import pallas as pl
from jax.experimental.pallas import tpu as pltpu
from jax.sharding import Mesh, PartitionSpec as P

TW = 8192
EPS = 1e-06
WIDE = 2176
F32, BF16 = jnp.float32, jnp.bfloat16
DP = ("xl", "z", "c")
TENSOR = ("y", "xh")


SWAP = [(0, 0), (1, 2), (2, 1), (3, 3)]


CROSS = [(c * 2 + xh, (1 - xh) * 2 + c) for c in (0, 1) for xh in (0, 1)]
VMEM = pl.BlockSpec(memory_space=pltpu.VMEM)
SMEM = pl.BlockSpec(memory_space=pltpu.SMEM)
HBM = pl.BlockSpec(memory_space=pltpu.HBM)


def flip(x, axis, size, bit):
    return lax.ppermute(x, axis, [(i, i ^ bit) for i in range(size)])


def shift(x, axis, size, by):
    return lax.ppermute(x, axis, [(i, (i + by) % size) for i in range(size)])


def corner(flip_xl, flip_c):
    return [
        (xl * 4 + c * 2 + xh, (xl ^ flip_xl) * 4 + (xh ^ flip_c) * 2 + c)
        for xl in (0, 1)
        for c in (0, 1)
        for xh in (0, 1)
    ]


def tie(*arrays):
    return lax.optimization_barrier(arrays)


def call(kernel, name, in_specs, out_specs, outs, scratch, flops, *args):
    return pl.pallas_call(
        kernel,
        in_specs=in_specs,
        out_specs=out_specs,
        out_shape=[jax.ShapeDtypeStruct(shape, dtype) for shape, dtype in outs],
        scratch_shapes=scratch,
        compiler_params=pltpu.CompilerParams(vmem_limit_bytes=20 * 2**20),
        cost_estimate=pl.CostEstimate(flops=flops, bytes_accessed=6 * 2**20, transcendentals=0),
        name=name,
    )(*args)


def put_parts(out_ref, x):
    for part in range(3):
        rounded = x.astype(BF16)
        out_ref[part * 16 : part * 16 + 16, 2048:] = rounded
        x = x - rounded.astype(F32)


def head_kernel(teacher_ref, student_ref, student_gain_ref, out_ref, squares_ref):
    student_f = student_ref[...].astype(F32)
    mean = jnp.sum(student_f * student_f, axis=1, keepdims=True) / 2048
    out_ref[:, :2048] = (student_f * lax.rsqrt(mean + EPS) * student_gain_ref[...]).astype(BF16)
    out_ref[:, 2048:] = jnp.zeros((128, 128), BF16)
    squares = []
    for i in range(16):
        t = teacher_ref[i * 128 : (i + 1) * 128, :].astype(F32)
        t = t * t
        t = t[:, :128] + t[:, 128:256] + t[:, 256:384] + t[:, 384:]
        squares.append(jnp.sum(t.T, axis=0, keepdims=True))
    squares = jnp.concatenate(squares, axis=0)
    squares_ref[...] = squares
    put_parts(out_ref, squares)


def join_kernel(rows_ref, cross_ref, out_ref, buffer, sem):
    buffer[...] = rows_ref[...]
    squares = cross_ref[...]
    for part in (2, 1, 0):
        squares += rows_ref[part * 16 : part * 16 + 16, 2048:].astype(F32)
    put_parts(buffer, squares)
    copy = pltpu.make_async_copy(buffer, out_ref, sem)
    copy.start()
    copy.wait()


def place_kernel(z_ref, *rest):
    shards, (proj_ref, count_ref) = rest[:9], rest[9:]
    z = z_ref[0]
    tails = jnp.zeros((16, 512), F32)
    for offset, shard in zip((0, 1, 2, 3, -1, -2, -3), shards):
        at = lax.rem(z + (offset + 8), 8) * 128
        for x in range(2):
            proj_ref[pl.ds(pl.multiple_of(x * 1024 + at, 128), 128), :] = shard[x * 128 : (x + 1) * 128, :]
        tails += shard[256:272, :].astype(F32)
    at = lax.rem(z + 4, 8) * 128
    proj_ref[pl.ds(pl.multiple_of(at, 128), 128), :] = shards[7][...]
    proj_ref[pl.ds(pl.multiple_of(1024 + at, 128), 128), :] = shards[8][:128, :]
    tails += shards[8][128:144, :].astype(F32)
    lane = lax.broadcasted_iota(jnp.int32, (16, 512), 1)
    weight = jnp.where(lane == 0, 4.0, jnp.where(lane == 1, 0.25, 0.0))
    count_ref[...] = jnp.full((8, 128), jnp.sum(tails * weight), F32)


def load_rows(rows_hbm, rows, sems):
    copies = [
        pltpu.make_async_copy(rows_hbm.at[pl.ds(i * 4, 4)], rows.at[pl.ds(i * 4, 4)], sems.at[i]) for i in range(2)
    ]
    for copy in copies:
        copy.start()
    return copies


def slopes(i, half, length, factor, rows, proj_ref, teacher_ref, scale, gain):
    predicted = jnp.dot(rows, proj_ref[...], preferred_element_type=F32)
    lane = lax.broadcasted_iota(jnp.int32, (128, 128), 1)
    row = lax.broadcasted_iota(jnp.int32, (128, 1), 0)
    loss = jnp.zeros((8, 512), F32)
    found = []
    for b in range(4):
        place = (i * 4 + b) * 2 + half
        s = jnp.sum(jnp.where(lane == place, scale, 0.0), axis=1, keepdims=True)
        target = teacher_ref[i * 4 + b, half].astype(F32) * s * gain
        valid = (place * 128 + row) < length
        diff = jnp.where(valid, predicted[b * 128 : (b + 1) * 128] - target, 0.0)
        found.append((diff * factor).astype(BF16))
        loss += jnp.sum((diff * diff).reshape(16, 8, 512), axis=0)
    loss = loss[:, :128] + loss[:, 128:256] + loss[:, 256:384] + loss[:, 384:]
    return jnp.concatenate(found, axis=0), loss


def grad_part(rows, slope, x):
    return lax.dot_general(
        rows[:, x * 1024 : (x + 1) * 1024], slope, (((0,), (0,)), ((), ())), preferred_element_type=F32
    )


def columns(scale):
    return jnp.concatenate([scale, jnp.zeros((112, 128), F32)], axis=0).T


def near_kernel(ints, rows_hbm, proj_ref, count_ref, teacher_ref, gain_ref, *rest):
    grad_ref, loss_ref, scale_ref, rows_ref, notes, sems = rest
    notes_copy = pltpu.make_async_copy(rows_hbm.at[:, pl.ds(0, 48), pl.ds(2048, 128)], notes, sems.at[2])
    notes_copy.start()
    copies = load_rows(rows_hbm, rows_ref, sems)
    notes_copy.wait()
    squares = jnp.zeros((16, 128), F32)
    for part in (2, 1, 0):
        for y in range(8):
            squares += notes[y, part * 16 : part * 16 + 16, :].astype(F32)
    scale = lax.rsqrt(squares / TW + EPS)
    scale_ref[...] = scale
    scale = columns(scale)
    factor = 2.0 / count_ref[0:1, 0:1]
    for i in range(2):
        copies[i].wait()
        rows = rows_ref[i * 4 : i * 4 + 4, :, :2048].reshape(512, 2048)
        slope, loss = slopes(i, ints[0], ints[1], factor, rows, proj_ref, teacher_ref, scale, gain_ref[...])
        loss_ref[...] = loss if i == 0 else loss_ref[...] + loss
        for x in range(2):
            lanes = slice(x * 512, (x + 1) * 512)
            part = grad_part(rows, slope, x)
            grad_ref[:, lanes] = part if i == 0 else grad_ref[:, lanes] + part


def far_kernel(ints, rows_hbm, proj_ref, count_ref, teacher_ref, gain_ref, *rest):
    scale_ref, grad_in, loss_in, grad_hbm, sums_ref, rows_ref, total, sems = rest
    copies = load_rows(rows_hbm, rows_ref, sems)
    scale = columns(scale_ref[...])
    factor = 2.0 / count_ref[0:1, 0:1]
    sums_ref[16:24, :] = loss_in[...]
    out = []
    for i in range(2):
        copies[i].wait()
        rows = rows_ref[i * 4 : i * 4 + 4, :, :2048].reshape(512, 2048)
        slope, loss = slopes(i, 1 - ints[0], ints[1], factor, rows, proj_ref, teacher_ref, scale, gain_ref[...])
        sums_ref[16:24, :] += loss
        for x in range(2):
            lanes = slice(x * 512, (x + 1) * 512)
            part = grad_part(rows, slope, x)
            total[x] = (grad_in[:, lanes] if i == 0 else total[x]) + part
            if i == 1:
                copy = pltpu.make_async_copy(total.at[x], grad_hbm.at[:, pl.ds(x * 512, 512)], sems.at[2 + x])
                copy.start()
                out.append(copy)
    for x in range(2):
        g = total[x] * proj_ref[x * 1024 : (x + 1) * 1024, :].astype(F32)
        g = g[:, :128] + g[:, 128:256] + g[:, 256:384] + g[:, 384:]
        sums_ref[x * 8 : (x + 1) * 8, :] = jnp.sum(g.reshape(8, 128, 128), axis=2)
    for copy in out:
        copy.wait()


def own_rows(projection, teacher_gain, lengths):
    length = lengths[0]
    lane = lax.broadcasted_iota(jnp.int32, (8, 512), 1)
    digits = jnp.where(lane == 0, length >> 4, jnp.where(lane == 1, length & 15, 0)).astype(BF16)
    return jnp.concatenate([projection, digits, jnp.broadcast_to(teacher_gain, (8, 512))], axis=0)


def projection_flips(own):
    return [
        lax.ppermute(own, ("xl", "xh"), [(i, i ^ (fx * 2 + fc)) for i in range(4)]) for fx, fc in ((0, 1), (1, 0), (1, 1))
    ]


def projection_block(own, by_xh, by_xl, by_both):
    xl, xh = lax.axis_index("xl"), lax.axis_index("xh")
    parts = []
    for x in (0, 1):
        for k in (0, 1):
            a = jnp.where(xh == k, own, by_xh)
            b = jnp.where(xh == k, by_xl, by_both)
            parts.append(jnp.where(xl == x, a, b))
    return jnp.concatenate([p[:64] for p in parts] + [p[64:68] for p in parts], axis=0)


def on_device(teacher_hidden, teacher_gain, student_hidden, student_gain, projection, lengths):
    c, xl, xh, z = (lax.axis_index(a) for a in ("c", "xl", "xh", "z"))
    own = lax.ppermute(own_rows(projection, teacher_gain, lengths), ("c", "xh"), SWAP)
    scaled, squares = call(
        head_kernel,
        "head",
        [VMEM] * 3,
        [VMEM] * 2,
        [((128, WIDE), BF16), ((16, 128), F32)],
        [],
        10**7,
        teacher_hidden,
        student_hidden,
        student_gain.reshape(1, 2048),
    )
    scaled, squares, own = tie(scaled, squares, own)
    scaled = lax.ppermute(scaled, ("c", "xh"), SWAP)
    cross = lax.ppermute(squares, ("c", "xh"), CROSS)
    flips = projection_flips(own)
    scaled, cross, *flips = tie(scaled, cross, *flips)
    (joined,) = call(
        join_kernel,
        "join",
        [VMEM] * 2,
        [HBM],
        [((128, WIDE), BF16)],
        [pltpu.VMEM((128, WIDE), BF16), pltpu.SemaphoreType.DMA],
        10**5,
        scaled,
        cross,
    )
    near = lax.all_gather(joined, "y", axis=0, tiled=True)

    flips, _ = tie(flips, joined)
    block = projection_block(own, *flips)
    up1, down1 = shift(block, "z", 8, 1), shift(block, "z", 8, -1)
    teacher, _ = tie(teacher_hidden, block)
    teacher = lax.ppermute(teacher, ("c", "xh"), SWAP)
    up2, down2 = shift(up1, "z", 8, 1), shift(down1, "z", 8, -1)
    up3, down3 = shift(up2, "z", 8, 1), shift(down2, "z", 8, -1)
    up3, down3, teacher = tie(up3, down3, teacher)
    teacher = teacher.reshape(8, 2, 128, 512)
    up4 = shift(up3[:128], "z", 8, 1)
    down4 = shift(down3[128:], "z", 8, -1)
    proj_full, count = call(
        place_kernel,
        "place",
        [SMEM] + [VMEM] * 9,
        [VMEM] * 2,
        [((2048, 512), BF16), ((8, 128), F32)],
        [],
        10**6,
        z.reshape(1),
        *(block, down1, down2, down3, up1, up2, up3, up4, down4),
    )
    gain = own[72:73].astype(F32)
    length = (own[64, 0].astype(F32) * 16 + own[64, 1].astype(F32)).astype(jnp.int32)
    ints = jnp.stack([c, length]).astype(jnp.int32)
    near, proj_full, ints, gain = tie(near, proj_full, ints, gain)
    far = flip(near, "c", 2, 1)
    grad, loss_part, scale = call(
        near_kernel,
        "near_rows",
        [SMEM, HBM] + [VMEM] * 4,
        [VMEM] * 3,
        [((1024, 1024), F32), ((8, 128), F32), ((16, 128), F32)],
        [pltpu.VMEM((8, 128, WIDE), BF16), pltpu.VMEM((8, 48, 128), BF16), pltpu.SemaphoreType.DMA((3,))],
        4 * 1024 * 2048 * 512,
        *(ints, near.reshape(8, 128, WIDE), proj_full, count, teacher, gain),
    )
    grad, sums = call(
        far_kernel,
        "far_rows",
        [SMEM, HBM] + [VMEM] * 7,
        [HBM, VMEM],
        [((1024, 1024), F32), ((24, 128), F32)],
        [pltpu.VMEM((8, 128, WIDE), BF16), pltpu.VMEM((2, 1024, 512), F32), pltpu.SemaphoreType.DMA((4,))],
        4 * 1024 * 2048 * 512,
        *(ints, far.reshape(8, 128, WIDE), proj_full, count, teacher, gain, scale, grad, loss_part),
    )
    mine = lax.psum_scatter(grad, "z", scatter_dimension=0, tiled=True)

    for axis, size, bit in (
        ("c", 2, 1),
        ("z", 8, 1),
        ("z", 8, 2),
        ("z", 8, 4),
        ("y", 8, 1),
        ("y", 8, 2),
        ("y", 8, 4),
        ("xl", 2, 1),
        ("xh", 2, 1),
    ):
        sums = sums + flip(sums, axis, size, bit)
    grad_proj = jnp.zeros((64, 512), F32)
    for fx in (0, 1):
        for fc in (0, 1):
            send = lax.dynamic_slice(mine, ((xh ^ fc) * 64, (xl ^ fx) * 512), (64, 512))
            grad_proj += lax.ppermute(send, ("xl", "c", "xh"), corner(fx, fc))
    loss = jnp.sum(sums[16:]) / (count[0, 0] * TW)
    grad_gain = sums[:16].reshape(2048) / student_gain
    return (loss, grad_gain, grad_proj)


def solution(mesh):
    parts = Mesh(mesh.devices.reshape(2, 8, 2, 8, 2), DP + TENSOR)
    return jax.shard_map(
        on_device,
        mesh=parts,
        in_specs=(P(DP, TENSOR), P(TENSOR), P(DP + TENSOR, None), P(), P(DP, TENSOR), P(DP)),
        out_specs=(P(), P(), P(DP, TENSOR)),
        check_vma=False,
    )
```

time: 379 us -> 214 us (0.56)
  blocking collectives: 195 us -> 0 us
  starting transfers between devices: 0.12 us -> 110 us
  waiting for transfers between devices: 130 us -> 47.1 us
  Pallas kernels: 0 us -> 19.2 us
  matrix products: 15.9 us -> 0 us
    psum x3 -> x0, blocking collectives: 195 us -> none  [the longest x1 98.6 us: on_device(): loss_all, gain_all = lax.psum((loss_part, gain_part), ('dp', 'tensor'))]
    ppermute x0 -> x29, starting transfers between devices: none -> 110 us  [the longest x10 37.7 us: flip(): return lax.ppermute(x, axis, [(i, i ^ bit) for i in range(size)])]
    all_gather x2 -> x1, waiting for transfers between devices: 110 us -> 11.9 us  [on_device(): near = lax.all_gather(joined, 'y', axis=0, tiled=True)]
    ppermute x0 -> x29, waiting for transfers between devices: none -> 30 us  [the longest x10 15.2 us: flip(): return lax.ppermute(x, axis, [(i, i ^ bit) for i in range(size)])]
    unnamed x4 -> x2, waiting for transfers between devices: 20.1 us -> 0.03 us
    pallas_call x0 -> x5, Pallas kernels: none -> 19.2 us  [call(): pl.pallas_call(kernel, in_specs=in_specs, out_specs=out_specs, out_shape=...]
    dot_general x2 -> x0, matrix products: 15.9 us -> none  [the longest x1 9.66 us: on_device(): jnp.dot(block_rows, proj_full, preferred_element_type=jnp.float32)]
    reduce_scatter x0 -> x1, waiting for transfers between devices: none -> 5.17 us  [on_device(): mine = lax.psum_scatter(grad, 'z', scatter_dimension=0, tiled=True)]
  transfers between devices with their start and end apart: 3 -> 31, of which waited for: 2 -> 18; matrix products, arithmetic and copies ran while one was open for 3% -> 2% of each run, Pallas kernels for 0% -> 4%
where the time goes in v3:
time: 214 us; the launch traced here: 211 us
  starting transfers between devices  110 us (51%)
  waiting for transfers between devices  47.1 us (22%)
  Pallas kernels  19.2 us (9%)
  between operations  19 us (9%)
  local copies, waits for them, and re-layouts  12.9 us (6%)
  other arithmetic  3.61 us (2%)
    ppermute x10, starting transfers between devices, flip(): return lax.ppermute(x, axis, [(i, i ^ bit) for i in range(size)])  37.7 us
    ppermute x8, starting transfers between devices, shift(): return lax.ppermute(x, axis, [(i, (i + by) % size) for i in range(size)])  32.7 us
    pallas_call x5, Pallas kernels, call(): pl.pallas_call(kernel, in_specs=in_specs, out_specs=out_specs, out_shape=...  19.2 us
    ppermute x10, waiting for transfers between devices, flip(): return lax.ppermute(x, axis, [(i, i ^ bit) for i in range(size)])  15.2 us
    ppermute x4, starting transfers between devices, on_device(): grad_proj += lax.ppermute(send, ('xl', 'c', 'xh'), corner(fx, fc))  13.7 us
    all_gather x1, waiting for transfers between devices, on_device(): near = lax.all_gather(joined, 'y', axis=0, tiled=True)  11.9 us
    ppermute x8, waiting for transfers between devices, shift(): return lax.ppermute(x, axis, [(i, (i + by) % size) for i in range(size)])  11 us
    unnamed x20, local copies, waits for them, and re-layouts  9.13 us
  transfers between devices with their start and end apart: 31, of which 18 were waited for; matrix products, arithmetic and copies ran while one was open for 2% of the time, Pallas kernels for 4%

profile of v3, /device:TPU:1, one launch (start us, length us, event | category | flops | bytes accessed | tf_op | source)
XLA Modules:
  0.0 211.4 jit_solution(5953400851621139853)
XLA Ops:
  9.4 6.0 %collective-permute-start = (bf16[80,512]{1,0:T(8,128)(2,1)S(1)}, bf16[80,512]{1,0:T(8,128)(2,1)S(1)}, u32[]{:S(2)}, u32[]{:S(2)}) collective-permute-start(bf16[80,512]{1,0:T(8,128)(2,1)S(1)} %pad_maximum_fusion), channel_id=1, source_target_pairs={{0,0},{1,16},{16,1},{17,17},{2,2},{3,18},{18,3},{19,19},{4,4},{5,2... | collective-permute-start | bytes 245768 | tf_op jit(solution)/shard_map/ppermute | solution.py:227
  19.5 3.2 %collective-permute-start.1 = (bf16[128,2176]{1,0:T(8,128)(2,1)S(1)}, bf16[128,2176]{1,0:T(8,128)(2,1)S(1)}, u32[]{:S(2)}, u32[]{:S(2)}) collective-permute-start(bf16[128,2176]{1,0:T(8,128)(2,1)S(1)} %get-tuple-element.33), channel_id=1, source_target_pairs={{0,0},{1,16},{16,1},{17,17},{2,2},{3,18},{18,3},{19,19},{4,4},{5,2... | collective-permute-start | bytes 1671176 | tf_op jit(solution)/shard_map/ppermute | solution.py:241
  26.9 4.8 %collective-permute-start.5 = (bf16[80,512]{1,0:T(8,128)(2,1)S(1)}, bf16[80,512]{1,0:T(8,128)(2,1)S(1)}, u32[]{:S(2)}, u32[]{:S(2)}) collective-permute-start(bf16[80,512]{1,0:T(8,128)(2,1)S(1)} %collective-permute-done), channel_id=1, source_target_pairs={{0,257},{1,256},{256,1},{257,0},{2,259},{3,258},{258,3},{259,2},{4... | collective-permute-start | bytes 245768 | tf_op jit(solution)/shard_map/ppermute | solution.py:210
  36.3 4.8 %collective-permute-start.12 = (bf16[2048,512]{1,0:T(8,128)(2,1)S(1)}, bf16[2048,512]{1,0:T(8,128)(2,1)}, u32[]{:S(2)}, u32[]{:S(2)}) collective-permute-start(bf16[2048,512]{1,0:T(8,128)(2,1)S(1)} %copy-done.2), channel_id=1, source_target_pairs={{0,0},{1,16},{16,1},{17,17},{2,2},{3,18},{18,3},{19,19},{4,4},{5,2... | collective-permute-start | bytes 6291464 | tf_op jit(solution)/shard_map/ppermute | solution.py:262
  41.1 3.9 %collective-permute-start.8 = (bf16[272,512]{1,0:T(8,128)(2,1)S(1)}, bf16[272,512]{1,0:T(8,128)(2,1)S(1)}, u32[]{:S(2)}, u32[]{:S(2)}) collective-permute-start(bf16[272,512]{1,0:T(8,128)(2,1)S(1)} %concatenate.7.rest_0_), channel_id=1, source_target_pairs={{0,32},{32,64},{64,96},{96,128},{128,160},{160,192},{192,224},{224... | collective-permute-start | bytes 835592 | tf_op jit(solution)/shard_map/ppermute | solution.py:30
  45.0 8.6 %collective-permute-start.6 = (bf16[272,512]{1,0:T(8,128)(2,1)S(1)}, bf16[272,512]{1,0:T(8,128)(2,1)S(1)}, u32[]{:S(2)}, u32[]{:S(2)}) collective-permute-start(bf16[272,512]{1,0:T(8,128)(2,1)S(1)} %concatenate.7.rest_0_), channel_id=1, source_target_pairs={{0,224},{32,0},{64,32},{96,64},{128,96},{160,128},{192,160},{224,1... | collective-permute-start | bytes 835592 | tf_op jit(solution)/shard_map/ppermute | solution.py:30
  53.6 4.4 %collective-permute-done.8.rest_4_ = bf16[272,512]{1,0:T(8,128)(2,1)S(1)} collective-permute-done((bf16[272,512]{1,0:T(8,128)(2,1)S(1)}, bf16[272,512]{1,0:T(8,128)(2,1)S(1)}, u32[]{:S(2)}, u32[]{:S(2)}) %collective-permute-start.8) | collective-permute-done | bytes 278560 | tf_op jit(solution)/shard_map/ppermute | solution.py:30
  59.9 4.6 %collective-permute-start.7 = (bf16[272,512]{1,0:T(8,128)(2,1)S(1)}, bf16[272,512]{1,0:T(8,128)(2,1)}, u32[]{:S(2)}, u32[]{:S(2)}) collective-permute-start(bf16[272,512]{1,0:T(8,128)(2,1)S(1)} %collective-permute-done.6.rest_1_), channel_id=1, source_target_pairs={{0,224},{32,0},{64,32},{96,64},{128,96},{160,128},{192,160},{224,1... | collective-permute-start | bytes 835592 | tf_op jit(solution)/shard_map/ppermute | solution.py:30
  64.4 3.5 %collective-permute-done.9.rest_5_ = bf16[272,512]{1,0:T(8,128)(2,1)} collective-permute-done((bf16[272,512]{1,0:T(8,128)(2,1)S(1)}, bf16[272,512]{1,0:T(8,128)(2,1)}, u32[]{:S(2)}, u32[]{:S(2)}) %collective-permute-start.9) | collective-permute-done | bytes 278560 | tf_op jit(solution)/shard_map/ppermute | solution.py:30
  69.9 4.6 %collective-permute-start.11 = (bf16[272,512]{1,0:T(8,128)(2,1)}, bf16[272,512]{1,0:T(8,128)(2,1)S(1)}, u32[]{:S(2)}, u32[]{:S(2)}) collective-permute-start(bf16[272,512]{1,0:T(8,128)(2,1)} %collective-permute-done.7.rest_2_), channel_id=1, source_target_pairs={{0,224},{32,0},{64,32},{96,64},{128,96},{160,128},{192,160},{224,1... | collective-permute-start | bytes 835592 | tf_op jit(solution)/shard_map/ppermute | solution.py:30
  80.2 5.3 %collective-permute-start.14 = (bf16[144,512]{1,0:T(8,128)(2,1)S(1)}, bf16[144,512]{1,0:T(8,128)(2,1)S(1)}, u32[]{:S(2)}, u32[]{:S(2)}) collective-permute-start(bf16[144,512]{1,0:T(8,128)(2,1)S(1)} %slice.57), channel_id=1, source_target_pairs={{0,224},{32,0},{64,32},{96,64},{128,96},{160,128},{192,160},{224,1... | collective-permute-start | bytes 442376 | tf_op jit(solution)/shard_map/ppermute | solution.py:30
  89.6 11.9 %all-gather.2.cloned.1.call-done = bf16[1024,2176]{1,0:T(8,128)(2,1)} async-done(((bf16[128,2176]{1,0:T(8,128)(2,1)}), bf16[1024,2176]{1,0:T(8,128)(2,1)}) %all-gather.2.cloned.1.call-update) | async-done | bytes 4456464 | tf_op jit(solution)/shard_map/all_gather | solution.py:256
  106.4 7.4 %near_rows.1 = (f32[1024,1024]{1,0:T(8,128)S(1)}, f32[8,128]{1,0:T(8,128)S(1)}, f32[16,128]{1,0:T(8,128)S(1)}) custom-call(s32[2]{0:T(128)S(1)} %pad_add_fusion.ints, bf16[8,128,2176]{2,1,0:T(8,128)(2,1)S(1)} %bitcast.15, bf16[2048,512]{1,0:T(8,128)(2,1)S(1)} %get-tuple-element.50.proj_ref, f32[8,128]{1,0:T(8,128)S(1)} %get-tuple-element.51.count_ref, ...), custom_call_target="tpu_custom_call" | custom-call | flops 4294967296 | bytes 6291456 | tf_op jit(solution)/shard_map/near_rows/pallas_call | solution.py:47
  115.4 8.9 %far_rows.1 = (f32[1024,1024]{1,0:T(8,128)S(1)}, f32[24,128]{1,0:T(8,128)S(1)}) custom-call(s32[2]{0:T(128)S(1)} %pad_add_fusion.ints, bf16[8,128,2176]{2,1,0:T(8,128)(2,1)S(1)} %bitcast.16, bf16[2048,512]{1,0:T(8,128)(2,1)S(1)} %copy-done.8, f32[8,128]{1,0:T(8,128)S(1)} %get-tuple-element.51.count_ref, bf16[8,2,128,512]{3,2,1,0:T(8,128)(2,1)} %bitcast.7.teacher_ref, ...), custom_call_target="tpu_custom_call" | custom-call | flops 4294967296 | bytes 6291456 | tf_op jit(solution)/shard_map/far_rows/pallas_call | solution.py:47
  129.4 3.3 %collective-permute-start.17 = (f32[24,128]{1,0:T(8,128)S(1)}, f32[24,128]{1,0:T(8,128)S(1)}, u32[]{:S(2)}, u32[]{:S(2)}) collective-permute-start(f32[24,128]{1,0:T(8,128)S(1)} %add.59), channel_id=1, source_target_pairs={{0,32},{32,0},{64,96},{96,64},{128,160},{160,128},{192,224},{224,1... | collective-permute-start | bytes 36872 | tf_op jit(solution)/shard_map/ppermute | solution.py:26
  133.8 4.3 %collective-permute-start.18 = (f32[24,128]{1,0:T(8,128)S(1)}, f32[24,128]{1,0:T(8,128)S(1)}, u32[]{:S(2)}, u32[]{:S(2)}) collective-permute-start(f32[24,128]{1,0:T(8,128)S(1)} %add.60), channel_id=1, source_target_pairs={{0,64},{32,96},{64,0},{96,32},{128,192},{160,224},{192,128},{224,1... | collective-permute-start | bytes 36872 | tf_op jit(solution)/shard_map/ppermute | solution.py:26
  139.2 7.6 %collective-permute-start.19 = (f32[24,128]{1,0:T(8,128)S(1)}, f32[24,128]{1,0:T(8,128)S(1)}, u32[]{:S(2)}, u32[]{:S(2)}) collective-permute-start(f32[24,128]{1,0:T(8,128)S(1)} %add.61), channel_id=1, source_target_pairs={{0,128},{32,160},{64,192},{96,224},{128,0},{160,32},{192,64},{224,... | collective-permute-start | bytes 36872 | tf_op jit(solution)/shard_map/ppermute | solution.py:26
  153.0 3.6 %collective-permute-start.21 = (f32[24,128]{1,0:T(8,128)S(1)}, f32[24,128]{1,0:T(8,128)S(1)}, u32[]{:S(2)}, u32[]{:S(2)}) collective-permute-start(f32[24,128]{1,0:T(8,128)S(1)} %add.63), channel_id=1, source_target_pairs={{0,4},{2,6},{4,0},{6,2},{8,12},{10,14},{12,8},{14,10},{1,5},{3,7},... | collective-permute-start | bytes 36872 | tf_op jit(solution)/shard_map/ppermute | solution.py:26
  158.7 4.7 %collective-permute-start.22 = (f32[24,128]{1,0:T(8,128)S(1)}, f32[24,128]{1,0:T(8,128)S(1)}, u32[]{:S(2)}, u32[]{:S(2)}) collective-permute-start(f32[24,128]{1,0:T(8,128)S(1)} %add.64), channel_id=1, source_target_pairs={{0,8},{2,10},{4,12},{6,14},{8,0},{10,2},{12,4},{14,6},{1,9},{3,11}... | collective-permute-start | bytes 36872 | tf_op jit(solution)/shard_map/ppermute | solution.py:26
  163.5 3.6 %collective-permute-done.22 = f32[24,128]{1,0:T(8,128)S(1)} collective-permute-done((f32[24,128]{1,0:T(8,128)S(1)}, f32[24,128]{1,0:T(8,128)S(1)}, u32[]{:S(2)}, u32[]{:S(2)}) %collective-permute-start.22) | collective-permute-done | bytes 12320 | tf_op jit(solution)/shard_map/ppermute | solution.py:26
  171.9 4.6 %collective-permute-start.24 = (f32[24,128]{1,0:T(8,128)S(1)}, f32[24,128]{1,0:T(8,128)S(1)}, u32[]{:S(2)}, u32[]{:S(2)}) collective-permute-start(f32[24,128]{1,0:T(8,128)S(1)} %add.66), channel_id=1, source_target_pairs={{0,1},{1,0},{2,3},{3,2},{4,5},{5,4},{6,7},{7,6},{8,9},{9,8},{10,11... | collective-permute-start | bytes 36872 | tf_op jit(solution)/shard_map/ppermute | solution.py:26
  179.1 5.2 %reduce-scatter.2.cloned.1.call-done = f32[128,1024]{1,0:T(8,128)} async-done(((f32[1024,1024]{1,0:T(8,128)}), f32[128,1024]{1,0:T(8,128)}) %reduce-scatter.2.cloned.1.call-update) | async-done | bytes 524304 | tf_op jit(solution)/shard_map/reduce_scatter | solution.py:305
  185.4 4.3 %collective-permute-start.28 = (f32[64,512]{1,0:T(8,128)S(1)}, f32[64,512]{1,0:T(8,128)S(1)}, u32[]{:S(2)}, u32[]{:S(2)}) collective-permute-start(f32[64,512]{1,0:T(8,128)S(1)} %get-tuple-element.60), channel_id=1, source_target_pairs={{0,272},{1,256},{16,273},{17,257},{256,16},{257,0},{272,17},{273,1... | collective-permute-start | bytes 393224 | tf_op jit(solution)/shard_map/ppermute | solution.py:323
  189.8 5.2 %collective-permute-start.27 = (f32[64,512]{1,0:T(8,128)S(1)}, f32[64,512]{1,0:T(8,128)S(1)}, u32[]{:S(2)}, u32[]{:S(2)}) collective-permute-start(f32[64,512]{1,0:T(8,128)S(1)} %get-tuple-element.61), channel_id=1, source_target_pairs={{0,256},{1,272},{16,257},{17,273},{256,0},{257,16},{272,1},{273,17... | collective-permute-start | bytes 393224 | tf_op jit(solution)/shard_map/ppermute | solution.py:323
  (99 shorter events, 64.1 us)
Async XLA Ops:
  7.2 94.4 %all-gather.2.cloned.1.call-start = ((), (), s32[]{:S(2)}) async-start(), calls=%async_computation.1 | async-start | bytes 5013504 | tf_op jit(solution)/shard_map/all_gather | solution.py:256
  9.4 10.1 %collective-permute-start = (bf16[80,512]{1,0:T(8,128)(2,1)S(1)}, bf16[80,512]{1,0:T(8,128)(2,1)S(1)}, u32[]{:S(2)}, u32[]{:S(2)}) collective-permute-start(bf16[80,512]{1,0:T(8,128)(2,1)S(1)} %pad_maximum_fusion), channel_id=1, source_target_pairs={{0,0},{1,16},{16,1},{17,17},{2,2},{3,18},{18,3},{19,19},{4,4},{5,2... | collective-permute-start | bytes 245768 | tf_op jit(solution)/shard_map/ppermute | solution.py:227
  19.5 15.6 %collective-permute-start.1 = (bf16[128,2176]{1,0:T(8,128)(2,1)S(1)}, bf16[128,2176]{1,0:T(8,128)(2,1)S(1)}, u32[]{:S(2)}, u32[]{:S(2)}) collective-permute-start(bf16[128,2176]{1,0:T(8,128)(2,1)S(1)} %get-tuple-element.33), channel_id=1, source_target_pairs={{0,0},{1,16},{16,1},{17,17},{2,2},{3,18},{18,3},{19,19},{4,4},{5,2... | collective-permute-start | bytes 1671176 | tf_op jit(solution)/shard_map/ppermute | solution.py:241
  22.7 12.3 %collective-permute-start.3 = (bf16[80,512]{1,0:T(8,128)(2,1)S(1)}, bf16[80,512]{1,0:T(8,128)(2,1)S(1)}, u32[]{:S(2)}, u32[]{:S(2)}) collective-permute-start(bf16[80,512]{1,0:T(8,128)(2,1)S(1)} %collective-permute-done), channel_id=1, source_target_pairs={{0,1},{1,0},{256,257},{257,256},{2,3},{3,2},{258,259},{259,258},{4... | collective-permute-start | bytes 245768 | tf_op jit(solution)/shard_map/ppermute | solution.py:210
  24.7 10.4 %collective-permute-start.4 = (bf16[80,512]{1,0:T(8,128)(2,1)S(1)}, bf16[80,512]{1,0:T(8,128)(2,1)S(1)}, u32[]{:S(2)}, u32[]{:S(2)}) collective-permute-start(bf16[80,512]{1,0:T(8,128)(2,1)S(1)} %collective-permute-done), channel_id=1, source_target_pairs={{0,256},{1,257},{256,0},{257,1},{2,258},{3,259},{258,2},{259,3},{4... | collective-permute-start | bytes 245768 | tf_op jit(solution)/shard_map/ppermute | solution.py:210
  26.9 8.2 %collective-permute-start.5 = (bf16[80,512]{1,0:T(8,128)(2,1)S(1)}, bf16[80,512]{1,0:T(8,128)(2,1)S(1)}, u32[]{:S(2)}, u32[]{:S(2)}) collective-permute-start(bf16[80,512]{1,0:T(8,128)(2,1)S(1)} %collective-permute-done), channel_id=1, source_target_pairs={{0,257},{1,256},{256,1},{257,0},{2,259},{3,258},{258,3},{259,2},{4... | collective-permute-start | bytes 245768 | tf_op jit(solution)/shard_map/ppermute | solution.py:210
  36.0 148.3 %reduce-scatter.2.cloned.1.call-start = ((), (), s32[]{:S(2)}) async-start(), calls=%async_computation.2 | async-start | bytes 4718592 | tf_op jit(solution)/shard_map/reduce_scatter | solution.py:305
  36.3 41.9 %collective-permute-start.12 = (bf16[2048,512]{1,0:T(8,128)(2,1)S(1)}, bf16[2048,512]{1,0:T(8,128)(2,1)}, u32[]{:S(2)}, u32[]{:S(2)}) collective-permute-start(bf16[2048,512]{1,0:T(8,128)(2,1)S(1)} %copy-done.2), channel_id=1, source_target_pairs={{0,0},{1,16},{16,1},{17,17},{2,2},{3,18},{18,3},{19,19},{4,4},{5,2... | collective-permute-start | bytes 6291464 | tf_op jit(solution)/shard_map/ppermute | solution.py:262
  41.1 16.8 %collective-permute-start.8 = (bf16[272,512]{1,0:T(8,128)(2,1)S(1)}, bf16[272,512]{1,0:T(8,128)(2,1)S(1)}, u32[]{:S(2)}, u32[]{:S(2)}) collective-permute-start(bf16[272,512]{1,0:T(8,128)(2,1)S(1)} %concatenate.7.rest_0_), channel_id=1, source_target_pairs={{0,32},{32,64},{64,96},{96,128},{128,160},{160,192},{192,224},{224... | collective-permute-start | bytes 835592 | tf_op jit(solution)/shard_map/ppermute | solution.py:30
  45.0 14.9 %collective-permute-start.6 = (bf16[272,512]{1,0:T(8,128)(2,1)S(1)}, bf16[272,512]{1,0:T(8,128)(2,1)S(1)}, u32[]{:S(2)}, u32[]{:S(2)}) collective-permute-start(bf16[272,512]{1,0:T(8,128)(2,1)S(1)} %concatenate.7.rest_0_), channel_id=1, source_target_pairs={{0,224},{32,0},{64,32},{96,64},{128,96},{160,128},{192,160},{224,1... | collective-permute-start | bytes 835592 | tf_op jit(solution)/shard_map/ppermute | solution.py:30
  57.9 10.0 %collective-permute-start.9 = (bf16[272,512]{1,0:T(8,128)(2,1)S(1)}, bf16[272,512]{1,0:T(8,128)(2,1)}, u32[]{:S(2)}, u32[]{:S(2)}) collective-permute-start(bf16[272,512]{1,0:T(8,128)(2,1)S(1)} %collective-permute-done.8.rest_4_), channel_id=1, source_target_pairs={{0,32},{32,64},{64,96},{96,128},{128,160},{160,192},{192,224},{224... | collective-permute-start | bytes 835592 | tf_op jit(solution)/shard_map/ppermute | solution.py:30
  59.9 10.0 %collective-permute-start.7 = (bf16[272,512]{1,0:T(8,128)(2,1)S(1)}, bf16[272,512]{1,0:T(8,128)(2,1)}, u32[]{:S(2)}, u32[]{:S(2)}) collective-permute-start(bf16[272,512]{1,0:T(8,128)(2,1)S(1)} %collective-permute-done.6.rest_1_), channel_id=1, source_target_pairs={{0,224},{32,0},{64,32},{96,64},{128,96},{160,128},{192,160},{224,1... | collective-permute-start | bytes 835592 | tf_op jit(solution)/shard_map/ppermute | solution.py:30
  68.0 9.3 %collective-permute-start.10 = (bf16[272,512]{1,0:T(8,128)(2,1)}, bf16[272,512]{1,0:T(8,128)(2,1)S(1)}, u32[]{:S(2)}, u32[]{:S(2)}) collective-permute-start(bf16[272,512]{1,0:T(8,128)(2,1)} %collective-permute-done.9.rest_5_), channel_id=1, source_target_pairs={{0,32},{32,64},{64,96},{96,128},{128,160},{160,192},{192,224},{224... | collective-permute-start | bytes 835592 | tf_op jit(solution)/shard_map/ppermute | solution.py:30
  69.9 8.4 %collective-permute-start.11 = (bf16[272,512]{1,0:T(8,128)(2,1)}, bf16[272,512]{1,0:T(8,128)(2,1)S(1)}, u32[]{:S(2)}, u32[]{:S(2)}) collective-permute-start(bf16[272,512]{1,0:T(8,128)(2,1)} %collective-permute-done.7.rest_2_), channel_id=1, source_target_pairs={{0,224},{32,0},{64,32},{96,64},{128,96},{160,128},{192,160},{224,1... | collective-permute-start | bytes 835592 | tf_op jit(solution)/shard_map/ppermute | solution.py:30
  78.3 10.0 %collective-permute-start.13 = (bf16[128,512]{1,0:T(8,128)(2,1)S(1)}, bf16[128,512]{1,0:T(8,128)(2,1)S(1)}, u32[]{:S(2)}, u32[]{:S(2)}) collective-permute-start(bf16[128,512]{1,0:T(8,128)(2,1)S(1)} %slice.56), channel_id=1, source_target_pairs={{0,32},{32,64},{64,96},{96,128},{128,160},{160,192},{192,224},{224... | collective-permute-start | bytes 393224 | tf_op jit(solution)/shard_map/ppermute | solution.py:30
  80.2 8.1 %collective-permute-start.14 = (bf16[144,512]{1,0:T(8,128)(2,1)S(1)}, bf16[144,512]{1,0:T(8,128)(2,1)S(1)}, u32[]{:S(2)}, u32[]{:S(2)}) collective-permute-start(bf16[144,512]{1,0:T(8,128)(2,1)S(1)} %slice.57), channel_id=1, source_target_pairs={{0,224},{32,0},{64,32},{96,64},{128,96},{160,128},{192,160},{224,1... | collective-permute-start | bytes 442376 | tf_op jit(solution)/shard_map/ppermute | solution.py:30
  101.5 12.2 %collective-permute-start.15 = (bf16[1024,2176]{1,0:T(8,128)(2,1)}, bf16[1024,2176]{1,0:T(8,128)(2,1)S(1)}, u32[]{:S(2)}, u32[]{:S(2)}) collective-permute-start(bf16[1024,2176]{1,0:T(8,128)(2,1)} %all-gather.2.cloned.1.call-done), channel_id=1, source_target_pairs={{0,16},{16,0},{1,17},{17,1},{2,18},{18,2},{3,19},{19,3},{4,20},{20... | collective-permute-start | bytes 13369352 | tf_op jit(solution)/shard_map/ppermute | solution.py:26
  139.2 8.9 %collective-permute-start.19 = (f32[24,128]{1,0:T(8,128)S(1)}, f32[24,128]{1,0:T(8,128)S(1)}, u32[]{:S(2)}, u32[]{:S(2)}) collective-permute-start(f32[24,128]{1,0:T(8,128)S(1)} %add.61), channel_id=1, source_target_pairs={{0,128},{32,160},{64,192},{96,224},{128,0},{160,32},{192,64},{224,... | collective-permute-start | bytes 36872 | tf_op jit(solution)/shard_map/ppermute | solution.py:26
  153.0 5.7 %collective-permute-start.21 = (f32[24,128]{1,0:T(8,128)S(1)}, f32[24,128]{1,0:T(8,128)S(1)}, u32[]{:S(2)}, u32[]{:S(2)}) collective-permute-start(f32[24,128]{1,0:T(8,128)S(1)} %add.63), channel_id=1, source_target_pairs={{0,4},{2,6},{4,0},{6,2},{8,12},{10,14},{12,8},{14,10},{1,5},{3,7},... | collective-permute-start | bytes 36872 | tf_op jit(solution)/shard_map/ppermute | solution.py:26
  158.7 8.3 %collective-permute-start.22 = (f32[24,128]{1,0:T(8,128)S(1)}, f32[24,128]{1,0:T(8,128)S(1)}, u32[]{:S(2)}, u32[]{:S(2)}) collective-permute-start(f32[24,128]{1,0:T(8,128)S(1)} %add.64), channel_id=1, source_target_pairs={{0,8},{2,10},{4,12},{6,14},{8,0},{10,2},{12,4},{14,6},{1,9},{3,11}... | collective-permute-start | bytes 36872 | tf_op jit(solution)/shard_map/ppermute | solution.py:26
  171.9 5.9 %collective-permute-start.24 = (f32[24,128]{1,0:T(8,128)S(1)}, f32[24,128]{1,0:T(8,128)S(1)}, u32[]{:S(2)}, u32[]{:S(2)}) collective-permute-start(f32[24,128]{1,0:T(8,128)S(1)} %add.66), channel_id=1, source_target_pairs={{0,1},{1,0},{2,3},{3,2},{4,5},{5,4},{6,7},{7,6},{8,9},{9,8},{10,11... | collective-permute-start | bytes 36872 | tf_op jit(solution)/shard_map/ppermute | solution.py:26
  185.4 14.3 %collective-permute-start.28 = (f32[64,512]{1,0:T(8,128)S(1)}, f32[64,512]{1,0:T(8,128)S(1)}, u32[]{:S(2)}, u32[]{:S(2)}) collective-permute-start(f32[64,512]{1,0:T(8,128)S(1)} %get-tuple-element.60), channel_id=1, source_target_pairs={{0,272},{1,256},{16,273},{17,257},{256,16},{257,0},{272,17},{273,1... | collective-permute-start | bytes 393224 | tf_op jit(solution)/shard_map/ppermute | solution.py:323
  189.8 10.0 %collective-permute-start.27 = (f32[64,512]{1,0:T(8,128)S(1)}, f32[64,512]{1,0:T(8,128)S(1)}, u32[]{:S(2)}, u32[]{:S(2)}) collective-permute-start(f32[64,512]{1,0:T(8,128)S(1)} %get-tuple-element.61), channel_id=1, source_target_pairs={{0,256},{1,272},{16,257},{17,273},{256,0},{257,16},{272,1},{273,17... | collective-permute-start | bytes 393224 | tf_op jit(solution)/shard_map/ppermute | solution.py:323
  195.0 7.8 %collective-permute-start.25 = (f32[64,512]{1,0:T(8,128)S(1)}, f32[64,512]{1,0:T(8,128)S(1)}, u32[]{:S(2)}, u32[]{:S(2)}) collective-permute-start(f32[64,512]{1,0:T(8,128)S(1)} %get-tuple-element.62), channel_id=1, source_target_pairs={{0,0},{1,16},{16,1},{17,17},{256,256},{257,272},{272,257},{273,273... | collective-permute-start | bytes 393224 | tf_op jit(solution)/shard_map/ppermute | solution.py:323
  (17 other events, 171.9 us)
Sparse Core Ops, SparseCore 0:
  36.1 65.3 all-gather.1
  126.4 57.8 reduce-scatter.1

commit v4 on v3

--- a/solution.py
+++ b/solution.py
@@ -50,7 +50,7 @@
         out_specs=out_specs,
         out_shape=[jax.ShapeDtypeStruct(shape, dtype) for shape, dtype in outs],
         scratch_shapes=scratch,
-        compiler_params=pltpu.CompilerParams(vmem_limit_bytes=20 * 2**20),
+        compiler_params=pltpu.CompilerParams(vmem_limit_bytes=16 * 2**20),
         cost_estimate=pl.CostEstimate(flops=flops, bytes_accessed=6 * 2**20, transcendentals=0),
         name=name,
     )(*args)
@@ -171,12 +171,11 @@
 
 
 def far_kernel(ints, rows_hbm, proj_ref, count_ref, teacher_ref, gain_ref, *rest):
-    scale_ref, grad_in, loss_in, grad_hbm, sums_ref, rows_ref, total, sems = rest
+    scale_ref, grad_in, loss_in, grad_ref, sums_ref, rows_ref, sems = rest
     copies = load_rows(rows_hbm, rows_ref, sems)
     scale = columns(scale_ref[...])
     factor = 2.0 / count_ref[0:1, 0:1]
     sums_ref[16:24, :] = loss_in[...]
-    out = []
     for i in range(2):
         copies[i].wait()
         rows = rows_ref[i * 4 : i * 4 + 4, :, :2048].reshape(512, 2048)
@@ -185,17 +184,11 @@
         for x in range(2):
             lanes = slice(x * 512, (x + 1) * 512)
             part = grad_part(rows, slope, x)
-            total[x] = (grad_in[:, lanes] if i == 0 else total[x]) + part
-            if i == 1:
-                copy = pltpu.make_async_copy(total.at[x], grad_hbm.at[:, pl.ds(x * 512, 512)], sems.at[2 + x])
-                copy.start()
-                out.append(copy)
+            grad_ref[:, lanes] = (grad_in[:, lanes] if i == 0 else grad_ref[:, lanes]) + part
     for x in range(2):
-        g = total[x] * proj_ref[x * 1024 : (x + 1) * 1024, :].astype(F32)
+        g = grad_ref[:, x * 512 : (x + 1) * 512] * proj_ref[x * 1024 : (x + 1) * 1024, :].astype(F32)
         g = g[:, :128] + g[:, 128:256] + g[:, 256:384] + g[:, 384:]
         sums_ref[x * 8 : (x + 1) * 8, :] = jnp.sum(g.reshape(8, 128, 128), axis=2)
-    for copy in out:
-        copy.wait()
 
 
 def own_rows(projection, teacher_gain, lengths):
@@ -241,7 +234,7 @@
     scaled = lax.ppermute(scaled, ("c", "xh"), SWAP)
     cross = lax.ppermute(squares, ("c", "xh"), CROSS)
     flips = projection_flips(own)
-    scaled, cross, *flips = tie(scaled, cross, *flips)
+    scaled, cross, flips[0] = tie(scaled, cross, flips[0])
     (joined,) = call(
         join_kernel,
         "join",
@@ -255,7 +248,6 @@
     )
     near = lax.all_gather(joined, "y", axis=0, tiled=True)
 
-    flips, _ = tie(flips, joined)
     block = projection_block(own, *flips)
     up1, down1 = shift(block, "z", 8, 1), shift(block, "z", 8, -1)
     teacher, _ = tie(teacher_hidden, block)
@@ -296,9 +288,9 @@
         far_kernel,
         "far_rows",
         [SMEM, HBM] + [VMEM] * 7,
-        [HBM, VMEM],
+        [VMEM] * 2,
         [((1024, 1024), F32), ((24, 128), F32)],
-        [pltpu.VMEM((8, 128, WIDE), BF16), pltpu.VMEM((2, 1024, 512), F32), pltpu.SemaphoreType.DMA((4,))],
+        [pltpu.VMEM((8, 128, WIDE), BF16), pltpu.SemaphoreType.DMA((2,))],
         4 * 1024 * 2048 * 512,
         *(ints, far.reshape(8, 128, WIDE), proj_full, count, teacher, gain, scale, grad, loss_part),
     )
@@ -316,6 +308,7 @@
         ("xh", 2, 1),
     ):
         sums = sums + flip(sums, axis, size, bit)
+    mine, sums = tie(mine, sums)
     grad_proj = jnp.zeros((64, 512), F32)
     for fx in (0, 1):
         for fc in (0, 1):

time: 214 us -> 211 us (0.986)
  waiting for transfers between devices: 47.1 us -> 42.7 us
    all_gather x1, waiting for transfers between devices: 11.9 us -> 0.02 us  [on_device(): near = lax.all_gather(joined, 'y', axis=0, tiled=True)]
    ppermute x3, waiting for transfers between devices: 0.06 us -> 2.81 us  [projection_flips(): lax.ppermute(own, ('xl', 'xh'), [(i, i ^ fx * 2 + fc) for i in range(4)])]
    ppermute x1, starting transfers between devices: 2.55 us -> 4.87 us  [on_device(): cross = lax.ppermute(squares, ('c', 'xh'), CROSS)]
    ppermute x8, waiting for transfers between devices: 11 us -> 13.2 us  [shift(): return lax.ppermute(x, axis, [(i, (i + by) % size) for i in range(size)])]
  transfers between devices with their start and end apart: 31 -> 31, of which waited for: 18 -> 18; matrix products, arithmetic and copies ran while one was open for 2% -> 2% of each run, Pallas kernels for 4% -> 5%
where the time goes in v4:
time: 211 us; the launch traced here: 208 us
  starting transfers between devices  112 us (53%)
  waiting for transfers between devices  42.7 us (20%)
  between operations  19 us (9%)
  Pallas kernels  17.8 us (8%)
  local copies, waits for them, and re-layouts  12.9 us (6%)
  other arithmetic  3.6 us (2%)
    ppermute x10, starting transfers between devices, flip(): return lax.ppermute(x, axis, [(i, i ^ bit) for i in range(size)])  38.9 us
    ppermute x8, starting transfers between devices, shift(): return lax.ppermute(x, axis, [(i, (i + by) % size) for i in range(size)])  32.8 us
    pallas_call x5, Pallas kernels, call(): pl.pallas_call(kernel, in_specs=in_specs, out_specs=out_specs, out_shape=...  17.8 us
    ppermute x10, waiting for transfers between devices, flip(): return lax.ppermute(x, axis, [(i, i ^ bit) for i in range(size)])  16.4 us
    ppermute x4, starting transfers between devices, on_device(): grad_proj += lax.ppermute(send, ('xl', 'c', 'xh'), corner(fx, fc))  13.9 us
    ppermute x8, waiting for transfers between devices, shift(): return lax.ppermute(x, axis, [(i, (i + by) % size) for i in range(size)])  13.2 us
    unnamed x20, local copies, waits for them, and re-layouts  9.13 us
    ppermute x3, starting transfers between devices, projection_flips(): lax.ppermute(own, ('xl', 'xh'), [(i, i ^ fx * 2 + fc) for i in range(4)])  7.71 us
  transfers between devices with their start and end apart: 31, of which 18 were waited for; matrix products, arithmetic and copies ran while one was open for 2% of the time, Pallas kernels for 5%

profile of v4, /device:TPU:1, one launch (start us, length us, event | category | flops | bytes accessed | tf_op | source)
XLA Modules:
  0.0 208.3 jit_solution(12635207342707414402)
XLA Ops:
  9.4 6.0 %collective-permute-start = (bf16[80,512]{1,0:T(8,128)(2,1)S(1)}, bf16[80,512]{1,0:T(8,128)(2,1)S(1)}, u32[]{:S(2)}, u32[]{:S(2)}) collective-permute-start(bf16[80,512]{1,0:T(8,128)(2,1)S(1)} %pad_maximum_fusion), channel_id=1, source_target_pairs={{0,0},{1,16},{16,1},{17,17},{2,2},{3,18},{18,3},{19,19},{4,4},{5,2... | collective-permute-start | bytes 245768 | tf_op jit(solution)/shard_map/ppermute | solution.py:220
  19.5 3.2 %collective-permute-start.1 = (bf16[128,2176]{1,0:T(8,128)(2,1)S(1)}, bf16[128,2176]{1,0:T(8,128)(2,1)S(1)}, u32[]{:S(2)}, u32[]{:S(2)}) collective-permute-start(bf16[128,2176]{1,0:T(8,128)(2,1)S(1)} %get-tuple-element.30), channel_id=1, source_target_pairs={{0,0},{1,16},{16,1},{17,17},{2,2},{3,18},{18,3},{19,19},{4,4},{5,2... | collective-permute-start | bytes 1671176 | tf_op jit(solution)/shard_map/ppermute | solution.py:234
  24.7 4.9 %collective-permute-start.2 = (f32[16,128]{1,0:T(8,128)S(1)}, f32[16,128]{1,0:T(8,128)S(1)}, u32[]{:S(2)}, u32[]{:S(2)}) collective-permute-start(f32[16,128]{1,0:T(8,128)S(1)} %get-tuple-element.31), channel_id=1, source_target_pairs={{0,16},{1,0},{16,17},{17,1},{2,18},{3,2},{18,19},{19,3},{4,20},{5,... | collective-permute-start | bytes 24584 | tf_op jit(solution)/shard_map/ppermute | solution.py:235
  35.9 3.6 %collective-permute-start.5 = (bf16[80,512]{1,0:T(8,128)(2,1)S(1)}, bf16[80,512]{1,0:T(8,128)(2,1)S(1)}, u32[]{:S(2)}, u32[]{:S(2)}) collective-permute-start(bf16[80,512]{1,0:T(8,128)(2,1)S(1)} %collective-permute-done), channel_id=1, source_target_pairs={{0,257},{1,256},{256,1},{257,0},{2,259},{3,258},{258,3},{259,2},{4... | collective-permute-start | bytes 245768 | tf_op jit(solution)/shard_map/ppermute | solution.py:203
  42.6 4.9 %collective-permute-start.12 = (bf16[2048,512]{1,0:T(8,128)(2,1)S(1)}, bf16[2048,512]{1,0:T(8,128)(2,1)}, u32[]{:S(2)}, u32[]{:S(2)}) collective-permute-start(bf16[2048,512]{1,0:T(8,128)(2,1)S(1)} %copy-done.2), channel_id=1, source_target_pairs={{0,0},{1,16},{16,1},{17,17},{2,2},{3,18},{18,3},{19,19},{4,4},{5,2... | collective-permute-start | bytes 6291464 | tf_op jit(solution)/shard_map/ppermute | solution.py:254
  47.4 4.0 %collective-permute-start.8 = (bf16[272,512]{1,0:T(8,128)(2,1)S(1)}, bf16[272,512]{1,0:T(8,128)(2,1)S(1)}, u32[]{:S(2)}, u32[]{:S(2)}) collective-permute-start(bf16[272,512]{1,0:T(8,128)(2,1)S(1)} %concatenate.7.rest_0_), channel_id=1, source_target_pairs={{0,32},{32,64},{64,96},{96,128},{128,160},{160,192},{192,224},{224... | collective-permute-start | bytes 835592 | tf_op jit(solution)/shard_map/ppermute | solution.py:30
  51.5 8.6 %collective-permute-start.6 = (bf16[272,512]{1,0:T(8,128)(2,1)S(1)}, bf16[272,512]{1,0:T(8,128)(2,1)S(1)}, u32[]{:S(2)}, u32[]{:S(2)}) collective-permute-start(bf16[272,512]{1,0:T(8,128)(2,1)S(1)} %concatenate.7.rest_0_), channel_id=1, source_target_pairs={{0,224},{32,0},{64,32},{96,64},{128,96},{160,128},{192,160},{224,1... | collective-permute-start | bytes 835592 | tf_op jit(solution)/shard_map/ppermute | solution.py:30
  60.0 5.1 %collective-permute-done.8.rest_4_ = bf16[272,512]{1,0:T(8,128)(2,1)S(1)} collective-permute-done((bf16[272,512]{1,0:T(8,128)(2,1)S(1)}, bf16[272,512]{1,0:T(8,128)(2,1)S(1)}, u32[]{:S(2)}, u32[]{:S(2)}) %collective-permute-start.8) | collective-permute-done | bytes 278560 | tf_op jit(solution)/shard_map/ppermute | solution.py:30
  67.0 4.6 %collective-permute-start.7 = (bf16[272,512]{1,0:T(8,128)(2,1)S(1)}, bf16[272,512]{1,0:T(8,128)(2,1)}, u32[]{:S(2)}, u32[]{:S(2)}) collective-permute-start(bf16[272,512]{1,0:T(8,128)(2,1)S(1)} %collective-permute-done.6.rest_1_), channel_id=1, source_target_pairs={{0,224},{32,0},{64,32},{96,64},{128,96},{160,128},{192,160},{224,1... | collective-permute-start | bytes 835592 | tf_op jit(solution)/shard_map/ppermute | solution.py:30
  71.6 4.3 %collective-permute-done.9.rest_5_ = bf16[272,512]{1,0:T(8,128)(2,1)} collective-permute-done((bf16[272,512]{1,0:T(8,128)(2,1)S(1)}, bf16[272,512]{1,0:T(8,128)(2,1)}, u32[]{:S(2)}, u32[]{:S(2)}) %collective-permute-start.9) | collective-permute-done | bytes 278560 | tf_op jit(solution)/shard_map/ppermute | solution.py:30
  77.9 4.6 %collective-permute-start.11 = (bf16[272,512]{1,0:T(8,128)(2,1)}, bf16[272,512]{1,0:T(8,128)(2,1)S(1)}, u32[]{:S(2)}, u32[]{:S(2)}) collective-permute-start(bf16[272,512]{1,0:T(8,128)(2,1)} %collective-permute-done.7.rest_2_), channel_id=1, source_target_pairs={{0,224},{32,0},{64,32},{96,64},{128,96},{160,128},{192,160},{224,1... | collective-permute-start | bytes 835592 | tf_op jit(solution)/shard_map/ppermute | solution.py:30
  88.9 5.3 %collective-permute-start.14 = (bf16[144,512]{1,0:T(8,128)(2,1)S(1)}, bf16[144,512]{1,0:T(8,128)(2,1)S(1)}, u32[]{:S(2)}, u32[]{:S(2)}) collective-permute-start(bf16[144,512]{1,0:T(8,128)(2,1)S(1)} %slice.57), channel_id=1, source_target_pairs={{0,224},{32,0},{64,32},{96,64},{128,96},{160,128},{192,160},{224,1... | collective-permute-start | bytes 442376 | tf_op jit(solution)/shard_map/ppermute | solution.py:30
  98.3 4.7 %collective-permute-start.15 = (bf16[1024,2176]{1,0:T(8,128)(2,1)}, bf16[1024,2176]{1,0:T(8,128)(2,1)S(1)}, u32[]{:S(2)}, u32[]{:S(2)}) collective-permute-start(bf16[1024,2176]{1,0:T(8,128)(2,1)} %all-gather.2.cloned.1.call-done), channel_id=1, source_target_pairs={{0,16},{16,0},{1,17},{17,1},{2,18},{18,2},{3,19},{19,3},{4,20},{20... | collective-permute-start | bytes 13369352 | tf_op jit(solution)/shard_map/ppermute | solution.py:26
  105.3 7.4 %near_rows.1 = (f32[1024,1024]{1,0:T(8,128)S(1)}, f32[8,128]{1,0:T(8,128)S(1)}, f32[16,128]{1,0:T(8,128)S(1)}) custom-call(s32[2]{0:T(128)S(1)} %pad_add_fusion.ints, bf16[8,128,2176]{2,1,0:T(8,128)(2,1)S(1)} %bitcast.13, bf16[2048,512]{1,0:T(8,128)(2,1)S(1)} %get-tuple-element.42.proj_ref, f32[8,128]{1,0:T(8,128)S(1)} %get-tuple-element.43.count_ref, ...), custom_call_target="tpu_custom_call" | custom-call | flops 4294967296 | bytes 6291456 | tf_op jit(solution)/shard_map/near_rows/pallas_call | solution.py:47
  114.3 7.5 %far_rows.1 = (f32[1024,1024]{1,0:T(8,128)S(1)}, f32[24,128]{1,0:T(8,128)S(1)}) custom-call(s32[2]{0:T(128)S(1)} %pad_add_fusion.ints, bf16[8,128,2176]{2,1,0:T(8,128)(2,1)S(1)} %bitcast.14, bf16[2048,512]{1,0:T(8,128)(2,1)S(1)} %copy-done.8, f32[8,128]{1,0:T(8,128)S(1)} %get-tuple-element.43.count_ref, bf16[8,2,128,512]{3,2,1,0:T(8,128)(2,1)} %bitcast.7.teacher_ref, ...), custom_call_target="tpu_custom_call" | custom-call | flops 4294967296 | bytes 6291456 | tf_op jit(solution)/shard_map/far_rows/pallas_call | solution.py:47
  131.4 4.1 %collective-permute-start.18 = (f32[24,128]{1,0:T(8,128)S(1)}, f32[24,128]{1,0:T(8,128)S(1)}, u32[]{:S(2)}, u32[]{:S(2)}) collective-permute-start(f32[24,128]{1,0:T(8,128)S(1)} %add.60), channel_id=1, source_target_pairs={{0,64},{32,96},{64,0},{96,32},{128,192},{160,224},{192,128},{224,1... | collective-permute-start | bytes 36872 | tf_op jit(solution)/shard_map/ppermute | solution.py:26
  136.7 5.2 %collective-permute-start.19 = (f32[24,128]{1,0:T(8,128)S(1)}, f32[24,128]{1,0:T(8,128)S(1)}, u32[]{:S(2)}, u32[]{:S(2)}) collective-permute-start(f32[24,128]{1,0:T(8,128)S(1)} %add.61), channel_id=1, source_target_pairs={{0,128},{32,160},{64,192},{96,224},{128,0},{160,32},{192,64},{224,... | collective-permute-start | bytes 36872 | tf_op jit(solution)/shard_map/ppermute | solution.py:26
  141.9 3.4 %collective-permute-done.19 = f32[24,128]{1,0:T(8,128)S(1)} collective-permute-done((f32[24,128]{1,0:T(8,128)S(1)}, f32[24,128]{1,0:T(8,128)S(1)}, u32[]{:S(2)}, u32[]{:S(2)}) %collective-permute-start.19) | collective-permute-done | bytes 12320 | tf_op jit(solution)/shard_map/ppermute | solution.py:26
  150.1 4.0 %collective-permute-start.21 = (f32[24,128]{1,0:T(8,128)S(1)}, f32[24,128]{1,0:T(8,128)S(1)}, u32[]{:S(2)}, u32[]{:S(2)}) collective-permute-start(f32[24,128]{1,0:T(8,128)S(1)} %add.63), channel_id=1, source_target_pairs={{0,4},{2,6},{4,0},{6,2},{8,12},{10,14},{12,8},{14,10},{1,5},{3,7},... | collective-permute-start | bytes 36872 | tf_op jit(solution)/shard_map/ppermute | solution.py:26
  155.8 7.5 %collective-permute-start.22 = (f32[24,128]{1,0:T(8,128)S(1)}, f32[24,128]{1,0:T(8,128)S(1)}, u32[]{:S(2)}, u32[]{:S(2)}) collective-permute-start(f32[24,128]{1,0:T(8,128)S(1)} %add.64), channel_id=1, source_target_pairs={{0,8},{2,10},{4,12},{6,14},{8,0},{10,2},{12,4},{14,6},{1,9},{3,11}... | collective-permute-start | bytes 36872 | tf_op jit(solution)/shard_map/ppermute | solution.py:26
  164.4 3.9 %collective-permute-start.23 = (f32[24,128]{1,0:T(8,128)S(1)}, f32[24,128]{1,0:T(8,128)S(1)}, u32[]{:S(2)}, u32[]{:S(2)}) collective-permute-start(f32[24,128]{1,0:T(8,128)S(1)} %add.65), channel_id=1, source_target_pairs={{0,256},{256,0},{1,257},{257,1},{2,258},{258,2},{3,259},{259,3},{4... | collective-permute-start | bytes 36872 | tf_op jit(solution)/shard_map/ppermute | solution.py:26
  175.7 5.2 %reduce-scatter.2.cloned.1.call-done = f32[128,1024]{1,0:T(8,128)} async-done(((f32[1024,1024]{1,0:T(8,128)}), f32[128,1024]{1,0:T(8,128)}) %reduce-scatter.2.cloned.1.call-update) | async-done | bytes 524304 | tf_op jit(solution)/shard_map/reduce_scatter | solution.py:297
  182.6 4.3 %collective-permute-start.28 = (f32[64,512]{1,0:T(8,128)S(1)}, f32[64,512]{1,0:T(8,128)S(1)}, u32[]{:S(2)}, u32[]{:S(2)}) collective-permute-start(f32[64,512]{1,0:T(8,128)S(1)} %get-tuple-element.54), channel_id=1, source_target_pairs={{0,272},{1,256},{16,273},{17,257},{256,16},{257,0},{272,17},{273,1... | collective-permute-start | bytes 393224 | tf_op jit(solution)/shard_map/ppermute | solution.py:316
  186.9 4.9 %collective-permute-start.27 = (f32[64,512]{1,0:T(8,128)S(1)}, f32[64,512]{1,0:T(8,128)S(1)}, u32[]{:S(2)}, u32[]{:S(2)}) collective-permute-start(f32[64,512]{1,0:T(8,128)S(1)} %get-tuple-element.55), channel_id=1, source_target_pairs={{0,256},{1,272},{16,257},{17,273},{256,0},{257,16},{272,1},{273,17... | collective-permute-start | bytes 393224 | tf_op jit(solution)/shard_map/ppermute | solution.py:316
  (99 shorter events, 68.2 us)
Async XLA Ops:
  7.2 91.2 %all-gather.2.cloned.1.call-start = ((), (), s32[]{:S(2)}) async-start(), calls=%async_computation.1 | async-start | bytes 5013504 | tf_op jit(solution)/shard_map/all_gather | solution.py:249
  9.4 10.1 %collective-permute-start = (bf16[80,512]{1,0:T(8,128)(2,1)S(1)}, bf16[80,512]{1,0:T(8,128)(2,1)S(1)}, u32[]{:S(2)}, u32[]{:S(2)}) collective-permute-start(bf16[80,512]{1,0:T(8,128)(2,1)S(1)} %pad_maximum_fusion), channel_id=1, source_target_pairs={{0,0},{1,16},{16,1},{17,17},{2,2},{3,18},{18,3},{19,19},{4,4},{5,2... | collective-permute-start | bytes 245768 | tf_op jit(solution)/shard_map/ppermute | solution.py:220
  19.5 13.2 %collective-permute-start.1 = (bf16[128,2176]{1,0:T(8,128)(2,1)S(1)}, bf16[128,2176]{1,0:T(8,128)(2,1)S(1)}, u32[]{:S(2)}, u32[]{:S(2)}) collective-permute-start(bf16[128,2176]{1,0:T(8,128)(2,1)S(1)} %get-tuple-element.30), channel_id=1, source_target_pairs={{0,0},{1,16},{16,1},{17,17},{2,2},{3,18},{18,3},{19,19},{4,4},{5,2... | collective-permute-start | bytes 1671176 | tf_op jit(solution)/shard_map/ppermute | solution.py:234
  22.7 8.3 %collective-permute-start.3 = (bf16[80,512]{1,0:T(8,128)(2,1)S(1)}, bf16[80,512]{1,0:T(8,128)(2,1)S(1)}, u32[]{:S(2)}, u32[]{:S(2)}) collective-permute-start(bf16[80,512]{1,0:T(8,128)(2,1)S(1)} %collective-permute-done), channel_id=1, source_target_pairs={{0,1},{1,0},{256,257},{257,256},{2,3},{3,2},{258,259},{259,258},{4... | collective-permute-start | bytes 245768 | tf_op jit(solution)/shard_map/ppermute | solution.py:203
  24.7 6.4 %collective-permute-start.2 = (f32[16,128]{1,0:T(8,128)S(1)}, f32[16,128]{1,0:T(8,128)S(1)}, u32[]{:S(2)}, u32[]{:S(2)}) collective-permute-start(f32[16,128]{1,0:T(8,128)S(1)} %get-tuple-element.31), channel_id=1, source_target_pairs={{0,16},{1,0},{16,17},{17,1},{2,18},{3,2},{18,19},{19,3},{4,20},{5,... | collective-permute-start | bytes 24584 | tf_op jit(solution)/shard_map/ppermute | solution.py:235
  33.7 147.2 %reduce-scatter.2.cloned.1.call-start = ((), (), s32[]{:S(2)}) async-start(), calls=%async_computation.2 | async-start | bytes 4718592 | tf_op jit(solution)/shard_map/reduce_scatter | solution.py:297
  33.7 5.8 %collective-permute-start.4 = (bf16[80,512]{1,0:T(8,128)(2,1)S(1)}, bf16[80,512]{1,0:T(8,128)(2,1)S(1)}, u32[]{:S(2)}, u32[]{:S(2)}) collective-permute-start(bf16[80,512]{1,0:T(8,128)(2,1)S(1)} %collective-permute-done), channel_id=1, source_target_pairs={{0,256},{1,257},{256,0},{257,1},{2,258},{3,259},{258,2},{259,3},{4... | collective-permute-start | bytes 245768 | tf_op jit(solution)/shard_map/ppermute | solution.py:203
  35.9 6.4 %collective-permute-start.5 = (bf16[80,512]{1,0:T(8,128)(2,1)S(1)}, bf16[80,512]{1,0:T(8,128)(2,1)S(1)}, u32[]{:S(2)}, u32[]{:S(2)}) collective-permute-start(bf16[80,512]{1,0:T(8,128)(2,1)S(1)} %collective-permute-done), channel_id=1, source_target_pairs={{0,257},{1,256},{256,1},{257,0},{2,259},{3,258},{258,3},{259,2},{4... | collective-permute-start | bytes 245768 | tf_op jit(solution)/shard_map/ppermute | solution.py:203
  42.6 44.4 %collective-permute-start.12 = (bf16[2048,512]{1,0:T(8,128)(2,1)S(1)}, bf16[2048,512]{1,0:T(8,128)(2,1)}, u32[]{:S(2)}, u32[]{:S(2)}) collective-permute-start(bf16[2048,512]{1,0:T(8,128)(2,1)S(1)} %copy-done.2), channel_id=1, source_target_pairs={{0,0},{1,16},{16,1},{17,17},{2,2},{3,18},{18,3},{19,19},{4,4},{5,2... | collective-permute-start | bytes 6291464 | tf_op jit(solution)/shard_map/ppermute | solution.py:254
  47.4 17.7 %collective-permute-start.8 = (bf16[272,512]{1,0:T(8,128)(2,1)S(1)}, bf16[272,512]{1,0:T(8,128)(2,1)S(1)}, u32[]{:S(2)}, u32[]{:S(2)}) collective-permute-start(bf16[272,512]{1,0:T(8,128)(2,1)S(1)} %concatenate.7.rest_0_), channel_id=1, source_target_pairs={{0,32},{32,64},{64,96},{96,128},{128,160},{160,192},{192,224},{224... | collective-permute-start | bytes 835592 | tf_op jit(solution)/shard_map/ppermute | solution.py:30
  51.5 15.6 %collective-permute-start.6 = (bf16[272,512]{1,0:T(8,128)(2,1)S(1)}, bf16[272,512]{1,0:T(8,128)(2,1)S(1)}, u32[]{:S(2)}, u32[]{:S(2)}) collective-permute-start(bf16[272,512]{1,0:T(8,128)(2,1)S(1)} %concatenate.7.rest_0_), channel_id=1, source_target_pairs={{0,224},{32,0},{64,32},{96,64},{128,96},{160,128},{192,160},{224,1... | collective-permute-start | bytes 835592 | tf_op jit(solution)/shard_map/ppermute | solution.py:30
  65.1 10.8 %collective-permute-start.9 = (bf16[272,512]{1,0:T(8,128)(2,1)S(1)}, bf16[272,512]{1,0:T(8,128)(2,1)}, u32[]{:S(2)}, u32[]{:S(2)}) collective-permute-start(bf16[272,512]{1,0:T(8,128)(2,1)S(1)} %collective-permute-done.8.rest_4_), channel_id=1, source_target_pairs={{0,32},{32,64},{64,96},{96,128},{128,160},{160,192},{192,224},{224... | collective-permute-start | bytes 835592 | tf_op jit(solution)/shard_map/ppermute | solution.py:30
  67.0 10.8 %collective-permute-start.7 = (bf16[272,512]{1,0:T(8,128)(2,1)S(1)}, bf16[272,512]{1,0:T(8,128)(2,1)}, u32[]{:S(2)}, u32[]{:S(2)}) collective-permute-start(bf16[272,512]{1,0:T(8,128)(2,1)S(1)} %collective-permute-done.6.rest_1_), channel_id=1, source_target_pairs={{0,224},{32,0},{64,32},{96,64},{128,96},{160,128},{192,160},{224,1... | collective-permute-start | bytes 835592 | tf_op jit(solution)/shard_map/ppermute | solution.py:30
  75.9 10.1 %collective-permute-start.10 = (bf16[272,512]{1,0:T(8,128)(2,1)}, bf16[272,512]{1,0:T(8,128)(2,1)S(1)}, u32[]{:S(2)}, u32[]{:S(2)}) collective-permute-start(bf16[272,512]{1,0:T(8,128)(2,1)} %collective-permute-done.9.rest_5_), channel_id=1, source_target_pairs={{0,32},{32,64},{64,96},{96,128},{128,160},{160,192},{192,224},{224... | collective-permute-start | bytes 835592 | tf_op jit(solution)/shard_map/ppermute | solution.py:30
  77.9 9.1 %collective-permute-start.11 = (bf16[272,512]{1,0:T(8,128)(2,1)}, bf16[272,512]{1,0:T(8,128)(2,1)S(1)}, u32[]{:S(2)}, u32[]{:S(2)}) collective-permute-start(bf16[272,512]{1,0:T(8,128)(2,1)} %collective-permute-done.7.rest_2_), channel_id=1, source_target_pairs={{0,224},{32,0},{64,32},{96,64},{128,96},{160,128},{192,160},{224,1... | collective-permute-start | bytes 835592 | tf_op jit(solution)/shard_map/ppermute | solution.py:30
  87.0 10.0 %collective-permute-start.13 = (bf16[128,512]{1,0:T(8,128)(2,1)S(1)}, bf16[128,512]{1,0:T(8,128)(2,1)S(1)}, u32[]{:S(2)}, u32[]{:S(2)}) collective-permute-start(bf16[128,512]{1,0:T(8,128)(2,1)S(1)} %slice.56), channel_id=1, source_target_pairs={{0,32},{32,64},{64,96},{96,128},{128,160},{160,192},{192,224},{224... | collective-permute-start | bytes 393224 | tf_op jit(solution)/shard_map/ppermute | solution.py:30
  88.9 8.1 %collective-permute-start.14 = (bf16[144,512]{1,0:T(8,128)(2,1)S(1)}, bf16[144,512]{1,0:T(8,128)(2,1)S(1)}, u32[]{:S(2)}, u32[]{:S(2)}) collective-permute-start(bf16[144,512]{1,0:T(8,128)(2,1)S(1)} %slice.57), channel_id=1, source_target_pairs={{0,224},{32,0},{64,32},{96,64},{128,96},{160,128},{192,160},{224,1... | collective-permute-start | bytes 442376 | tf_op jit(solution)/shard_map/ppermute | solution.py:30
  98.3 14.4 %collective-permute-start.15 = (bf16[1024,2176]{1,0:T(8,128)(2,1)}, bf16[1024,2176]{1,0:T(8,128)(2,1)S(1)}, u32[]{:S(2)}, u32[]{:S(2)}) collective-permute-start(bf16[1024,2176]{1,0:T(8,128)(2,1)} %all-gather.2.cloned.1.call-done), channel_id=1, source_target_pairs={{0,16},{16,0},{1,17},{17,1},{2,18},{18,2},{3,19},{19,3},{4,20},{20... | collective-permute-start | bytes 13369352 | tf_op jit(solution)/shard_map/ppermute | solution.py:26
  136.7 8.6 %collective-permute-start.19 = (f32[24,128]{1,0:T(8,128)S(1)}, f32[24,128]{1,0:T(8,128)S(1)}, u32[]{:S(2)}, u32[]{:S(2)}) collective-permute-start(f32[24,128]{1,0:T(8,128)S(1)} %add.61), channel_id=1, source_target_pairs={{0,128},{32,160},{64,192},{96,224},{128,0},{160,32},{192,64},{224,... | collective-permute-start | bytes 36872 | tf_op jit(solution)/shard_map/ppermute | solution.py:26
  155.8 8.5 %collective-permute-start.22 = (f32[24,128]{1,0:T(8,128)S(1)}, f32[24,128]{1,0:T(8,128)S(1)}, u32[]{:S(2)}, u32[]{:S(2)}) collective-permute-start(f32[24,128]{1,0:T(8,128)S(1)} %add.64), channel_id=1, source_target_pairs={{0,8},{2,10},{4,12},{6,14},{8,0},{10,2},{12,4},{14,6},{1,9},{3,11}... | collective-permute-start | bytes 36872 | tf_op jit(solution)/shard_map/ppermute | solution.py:26
  169.8 5.9 %collective-permute-start.24 = (f32[24,128]{1,0:T(8,128)S(1)}, f32[24,128]{1,0:T(8,128)S(1)}, u32[]{:S(2)}, u32[]{:S(2)}) collective-permute-start(f32[24,128]{1,0:T(8,128)S(1)} %add.66), channel_id=1, source_target_pairs={{0,1},{1,0},{2,3},{3,2},{4,5},{5,4},{6,7},{7,6},{8,9},{9,8},{10,11... | collective-permute-start | bytes 36872 | tf_op jit(solution)/shard_map/ppermute | solution.py:26
  182.6 15.2 %collective-permute-start.28 = (f32[64,512]{1,0:T(8,128)S(1)}, f32[64,512]{1,0:T(8,128)S(1)}, u32[]{:S(2)}, u32[]{:S(2)}) collective-permute-start(f32[64,512]{1,0:T(8,128)S(1)} %get-tuple-element.54), channel_id=1, source_target_pairs={{0,272},{1,256},{16,273},{17,257},{256,16},{257,0},{272,17},{273,1... | collective-permute-start | bytes 393224 | tf_op jit(solution)/shard_map/ppermute | solution.py:316
  186.9 10.9 %collective-permute-start.27 = (f32[64,512]{1,0:T(8,128)S(1)}, f32[64,512]{1,0:T(8,128)S(1)}, u32[]{:S(2)}, u32[]{:S(2)}) collective-permute-start(f32[64,512]{1,0:T(8,128)S(1)} %get-tuple-element.55), channel_id=1, source_target_pairs={{0,256},{1,272},{16,257},{17,273},{256,0},{257,16},{272,1},{273,17... | collective-permute-start | bytes 393224 | tf_op jit(solution)/shard_map/ppermute | solution.py:316
  191.9 7.8 %collective-permute-start.25 = (f32[64,512]{1,0:T(8,128)S(1)}, f32[64,512]{1,0:T(8,128)S(1)}, u32[]{:S(2)}, u32[]{:S(2)}) collective-permute-start(f32[64,512]{1,0:T(8,128)S(1)} %get-tuple-element.56), channel_id=1, source_target_pairs={{0,0},{1,16},{16,1},{17,17},{256,256},{257,272},{272,257},{273,273... | collective-permute-start | bytes 393224 | tf_op jit(solution)/shard_map/ppermute | solution.py:316
  (17 other events, 177.5 us)
Sparse Core Ops, SparseCore 0:
  33.8 62.7 all-gather.1
  124.0 56.8 reduce-scatter.1

commit v5 on v4

--- a/solution.py
+++ b/solution.py
@@ -30,12 +30,9 @@
     return lax.ppermute(x, axis, [(i, (i + by) % size) for i in range(size)])
 
 
-def corner(flip_xl, flip_c):
+def across(flip_xl):
     return [
-        (xl * 4 + c * 2 + xh, (xl ^ flip_xl) * 4 + (xh ^ flip_c) * 2 + c)
-        for xl in (0, 1)
-        for c in (0, 1)
-        for xh in (0, 1)
+        (xl * 4 + c * 2 + xh, (xl ^ flip_xl) * 4 + xh * 2 + c) for xl in (0, 1) for c in (0, 1) for xh in (0, 1)
     ]
 
 
@@ -146,10 +143,11 @@
 
 
 def near_kernel(ints, rows_hbm, proj_ref, count_ref, teacher_ref, gain_ref, *rest):
-    grad_ref, loss_ref, scale_ref, rows_ref, notes, sems = rest
+    grad_ref, loss_ref, scale_ref, proj_out, rows_ref, notes, sems = rest
     notes_copy = pltpu.make_async_copy(rows_hbm.at[:, pl.ds(0, 48), pl.ds(2048, 128)], notes, sems.at[2])
     notes_copy.start()
     copies = load_rows(rows_hbm, rows_ref, sems)
+    proj_out[...] = proj_ref[...]
     notes_copy.wait()
     squares = jnp.zeros((16, 128), F32)
     for part in (2, 1, 0):
@@ -256,8 +254,8 @@
     up3, down3 = shift(up2, "z", 8, 1), shift(down2, "z", 8, -1)
     up3, down3, teacher = tie(up3, down3, teacher)
     teacher = teacher.reshape(8, 2, 128, 512)
-    up4 = shift(up3[:128], "z", 8, 1)
-    down4 = shift(down3[128:], "z", 8, -1)
+    down4 = shift(down3[:128], "z", 8, -1)
+    up4 = shift(up3[128:], "z", 8, 1)
     proj_full, count = call(
         place_kernel,
         "place",
@@ -267,19 +265,19 @@
         [],
         10**6,
         z.reshape(1),
-        *(block, down1, down2, down3, up1, up2, up3, up4, down4),
+        *(block, down1, down2, down3, up1, up2, up3, down4, up4),
     )
     gain = own[72:73].astype(F32)
     length = (own[64, 0].astype(F32) * 16 + own[64, 1].astype(F32)).astype(jnp.int32)
     ints = jnp.stack([c, length]).astype(jnp.int32)
     near, proj_full, ints, gain = tie(near, proj_full, ints, gain)
     far = flip(near, "c", 2, 1)
-    grad, loss_part, scale = call(
+    grad, loss_part, scale, proj_full = call(
         near_kernel,
         "near_rows",
         [SMEM, HBM] + [VMEM] * 4,
-        [VMEM] * 3,
-        [((1024, 1024), F32), ((8, 128), F32), ((16, 128), F32)],
+        [VMEM] * 4,
+        [((1024, 1024), F32), ((8, 128), F32), ((16, 128), F32), ((2048, 512), BF16)],
         [pltpu.VMEM((8, 128, WIDE), BF16), pltpu.VMEM((8, 48, 128), BF16), pltpu.SemaphoreType.DMA((3,))],
         4 * 1024 * 2048 * 512,
         *(ints, near.reshape(8, 128, WIDE), proj_full, count, teacher, gain),
@@ -309,11 +307,12 @@
     ):
         sums = sums + flip(sums, axis, size, bit)
     mine, sums = tie(mine, sums)
-    grad_proj = jnp.zeros((64, 512), F32)
+    rows = jnp.zeros((128, 512), F32)
     for fx in (0, 1):
-        for fc in (0, 1):
-            send = lax.dynamic_slice(mine, ((xh ^ fc) * 64, (xl ^ fx) * 512), (64, 512))
-            grad_proj += lax.ppermute(send, ("xl", "c", "xh"), corner(fx, fc))
+        sent = lax.dynamic_slice(mine, (0, (xl ^ fx) * 512), (128, 512))
+        rows += lax.ppermute(sent, ("xl", "c", "xh"), across(fx))
+    sent = lax.dynamic_slice(rows, ((1 - c) * 64, 0), (64, 512))
+    grad_proj = lax.dynamic_slice(rows, (c * 64, 0), (64, 512)) + flip(sent, "c", 2, 1)
     loss = jnp.sum(sums[16:]) / (count[0, 0] * TW)
     grad_gain = sums[:16].reshape(2048) / student_gain
     return (loss, grad_gain, grad_proj)

time: 211 us -> 208 us (0.986)
  starting transfers between devices: 112 us -> 107 us
  waiting for transfers between devices: 42.7 us -> 47.2 us
    ppermute x4 -> x2, starting transfers between devices: 13.9 us -> 7.69 us  [on_device(): rows += lax.ppermute(sent, ('xl', 'c', 'xh'), across(fx))]
    ppermute x10 -> x11, waiting for transfers between devices: 16.4 us -> 18.8 us  [flip(): return lax.ppermute(x, axis, [(i, i ^ bit) for i in range(size)])]
    unnamed x20 -> x16, local copies, waits for them, and re-layouts: 9.13 us -> 7.56 us
    ppermute x10 -> x11, starting transfers between devices: 38.9 us -> 40.1 us  [flip(): return lax.ppermute(x, axis, [(i, i ^ bit) for i in range(size)])]
  transfers between devices with their start and end apart: 31 -> 30, of which waited for: 18 -> 20; matrix products, arithmetic and copies ran while one was open for 2% -> 2% of each run, Pallas kernels for 5% -> 5%
where the time goes in v5:
time: 208 us; the launch traced here: 206 us
  starting transfers between devices  107 us (51%)
  waiting for transfers between devices  47.2 us (23%)
  between operations  19 us (9%)
  Pallas kernels  17.8 us (9%)
  local copies, waits for them, and re-layouts  11.3 us (5%)
  other arithmetic  3.62 us (2%)
    ppermute x11, starting transfers between devices, flip(): return lax.ppermute(x, axis, [(i, i ^ bit) for i in range(size)])  40.1 us
    ppermute x8, starting transfers between devices, shift(): return lax.ppermute(x, axis, [(i, (i + by) % size) for i in range(size)])  32.8 us
    ppermute x11, waiting for transfers between devices, flip(): return lax.ppermute(x, axis, [(i, i ^ bit) for i in range(size)])  18.8 us
    pallas_call x5, Pallas kernels, call(): pl.pallas_call(kernel, in_specs=in_specs, out_specs=out_specs, out_shape=...  17.8 us
    ppermute x8, waiting for transfers between devices, shift(): return lax.ppermute(x, axis, [(i, (i + by) % size) for i in range(size)])  13.2 us
    ppermute x3, starting transfers between devices, projection_flips(): lax.ppermute(own, ('xl', 'xh'), [(i, i ^ fx * 2 + fc) for i in range(4)])  7.71 us
    ppermute x2, starting transfers between devices, on_device(): rows += lax.ppermute(sent, ('xl', 'c', 'xh'), across(fx))  7.69 us
    unnamed x16, local copies, waits for them, and re-layouts  7.56 us
  transfers between devices with their start and end apart: 30, of which 20 were waited for; matrix products, arithmetic and copies ran while one was open for 2% of the time, Pallas kernels for 5%

profile of v5, /device:TPU:1, one launch (start us, length us, event | category | flops | bytes accessed | tf_op | source)
XLA Modules:
  0.0 206.3 jit_solution(1981367317368759087)
XLA Ops:
  9.4 6.0 %collective-permute-start = (bf16[80,512]{1,0:T(8,128)(2,1)S(1)}, bf16[80,512]{1,0:T(8,128)(2,1)S(1)}, u32[]{:S(2)}, u32[]{:S(2)}) collective-permute-start(bf16[80,512]{1,0:T(8,128)(2,1)S(1)} %pad_maximum_fusion), channel_id=1, source_target_pairs={{0,0},{1,16},{16,1},{17,17},{2,2},{3,18},{18,3},{19,19},{4,4},{5,2... | collective-permute-start | bytes 245768 | tf_op jit(solution)/shard_map/ppermute | solution.py:218
  19.5 3.2 %collective-permute-start.1 = (bf16[128,2176]{1,0:T(8,128)(2,1)S(1)}, bf16[128,2176]{1,0:T(8,128)(2,1)S(1)}, u32[]{:S(2)}, u32[]{:S(2)}) collective-permute-start(bf16[128,2176]{1,0:T(8,128)(2,1)S(1)} %get-tuple-element.31), channel_id=1, source_target_pairs={{0,0},{1,16},{16,1},{17,17},{2,2},{3,18},{18,3},{19,19},{4,4},{5,2... | collective-permute-start | bytes 1671176 | tf_op jit(solution)/shard_map/ppermute | solution.py:232
  24.7 4.9 %collective-permute-start.2 = (f32[16,128]{1,0:T(8,128)S(1)}, f32[16,128]{1,0:T(8,128)S(1)}, u32[]{:S(2)}, u32[]{:S(2)}) collective-permute-start(f32[16,128]{1,0:T(8,128)S(1)} %get-tuple-element.32), channel_id=1, source_target_pairs={{0,16},{1,0},{16,17},{17,1},{2,18},{3,2},{18,19},{19,3},{4,20},{5,... | collective-permute-start | bytes 24584 | tf_op jit(solution)/shard_map/ppermute | solution.py:233
  35.9 3.6 %collective-permute-start.5 = (bf16[80,512]{1,0:T(8,128)(2,1)S(1)}, bf16[80,512]{1,0:T(8,128)(2,1)S(1)}, u32[]{:S(2)}, u32[]{:S(2)}) collective-permute-start(bf16[80,512]{1,0:T(8,128)(2,1)S(1)} %collective-permute-done), channel_id=1, source_target_pairs={{0,257},{1,256},{256,1},{257,0},{2,259},{3,258},{258,3},{259,2},{4... | collective-permute-start | bytes 245768 | tf_op jit(solution)/shard_map/ppermute | solution.py:201
  42.5 4.9 %collective-permute-start.12 = (bf16[2048,512]{1,0:T(8,128)(2,1)S(1)}, bf16[2048,512]{1,0:T(8,128)(2,1)}, u32[]{:S(2)}, u32[]{:S(2)}) collective-permute-start(bf16[2048,512]{1,0:T(8,128)(2,1)S(1)} %copy-done.2), channel_id=1, source_target_pairs={{0,0},{1,16},{16,1},{17,17},{2,2},{3,18},{18,3},{19,19},{4,4},{5,2... | collective-permute-start | bytes 6291464 | tf_op jit(solution)/shard_map/ppermute | solution.py:252
  47.4 4.0 %collective-permute-start.8 = (bf16[272,512]{1,0:T(8,128)(2,1)S(1)}, bf16[272,512]{1,0:T(8,128)(2,1)S(1)}, u32[]{:S(2)}, u32[]{:S(2)}) collective-permute-start(bf16[272,512]{1,0:T(8,128)(2,1)S(1)} %concatenate.7.rest_0_), channel_id=1, source_target_pairs={{0,32},{32,64},{64,96},{96,128},{128,160},{160,192},{192,224},{224... | collective-permute-start | bytes 835592 | tf_op jit(solution)/shard_map/ppermute | solution.py:30
  51.4 8.6 %collective-permute-start.6 = (bf16[272,512]{1,0:T(8,128)(2,1)S(1)}, bf16[272,512]{1,0:T(8,128)(2,1)S(1)}, u32[]{:S(2)}, u32[]{:S(2)}) collective-permute-start(bf16[272,512]{1,0:T(8,128)(2,1)S(1)} %concatenate.7.rest_0_), channel_id=1, source_target_pairs={{0,224},{32,0},{64,32},{96,64},{128,96},{160,128},{192,160},{224,1... | collective-permute-start | bytes 835592 | tf_op jit(solution)/shard_map/ppermute | solution.py:30
  60.0 5.1 %collective-permute-done.8.rest_4_ = bf16[272,512]{1,0:T(8,128)(2,1)S(1)} collective-permute-done((bf16[272,512]{1,0:T(8,128)(2,1)S(1)}, bf16[272,512]{1,0:T(8,128)(2,1)S(1)}, u32[]{:S(2)}, u32[]{:S(2)}) %collective-permute-start.8) | collective-permute-done | bytes 278560 | tf_op jit(solution)/shard_map/ppermute | solution.py:30
  67.1 4.6 %collective-permute-start.7 = (bf16[272,512]{1,0:T(8,128)(2,1)S(1)}, bf16[272,512]{1,0:T(8,128)(2,1)}, u32[]{:S(2)}, u32[]{:S(2)}) collective-permute-start(bf16[272,512]{1,0:T(8,128)(2,1)S(1)} %collective-permute-done.6.rest_1_), channel_id=1, source_target_pairs={{0,224},{32,0},{64,32},{96,64},{128,96},{160,128},{192,160},{224,1... | collective-permute-start | bytes 835592 | tf_op jit(solution)/shard_map/ppermute | solution.py:30
  71.6 4.3 %collective-permute-done.9.rest_5_ = bf16[272,512]{1,0:T(8,128)(2,1)} collective-permute-done((bf16[272,512]{1,0:T(8,128)(2,1)S(1)}, bf16[272,512]{1,0:T(8,128)(2,1)}, u32[]{:S(2)}, u32[]{:S(2)}) %collective-permute-start.9) | collective-permute-done | bytes 278560 | tf_op jit(solution)/shard_map/ppermute | solution.py:30
  77.9 4.6 %collective-permute-start.11 = (bf16[272,512]{1,0:T(8,128)(2,1)}, bf16[272,512]{1,0:T(8,128)(2,1)S(1)}, u32[]{:S(2)}, u32[]{:S(2)}) collective-permute-start(bf16[272,512]{1,0:T(8,128)(2,1)} %collective-permute-done.7.rest_2_), channel_id=1, source_target_pairs={{0,224},{32,0},{64,32},{96,64},{128,96},{160,128},{192,160},{224,1... | collective-permute-start | bytes 835592 | tf_op jit(solution)/shard_map/ppermute | solution.py:30
  89.0 5.3 %collective-permute-start.13 = (bf16[128,512]{1,0:T(8,128)(2,1)S(1)}, bf16[128,512]{1,0:T(8,128)(2,1)S(1)}, u32[]{:S(2)}, u32[]{:S(2)}) collective-permute-start(bf16[128,512]{1,0:T(8,128)(2,1)S(1)} %slice.56), channel_id=1, source_target_pairs={{0,224},{32,0},{64,32},{96,64},{128,96},{160,128},{192,160},{224,1... | collective-permute-start | bytes 393224 | tf_op jit(solution)/shard_map/ppermute | solution.py:30
  98.4 4.7 %collective-permute-start.15 = (bf16[1024,2176]{1,0:T(8,128)(2,1)}, bf16[1024,2176]{1,0:T(8,128)(2,1)S(1)}, u32[]{:S(2)}, u32[]{:S(2)}) collective-permute-start(bf16[1024,2176]{1,0:T(8,128)(2,1)} %all-gather.2.cloned.1.call-done), channel_id=1, source_target_pairs={{0,16},{16,0},{1,17},{17,1},{2,18},{18,2},{3,19},{19,3},{4,20},{20... | collective-permute-start | bytes 13369352 | tf_op jit(solution)/shard_map/ppermute | solution.py:26
  105.4 7.5 %near_rows.1 = (f32[1024,1024]{1,0:T(8,128)S(1)}, f32[8,128]{1,0:T(8,128)S(1)}, f32[16,128]{1,0:T(8,128)S(1)}, bf16[2048,512]{1,0:T(8,128)(2,1)S(1)}) custom-call(s32[2]{0:T(128)S(1)} %pad_add_fusion.ints, bf16[8,128,2176]{2,1,0:T(8,128)(2,1)S(1)} %bitcast.13, bf16[2048,512]{1,0:T(8,128)(2,1)S(1)} %get-tuple-element.43.proj_ref, ...), custom_call_target="tpu_custom_call" | custom-call | flops 4294967296 | bytes 6291456 | tf_op jit(solution)/shard_map/near_rows/pallas_call | solution.py:44
  112.9 7.5 %far_rows.1 = (f32[1024,1024]{1,0:T(8,128)S(1)}, f32[24,128]{1,0:T(8,128)S(1)}) custom-call(s32[2]{0:T(128)S(1)} %pad_add_fusion.ints, bf16[8,128,2176]{2,1,0:T(8,128)(2,1)S(1)} %bitcast.14, bf16[2048,512]{1,0:T(8,128)(2,1)S(1)} %get-tuple-element.47.proj_ref, f32[8,128]{1,0:T(8,128)S(1)} %get-tuple-element.44.count_ref, ...), custom_call_target="tpu_custom_call" | custom-call | flops 4294967296 | bytes 6291456 | tf_op jit(solution)/shard_map/far_rows/pallas_call | solution.py:44
  129.9 3.9 %collective-permute-start.18 = (f32[24,128]{1,0:T(8,128)S(1)}, f32[24,128]{1,0:T(8,128)S(1)}, u32[]{:S(2)}, u32[]{:S(2)}) collective-permute-start(f32[24,128]{1,0:T(8,128)S(1)} %add.53), channel_id=1, source_target_pairs={{0,64},{32,96},{64,0},{96,32},{128,192},{160,224},{192,128},{224,1... | collective-permute-start | bytes 36872 | tf_op jit(solution)/shard_map/ppermute | solution.py:26
  135.2 5.0 %collective-permute-start.19 = (f32[24,128]{1,0:T(8,128)S(1)}, f32[24,128]{1,0:T(8,128)S(1)}, u32[]{:S(2)}, u32[]{:S(2)}) collective-permute-start(f32[24,128]{1,0:T(8,128)S(1)} %add.54), channel_id=1, source_target_pairs={{0,128},{32,160},{64,192},{96,224},{128,0},{160,32},{192,64},{224,... | collective-permute-start | bytes 36872 | tf_op jit(solution)/shard_map/ppermute | solution.py:26
  140.2 3.6 %collective-permute-done.19 = f32[24,128]{1,0:T(8,128)S(1)} collective-permute-done((f32[24,128]{1,0:T(8,128)S(1)}, f32[24,128]{1,0:T(8,128)S(1)}, u32[]{:S(2)}, u32[]{:S(2)}) %collective-permute-start.19) | collective-permute-done | bytes 12320 | tf_op jit(solution)/shard_map/ppermute | solution.py:26
  148.6 4.0 %collective-permute-start.21 = (f32[24,128]{1,0:T(8,128)S(1)}, f32[24,128]{1,0:T(8,128)S(1)}, u32[]{:S(2)}, u32[]{:S(2)}) collective-permute-start(f32[24,128]{1,0:T(8,128)S(1)} %add.56), channel_id=1, source_target_pairs={{0,4},{2,6},{4,0},{6,2},{8,12},{10,14},{12,8},{14,10},{1,5},{3,7},... | collective-permute-start | bytes 36872 | tf_op jit(solution)/shard_map/ppermute | solution.py:26
  154.3 7.5 %collective-permute-start.22 = (f32[24,128]{1,0:T(8,128)S(1)}, f32[24,128]{1,0:T(8,128)S(1)}, u32[]{:S(2)}, u32[]{:S(2)}) collective-permute-start(f32[24,128]{1,0:T(8,128)S(1)} %add.57), channel_id=1, source_target_pairs={{0,8},{2,10},{4,12},{6,14},{8,0},{10,2},{12,4},{14,6},{1,9},{3,11}... | collective-permute-start | bytes 36872 | tf_op jit(solution)/shard_map/ppermute | solution.py:26
  162.9 3.7 %collective-permute-start.23 = (f32[24,128]{1,0:T(8,128)S(1)}, f32[24,128]{1,0:T(8,128)S(1)}, u32[]{:S(2)}, u32[]{:S(2)}) collective-permute-start(f32[24,128]{1,0:T(8,128)S(1)} %add.58), channel_id=1, source_target_pairs={{0,256},{256,0},{1,257},{257,1},{2,258},{258,2},{3,259},{259,3},{4... | collective-permute-start | bytes 36872 | tf_op jit(solution)/shard_map/ppermute | solution.py:26
  170.0 4.0 %collective-permute-done.24 = f32[24,128]{1,0:T(8,128)S(1)} collective-permute-done((f32[24,128]{1,0:T(8,128)S(1)}, f32[24,128]{1,0:T(8,128)S(1)}, u32[]{:S(2)}, u32[]{:S(2)}) %collective-permute-start.24) | collective-permute-done | bytes 12320 | tf_op jit(solution)/shard_map/ppermute | solution.py:26
  174.0 5.2 %reduce-scatter.2.cloned.1.call-done = f32[128,1024]{1,0:T(8,128)} async-done(((f32[1024,1024]{1,0:T(8,128)}), f32[128,1024]{1,0:T(8,128)}) %reduce-scatter.2.cloned.1.call-update) | async-done | bytes 524304 | tf_op jit(solution)/shard_map/reduce_scatter | solution.py:295
  180.3 5.1 %collective-permute-start.25 = (f32[128,512]{1,0:T(8,128)S(1)}, f32[128,512]{1,0:T(8,128)S(1)}, u32[]{:S(2)}, u32[]{:S(2)}) collective-permute-start(f32[128,512]{1,0:T(8,128)S(1)} %get-tuple-element.56), channel_id=1, source_target_pairs={{0,0},{1,16},{16,1},{17,17},{256,256},{257,272},{272,257},{273,273... | collective-permute-start | bytes 786440 | tf_op jit(solution)/shard_map/ppermute | solution.py:313
  (95 shorter events, 66.6 us)
Async XLA Ops:
  7.2 91.2 %all-gather.2.cloned.1.call-start = ((), (), s32[]{:S(2)}) async-start(), calls=%async_computation.1 | async-start | bytes 5013504 | tf_op jit(solution)/shard_map/all_gather | solution.py:247
  9.4 10.1 %collective-permute-start = (bf16[80,512]{1,0:T(8,128)(2,1)S(1)}, bf16[80,512]{1,0:T(8,128)(2,1)S(1)}, u32[]{:S(2)}, u32[]{:S(2)}) collective-permute-start(bf16[80,512]{1,0:T(8,128)(2,1)S(1)} %pad_maximum_fusion), channel_id=1, source_target_pairs={{0,0},{1,16},{16,1},{17,17},{2,2},{3,18},{18,3},{19,19},{4,4},{5,2... | collective-permute-start | bytes 245768 | tf_op jit(solution)/shard_map/ppermute | solution.py:218
  19.5 13.2 %collective-permute-start.1 = (bf16[128,2176]{1,0:T(8,128)(2,1)S(1)}, bf16[128,2176]{1,0:T(8,128)(2,1)S(1)}, u32[]{:S(2)}, u32[]{:S(2)}) collective-permute-start(bf16[128,2176]{1,0:T(8,128)(2,1)S(1)} %get-tuple-element.31), channel_id=1, source_target_pairs={{0,0},{1,16},{16,1},{17,17},{2,2},{3,18},{18,3},{19,19},{4,4},{5,2... | collective-permute-start | bytes 1671176 | tf_op jit(solution)/shard_map/ppermute | solution.py:232
  22.7 8.3 %collective-permute-start.3 = (bf16[80,512]{1,0:T(8,128)(2,1)S(1)}, bf16[80,512]{1,0:T(8,128)(2,1)S(1)}, u32[]{:S(2)}, u32[]{:S(2)}) collective-permute-start(bf16[80,512]{1,0:T(8,128)(2,1)S(1)} %collective-permute-done), channel_id=1, source_target_pairs={{0,1},{1,0},{256,257},{257,256},{2,3},{3,2},{258,259},{259,258},{4... | collective-permute-start | bytes 245768 | tf_op jit(solution)/shard_map/ppermute | solution.py:201
  24.7 6.4 %collective-permute-start.2 = (f32[16,128]{1,0:T(8,128)S(1)}, f32[16,128]{1,0:T(8,128)S(1)}, u32[]{:S(2)}, u32[]{:S(2)}) collective-permute-start(f32[16,128]{1,0:T(8,128)S(1)} %get-tuple-element.32), channel_id=1, source_target_pairs={{0,16},{1,0},{16,17},{17,1},{2,18},{3,2},{18,19},{19,3},{4,20},{5,... | collective-permute-start | bytes 24584 | tf_op jit(solution)/shard_map/ppermute | solution.py:233
  33.6 145.5 %reduce-scatter.2.cloned.1.call-start = ((), (), s32[]{:S(2)}) async-start(), calls=%async_computation.2 | async-start | bytes 4718592 | tf_op jit(solution)/shard_map/reduce_scatter | solution.py:295
  33.7 5.8 %collective-permute-start.4 = (bf16[80,512]{1,0:T(8,128)(2,1)S(1)}, bf16[80,512]{1,0:T(8,128)(2,1)S(1)}, u32[]{:S(2)}, u32[]{:S(2)}) collective-permute-start(bf16[80,512]{1,0:T(8,128)(2,1)S(1)} %collective-permute-done), channel_id=1, source_target_pairs={{0,256},{1,257},{256,0},{257,1},{2,258},{3,259},{258,2},{259,3},{4... | collective-permute-start | bytes 245768 | tf_op jit(solution)/shard_map/ppermute | solution.py:201
  35.9 6.4 %collective-permute-start.5 = (bf16[80,512]{1,0:T(8,128)(2,1)S(1)}, bf16[80,512]{1,0:T(8,128)(2,1)S(1)}, u32[]{:S(2)}, u32[]{:S(2)}) collective-permute-start(bf16[80,512]{1,0:T(8,128)(2,1)S(1)} %collective-permute-done), channel_id=1, source_target_pairs={{0,257},{1,256},{256,1},{257,0},{2,259},{3,258},{258,3},{259,2},{4... | collective-permute-start | bytes 245768 | tf_op jit(solution)/shard_map/ppermute | solution.py:201
  42.5 44.4 %collective-permute-start.12 = (bf16[2048,512]{1,0:T(8,128)(2,1)S(1)}, bf16[2048,512]{1,0:T(8,128)(2,1)}, u32[]{:S(2)}, u32[]{:S(2)}) collective-permute-start(bf16[2048,512]{1,0:T(8,128)(2,1)S(1)} %copy-done.2), channel_id=1, source_target_pairs={{0,0},{1,16},{16,1},{17,17},{2,2},{3,18},{18,3},{19,19},{4,4},{5,2... | collective-permute-start | bytes 6291464 | tf_op jit(solution)/shard_map/ppermute | solution.py:252
  47.4 17.7 %collective-permute-start.8 = (bf16[272,512]{1,0:T(8,128)(2,1)S(1)}, bf16[272,512]{1,0:T(8,128)(2,1)S(1)}, u32[]{:S(2)}, u32[]{:S(2)}) collective-permute-start(bf16[272,512]{1,0:T(8,128)(2,1)S(1)} %concatenate.7.rest_0_), channel_id=1, source_target_pairs={{0,32},{32,64},{64,96},{96,128},{128,160},{160,192},{192,224},{224... | collective-permute-start | bytes 835592 | tf_op jit(solution)/shard_map/ppermute | solution.py:30
  51.4 15.6 %collective-permute-start.6 = (bf16[272,512]{1,0:T(8,128)(2,1)S(1)}, bf16[272,512]{1,0:T(8,128)(2,1)S(1)}, u32[]{:S(2)}, u32[]{:S(2)}) collective-permute-start(bf16[272,512]{1,0:T(8,128)(2,1)S(1)} %concatenate.7.rest_0_), channel_id=1, source_target_pairs={{0,224},{32,0},{64,32},{96,64},{128,96},{160,128},{192,160},{224,1... | collective-permute-start | bytes 835592 | tf_op jit(solution)/shard_map/ppermute | solution.py:30
  65.1 10.8 %collective-permute-start.9 = (bf16[272,512]{1,0:T(8,128)(2,1)S(1)}, bf16[272,512]{1,0:T(8,128)(2,1)}, u32[]{:S(2)}, u32[]{:S(2)}) collective-permute-start(bf16[272,512]{1,0:T(8,128)(2,1)S(1)} %collective-permute-done.8.rest_4_), channel_id=1, source_target_pairs={{0,32},{32,64},{64,96},{96,128},{128,160},{160,192},{192,224},{224... | collective-permute-start | bytes 835592 | tf_op jit(solution)/shard_map/ppermute | solution.py:30
  67.1 10.8 %collective-permute-start.7 = (bf16[272,512]{1,0:T(8,128)(2,1)S(1)}, bf16[272,512]{1,0:T(8,128)(2,1)}, u32[]{:S(2)}, u32[]{:S(2)}) collective-permute-start(bf16[272,512]{1,0:T(8,128)(2,1)S(1)} %collective-permute-done.6.rest_1_), channel_id=1, source_target_pairs={{0,224},{32,0},{64,32},{96,64},{128,96},{160,128},{192,160},{224,1... | collective-permute-start | bytes 835592 | tf_op jit(solution)/shard_map/ppermute | solution.py:30
  76.0 10.1 %collective-permute-start.10 = (bf16[272,512]{1,0:T(8,128)(2,1)}, bf16[272,512]{1,0:T(8,128)(2,1)S(1)}, u32[]{:S(2)}, u32[]{:S(2)}) collective-permute-start(bf16[272,512]{1,0:T(8,128)(2,1)} %collective-permute-done.9.rest_5_), channel_id=1, source_target_pairs={{0,32},{32,64},{64,96},{96,128},{128,160},{160,192},{192,224},{224... | collective-permute-start | bytes 835592 | tf_op jit(solution)/shard_map/ppermute | solution.py:30
  77.9 9.1 %collective-permute-start.11 = (bf16[272,512]{1,0:T(8,128)(2,1)}, bf16[272,512]{1,0:T(8,128)(2,1)S(1)}, u32[]{:S(2)}, u32[]{:S(2)}) collective-permute-start(bf16[272,512]{1,0:T(8,128)(2,1)} %collective-permute-done.7.rest_2_), channel_id=1, source_target_pairs={{0,224},{32,0},{64,32},{96,64},{128,96},{160,128},{192,160},{224,1... | collective-permute-start | bytes 835592 | tf_op jit(solution)/shard_map/ppermute | solution.py:30
  87.0 10.0 %collective-permute-start.14 = (bf16[144,512]{1,0:T(8,128)(2,1)S(1)}, bf16[144,512]{1,0:T(8,128)(2,1)S(1)}, u32[]{:S(2)}, u32[]{:S(2)}) collective-permute-start(bf16[144,512]{1,0:T(8,128)(2,1)S(1)} %slice.57), channel_id=1, source_target_pairs={{0,32},{32,64},{64,96},{96,128},{128,160},{160,192},{192,224},{224... | collective-permute-start | bytes 442376 | tf_op jit(solution)/shard_map/ppermute | solution.py:30
  89.0 8.1 %collective-permute-start.13 = (bf16[128,512]{1,0:T(8,128)(2,1)S(1)}, bf16[128,512]{1,0:T(8,128)(2,1)S(1)}, u32[]{:S(2)}, u32[]{:S(2)}) collective-permute-start(bf16[128,512]{1,0:T(8,128)(2,1)S(1)} %slice.56), channel_id=1, source_target_pairs={{0,224},{32,0},{64,32},{96,64},{128,96},{160,128},{192,160},{224,1... | collective-permute-start | bytes 393224 | tf_op jit(solution)/shard_map/ppermute | solution.py:30
  98.4 14.5 %collective-permute-start.15 = (bf16[1024,2176]{1,0:T(8,128)(2,1)}, bf16[1024,2176]{1,0:T(8,128)(2,1)S(1)}, u32[]{:S(2)}, u32[]{:S(2)}) collective-permute-start(bf16[1024,2176]{1,0:T(8,128)(2,1)} %all-gather.2.cloned.1.call-done), channel_id=1, source_target_pairs={{0,16},{16,0},{1,17},{17,1},{2,18},{18,2},{3,19},{19,3},{4,20},{20... | collective-permute-start | bytes 13369352 | tf_op jit(solution)/shard_map/ppermute | solution.py:26
  135.2 8.6 %collective-permute-start.19 = (f32[24,128]{1,0:T(8,128)S(1)}, f32[24,128]{1,0:T(8,128)S(1)}, u32[]{:S(2)}, u32[]{:S(2)}) collective-permute-start(f32[24,128]{1,0:T(8,128)S(1)} %add.54), channel_id=1, source_target_pairs={{0,128},{32,160},{64,192},{96,224},{128,0},{160,32},{192,64},{224,... | collective-permute-start | bytes 36872 | tf_op jit(solution)/shard_map/ppermute | solution.py:26
  148.6 5.7 %collective-permute-start.21 = (f32[24,128]{1,0:T(8,128)S(1)}, f32[24,128]{1,0:T(8,128)S(1)}, u32[]{:S(2)}, u32[]{:S(2)}) collective-permute-start(f32[24,128]{1,0:T(8,128)S(1)} %add.56), channel_id=1, source_target_pairs={{0,4},{2,6},{4,0},{6,2},{8,12},{10,14},{12,8},{14,10},{1,5},{3,7},... | collective-permute-start | bytes 36872 | tf_op jit(solution)/shard_map/ppermute | solution.py:26
  154.3 8.5 %collective-permute-start.22 = (f32[24,128]{1,0:T(8,128)S(1)}, f32[24,128]{1,0:T(8,128)S(1)}, u32[]{:S(2)}, u32[]{:S(2)}) collective-permute-start(f32[24,128]{1,0:T(8,128)S(1)} %add.57), channel_id=1, source_target_pairs={{0,8},{2,10},{4,12},{6,14},{8,0},{10,2},{12,4},{14,6},{1,9},{3,11}... | collective-permute-start | bytes 36872 | tf_op jit(solution)/shard_map/ppermute | solution.py:26
  168.1 5.9 %collective-permute-start.24 = (f32[24,128]{1,0:T(8,128)S(1)}, f32[24,128]{1,0:T(8,128)S(1)}, u32[]{:S(2)}, u32[]{:S(2)}) collective-permute-start(f32[24,128]{1,0:T(8,128)S(1)} %add.59), channel_id=1, source_target_pairs={{0,1},{1,0},{2,3},{3,2},{4,5},{5,4},{6,7},{7,6},{8,9},{9,8},{10,11... | collective-permute-start | bytes 36872 | tf_op jit(solution)/shard_map/ppermute | solution.py:26
  180.3 11.3 %collective-permute-start.25 = (f32[128,512]{1,0:T(8,128)S(1)}, f32[128,512]{1,0:T(8,128)S(1)}, u32[]{:S(2)}, u32[]{:S(2)}) collective-permute-start(f32[128,512]{1,0:T(8,128)S(1)} %get-tuple-element.56), channel_id=1, source_target_pairs={{0,0},{1,16},{16,1},{17,17},{256,256},{257,272},{272,257},{273,273... | collective-permute-start | bytes 786440 | tf_op jit(solution)/shard_map/ppermute | solution.py:313
  185.4 8.9 %collective-permute-start.26 = (f32[128,512]{1,0:T(8,128)S(1)}, f32[128,512]{1,0:T(8,128)S(1)}, u32[]{:S(2)}, u32[]{:S(2)}) collective-permute-start(f32[128,512]{1,0:T(8,128)S(1)} %get-tuple-element.55), channel_id=1, source_target_pairs={{0,256},{1,272},{16,257},{17,273},{256,0},{257,16},{272,1},{273,17... | collective-permute-start | bytes 786440 | tf_op jit(solution)/shard_map/ppermute | solution.py:313
  (14 other events, 154.3 us)
Sparse Core Ops, SparseCore 0:
  33.8 62.7 all-gather.1
  122.5 56.6 reduce-scatter.1

commit v6 on v5

--- a/solution.py
+++ b/solution.py
@@ -232,7 +232,7 @@
     scaled = lax.ppermute(scaled, ("c", "xh"), SWAP)
     cross = lax.ppermute(squares, ("c", "xh"), CROSS)
     flips = projection_flips(own)
-    scaled, cross, flips[0] = tie(scaled, cross, flips[0])
+    scaled, cross, flips[0], flips[1] = tie(scaled, cross, flips[0], flips[1])
     (joined,) = call(
         join_kernel,
         "join",

time: 208 us -> 209 us (level)
  starting transfers between devices: 107 us -> 113 us
  waiting for transfers between devices: 47.2 us -> 43.4 us
    ppermute x11, waiting for transfers between devices: 18.8 us -> 14.2 us  [flip(): return lax.ppermute(x, axis, [(i, i ^ bit) for i in range(size)])]
    ppermute x11, starting transfers between devices: 40.1 us -> 42.9 us  [flip(): return lax.ppermute(x, axis, [(i, i ^ bit) for i in range(size)])]
  transfers between devices with their start and end apart: 30 -> 30, of which waited for: 20 -> 21; matrix products, arithmetic and copies ran while one was open for 2% -> 2% of each run, Pallas kernels for 5% -> 5%
where the time goes in v6:
time: 209 us; the launch traced here: 208 us
  starting transfers between devices  113 us (54%)
  waiting for transfers between devices  43.4 us (21%)
  between operations  18.9 us (9%)
  Pallas kernels  17.8 us (9%)
  local copies, waits for them, and re-layouts  11.3 us (5%)
  other arithmetic  3.62 us (2%)
    ppermute x11, starting transfers between devices, flip(): return lax.ppermute(x, axis, [(i, i ^ bit) for i in range(size)])  42.9 us
    ppermute x8, starting transfers between devices, shift(): return lax.ppermute(x, axis, [(i, (i + by) % size) for i in range(size)])  32.8 us
    pallas_call x5, Pallas kernels, call(): pl.pallas_call(kernel, in_specs=in_specs, out_specs=out_specs, out_shape=...  17.8 us
    ppermute x11, waiting for transfers between devices, flip(): return lax.ppermute(x, axis, [(i, i ^ bit) for i in range(size)])  14.2 us
    ppermute x8, waiting for transfers between devices, shift(): return lax.ppermute(x, axis, [(i, (i + by) % size) for i in range(size)])  13.2 us
    ppermute x3, starting transfers between devices, projection_flips(): lax.ppermute(own, ('xl', 'xh'), [(i, i ^ fx * 2 + fc) for i in range(4)])  8.32 us
    ppermute x2, starting transfers between devices, on_device(): rows += lax.ppermute(sent, ('xl', 'c', 'xh'), across(fx))  7.97 us
    unnamed x16, local copies, waits for them, and re-layouts  7.56 us
  transfers between devices with their start and end apart: 30, of which 21 were waited for; matrix products, arithmetic and copies ran while one was open for 2% of the time, Pallas kernels for 5%

profile of v6, /device:TPU:1, one launch (start us, length us, event | category | flops | bytes accessed | tf_op | source)
XLA Modules:
  0.0 207.8 jit_solution(14726697742901488459)
XLA Ops:
  9.4 6.0 %collective-permute-start = (bf16[80,512]{1,0:T(8,128)(2,1)S(1)}, bf16[80,512]{1,0:T(8,128)(2,1)S(1)}, u32[]{:S(2)}, u32[]{:S(2)}) collective-permute-start(bf16[80,512]{1,0:T(8,128)(2,1)S(1)} %pad_maximum_fusion), channel_id=1, source_target_pairs={{0,0},{1,16},{16,1},{17,17},{2,2},{3,18},{18,3},{19,19},{4,4},{5,2... | collective-permute-start | bytes 245768 | tf_op jit(solution)/shard_map/ppermute | solution.py:218
  19.5 3.2 %collective-permute-start.1 = (bf16[128,2176]{1,0:T(8,128)(2,1)S(1)}, bf16[128,2176]{1,0:T(8,128)(2,1)S(1)}, u32[]{:S(2)}, u32[]{:S(2)}) collective-permute-start(bf16[128,2176]{1,0:T(8,128)(2,1)S(1)} %get-tuple-element.32), channel_id=1, source_target_pairs={{0,0},{1,16},{16,1},{17,17},{2,2},{3,18},{18,3},{19,19},{4,4},{5,2... | collective-permute-start | bytes 1671176 | tf_op jit(solution)/shard_map/ppermute | solution.py:232
  26.9 5.5 %collective-permute-start.2 = (f32[16,128]{1,0:T(8,128)S(1)}, f32[16,128]{1,0:T(8,128)S(1)}, u32[]{:S(2)}, u32[]{:S(2)}) collective-permute-start(f32[16,128]{1,0:T(8,128)S(1)} %get-tuple-element.33), channel_id=1, source_target_pairs={{0,16},{1,0},{16,17},{17,1},{2,18},{3,2},{18,19},{19,3},{4,20},{5,... | collective-permute-start | bytes 24584 | tf_op jit(solution)/shard_map/ppermute | solution.py:233
  34.6 4.2 %collective-permute-start.5 = (bf16[80,512]{1,0:T(8,128)(2,1)S(1)}, bf16[80,512]{1,0:T(8,128)(2,1)S(1)}, u32[]{:S(2)}, u32[]{:S(2)}) collective-permute-start(bf16[80,512]{1,0:T(8,128)(2,1)S(1)} %collective-permute-done), channel_id=1, source_target_pairs={{0,257},{1,256},{256,1},{257,0},{2,259},{3,258},{258,3},{259,2},{4... | collective-permute-start | bytes 245768 | tf_op jit(solution)/shard_map/ppermute | solution.py:201
  41.2 5.9 %collective-permute-start.12 = (bf16[2048,512]{1,0:T(8,128)(2,1)S(1)}, bf16[2048,512]{1,0:T(8,128)(2,1)}, u32[]{:S(2)}, u32[]{:S(2)}) collective-permute-start(bf16[2048,512]{1,0:T(8,128)(2,1)S(1)} %copy-done.2), channel_id=1, source_target_pairs={{0,0},{1,16},{16,1},{17,17},{2,2},{3,18},{18,3},{19,19},{4,4},{5,2... | collective-permute-start | bytes 6291464 | tf_op jit(solution)/shard_map/ppermute | solution.py:252
  47.1 4.0 %collective-permute-start.8 = (bf16[272,512]{1,0:T(8,128)(2,1)S(1)}, bf16[272,512]{1,0:T(8,128)(2,1)S(1)}, u32[]{:S(2)}, u32[]{:S(2)}) collective-permute-start(bf16[272,512]{1,0:T(8,128)(2,1)S(1)} %concatenate.7.rest_0_), channel_id=1, source_target_pairs={{0,32},{32,64},{64,96},{96,128},{128,160},{160,192},{192,224},{224... | collective-permute-start | bytes 835592 | tf_op jit(solution)/shard_map/ppermute | solution.py:30
  51.1 8.6 %collective-permute-start.6 = (bf16[272,512]{1,0:T(8,128)(2,1)S(1)}, bf16[272,512]{1,0:T(8,128)(2,1)S(1)}, u32[]{:S(2)}, u32[]{:S(2)}) collective-permute-start(bf16[272,512]{1,0:T(8,128)(2,1)S(1)} %concatenate.7.rest_0_), channel_id=1, source_target_pairs={{0,224},{32,0},{64,32},{96,64},{128,96},{160,128},{192,160},{224,1... | collective-permute-start | bytes 835592 | tf_op jit(solution)/shard_map/ppermute | solution.py:30
  59.7 5.1 %collective-permute-done.8.rest_4_ = bf16[272,512]{1,0:T(8,128)(2,1)S(1)} collective-permute-done((bf16[272,512]{1,0:T(8,128)(2,1)S(1)}, bf16[272,512]{1,0:T(8,128)(2,1)S(1)}, u32[]{:S(2)}, u32[]{:S(2)}) %collective-permute-start.8) | collective-permute-done | bytes 278560 | tf_op jit(solution)/shard_map/ppermute | solution.py:30
  66.7 4.6 %collective-permute-start.7 = (bf16[272,512]{1,0:T(8,128)(2,1)S(1)}, bf16[272,512]{1,0:T(8,128)(2,1)}, u32[]{:S(2)}, u32[]{:S(2)}) collective-permute-start(bf16[272,512]{1,0:T(8,128)(2,1)S(1)} %collective-permute-done.6.rest_1_), channel_id=1, source_target_pairs={{0,224},{32,0},{64,32},{96,64},{128,96},{160,128},{192,160},{224,1... | collective-permute-start | bytes 835592 | tf_op jit(solution)/shard_map/ppermute | solution.py:30
  71.3 4.3 %collective-permute-done.9.rest_5_ = bf16[272,512]{1,0:T(8,128)(2,1)} collective-permute-done((bf16[272,512]{1,0:T(8,128)(2,1)S(1)}, bf16[272,512]{1,0:T(8,128)(2,1)}, u32[]{:S(2)}, u32[]{:S(2)}) %collective-permute-start.9) | collective-permute-done | bytes 278560 | tf_op jit(solution)/shard_map/ppermute | solution.py:30
  77.5 4.6 %collective-permute-start.11 = (bf16[272,512]{1,0:T(8,128)(2,1)}, bf16[272,512]{1,0:T(8,128)(2,1)S(1)}, u32[]{:S(2)}, u32[]{:S(2)}) collective-permute-start(bf16[272,512]{1,0:T(8,128)(2,1)} %collective-permute-done.7.rest_2_), channel_id=1, source_target_pairs={{0,224},{32,0},{64,32},{96,64},{128,96},{160,128},{192,160},{224,1... | collective-permute-start | bytes 835592 | tf_op jit(solution)/shard_map/ppermute | solution.py:30
  88.6 5.3 %collective-permute-start.13 = (bf16[128,512]{1,0:T(8,128)(2,1)S(1)}, bf16[128,512]{1,0:T(8,128)(2,1)S(1)}, u32[]{:S(2)}, u32[]{:S(2)}) collective-permute-start(bf16[128,512]{1,0:T(8,128)(2,1)S(1)} %slice.56), channel_id=1, source_target_pairs={{0,224},{32,0},{64,32},{96,64},{128,96},{160,128},{192,160},{224,1... | collective-permute-start | bytes 393224 | tf_op jit(solution)/shard_map/ppermute | solution.py:30
  99.6 3.1 %collective-permute-start.15 = (bf16[1024,2176]{1,0:T(8,128)(2,1)}, bf16[1024,2176]{1,0:T(8,128)(2,1)S(1)}, u32[]{:S(2)}, u32[]{:S(2)}) collective-permute-start(bf16[1024,2176]{1,0:T(8,128)(2,1)} %all-gather.2.cloned.1.call-done), channel_id=1, source_target_pairs={{0,16},{16,0},{1,17},{17,1},{2,18},{18,2},{3,19},{19,3},{4,20},{20... | collective-permute-start | bytes 13369352 | tf_op jit(solution)/shard_map/ppermute | solution.py:26
  105.0 7.5 %near_rows.1 = (f32[1024,1024]{1,0:T(8,128)S(1)}, f32[8,128]{1,0:T(8,128)S(1)}, f32[16,128]{1,0:T(8,128)S(1)}, bf16[2048,512]{1,0:T(8,128)(2,1)S(1)}) custom-call(s32[2]{0:T(128)S(1)} %pad_add_fusion.ints, bf16[8,128,2176]{2,1,0:T(8,128)(2,1)S(1)} %bitcast.13, bf16[2048,512]{1,0:T(8,128)(2,1)S(1)} %get-tuple-element.45.proj_ref, ...), custom_call_target="tpu_custom_call" | custom-call | flops 4294967296 | bytes 6291456 | tf_op jit(solution)/shard_map/near_rows/pallas_call | solution.py:44
  112.5 7.5 %far_rows.1 = (f32[1024,1024]{1,0:T(8,128)S(1)}, f32[24,128]{1,0:T(8,128)S(1)}) custom-call(s32[2]{0:T(128)S(1)} %pad_add_fusion.ints, bf16[8,128,2176]{2,1,0:T(8,128)(2,1)S(1)} %bitcast.14, bf16[2048,512]{1,0:T(8,128)(2,1)S(1)} %get-tuple-element.49.proj_ref, f32[8,128]{1,0:T(8,128)S(1)} %get-tuple-element.46.count_ref, ...), custom_call_target="tpu_custom_call" | custom-call | flops 4294967296 | bytes 6291456 | tf_op jit(solution)/shard_map/far_rows/pallas_call | solution.py:44
  129.5 3.9 %collective-permute-start.18 = (f32[24,128]{1,0:T(8,128)S(1)}, f32[24,128]{1,0:T(8,128)S(1)}, u32[]{:S(2)}, u32[]{:S(2)}) collective-permute-start(f32[24,128]{1,0:T(8,128)S(1)} %add.53), channel_id=1, source_target_pairs={{0,64},{32,96},{64,0},{96,32},{128,192},{160,224},{192,128},{224,1... | collective-permute-start | bytes 36872 | tf_op jit(solution)/shard_map/ppermute | solution.py:26
  134.8 7.2 %collective-permute-start.19 = (f32[24,128]{1,0:T(8,128)S(1)}, f32[24,128]{1,0:T(8,128)S(1)}, u32[]{:S(2)}, u32[]{:S(2)}) collective-permute-start(f32[24,128]{1,0:T(8,128)S(1)} %add.54), channel_id=1, source_target_pairs={{0,128},{32,160},{64,192},{96,224},{128,0},{160,32},{192,64},{224,... | collective-permute-start | bytes 36872 | tf_op jit(solution)/shard_map/ppermute | solution.py:26
  143.4 3.0 %collective-permute-start.20 = (f32[24,128]{1,0:T(8,128)S(1)}, f32[24,128]{1,0:T(8,128)S(1)}, u32[]{:S(2)}, u32[]{:S(2)}) collective-permute-start(f32[24,128]{1,0:T(8,128)S(1)} %add.55), channel_id=1, source_target_pairs={{0,2},{2,0},{4,6},{6,4},{8,10},{10,8},{12,14},{14,12},{1,3},{3,1},... | collective-permute-start | bytes 36872 | tf_op jit(solution)/shard_map/ppermute | solution.py:26
  148.2 4.1 %collective-permute-start.21 = (f32[24,128]{1,0:T(8,128)S(1)}, f32[24,128]{1,0:T(8,128)S(1)}, u32[]{:S(2)}, u32[]{:S(2)}) collective-permute-start(f32[24,128]{1,0:T(8,128)S(1)} %add.56), channel_id=1, source_target_pairs={{0,4},{2,6},{4,0},{6,2},{8,12},{10,14},{12,8},{14,10},{1,5},{3,7},... | collective-permute-start | bytes 36872 | tf_op jit(solution)/shard_map/ppermute | solution.py:26
  154.0 7.5 %collective-permute-start.22 = (f32[24,128]{1,0:T(8,128)S(1)}, f32[24,128]{1,0:T(8,128)S(1)}, u32[]{:S(2)}, u32[]{:S(2)}) collective-permute-start(f32[24,128]{1,0:T(8,128)S(1)} %add.57), channel_id=1, source_target_pairs={{0,8},{2,10},{4,12},{6,14},{8,0},{10,2},{12,4},{14,6},{1,9},{3,11}... | collective-permute-start | bytes 36872 | tf_op jit(solution)/shard_map/ppermute | solution.py:26
  162.5 3.5 %collective-permute-start.23 = (f32[24,128]{1,0:T(8,128)S(1)}, f32[24,128]{1,0:T(8,128)S(1)}, u32[]{:S(2)}, u32[]{:S(2)}) collective-permute-start(f32[24,128]{1,0:T(8,128)S(1)} %add.58), channel_id=1, source_target_pairs={{0,256},{256,0},{1,257},{257,1},{2,258},{258,2},{3,259},{259,3},{4... | collective-permute-start | bytes 36872 | tf_op jit(solution)/shard_map/ppermute | solution.py:26
  167.5 4.1 %collective-permute-start.24 = (f32[24,128]{1,0:T(8,128)S(1)}, f32[24,128]{1,0:T(8,128)S(1)}, u32[]{:S(2)}, u32[]{:S(2)}) collective-permute-start(f32[24,128]{1,0:T(8,128)S(1)} %add.59), channel_id=1, source_target_pairs={{0,1},{1,0},{2,3},{3,2},{4,5},{5,4},{6,7},{7,6},{8,9},{9,8},{10,11... | collective-permute-start | bytes 36872 | tf_op jit(solution)/shard_map/ppermute | solution.py:26
  173.5 6.0 %reduce-scatter.2.cloned.1.call-done = f32[128,1024]{1,0:T(8,128)} async-done(((f32[1024,1024]{1,0:T(8,128)}), f32[128,1024]{1,0:T(8,128)}) %reduce-scatter.2.cloned.1.call-update) | async-done | bytes 524304 | tf_op jit(solution)/shard_map/reduce_scatter | solution.py:295
  180.5 6.0 %collective-permute-start.25 = (f32[128,512]{1,0:T(8,128)S(1)}, f32[128,512]{1,0:T(8,128)S(1)}, u32[]{:S(2)}, u32[]{:S(2)}) collective-permute-start(f32[128,512]{1,0:T(8,128)S(1)} %get-tuple-element.58), channel_id=1, source_target_pairs={{0,0},{1,16},{16,1},{17,17},{256,256},{257,272},{272,257},{273,273... | collective-permute-start | bytes 786440 | tf_op jit(solution)/shard_map/ppermute | solution.py:313
  (95 shorter events, 64.3 us)
Async XLA Ops:
  7.2 92.4 %all-gather.2.cloned.1.call-start = ((), (), s32[]{:S(2)}) async-start(), calls=%async_computation.1 | async-start | bytes 5013504 | tf_op jit(solution)/shard_map/all_gather | solution.py:247
  9.4 10.1 %collective-permute-start = (bf16[80,512]{1,0:T(8,128)(2,1)S(1)}, bf16[80,512]{1,0:T(8,128)(2,1)S(1)}, u32[]{:S(2)}, u32[]{:S(2)}) collective-permute-start(bf16[80,512]{1,0:T(8,128)(2,1)S(1)} %pad_maximum_fusion), channel_id=1, source_target_pairs={{0,0},{1,16},{16,1},{17,17},{2,2},{3,18},{18,3},{19,19},{4,4},{5,2... | collective-permute-start | bytes 245768 | tf_op jit(solution)/shard_map/ppermute | solution.py:218
  19.5 14.1 %collective-permute-start.1 = (bf16[128,2176]{1,0:T(8,128)(2,1)S(1)}, bf16[128,2176]{1,0:T(8,128)(2,1)S(1)}, u32[]{:S(2)}, u32[]{:S(2)}) collective-permute-start(bf16[128,2176]{1,0:T(8,128)(2,1)S(1)} %get-tuple-element.32), channel_id=1, source_target_pairs={{0,0},{1,16},{16,1},{17,17},{2,2},{3,18},{18,3},{19,19},{4,4},{5,2... | collective-permute-start | bytes 1671176 | tf_op jit(solution)/shard_map/ppermute | solution.py:232
  22.7 10.4 %collective-permute-start.3 = (bf16[80,512]{1,0:T(8,128)(2,1)S(1)}, bf16[80,512]{1,0:T(8,128)(2,1)S(1)}, u32[]{:S(2)}, u32[]{:S(2)}) collective-permute-start(bf16[80,512]{1,0:T(8,128)(2,1)S(1)} %collective-permute-done), channel_id=1, source_target_pairs={{0,1},{1,0},{256,257},{257,256},{2,3},{3,2},{258,259},{259,258},{4... | collective-permute-start | bytes 245768 | tf_op jit(solution)/shard_map/ppermute | solution.py:201
  24.7 8.9 %collective-permute-start.4 = (bf16[80,512]{1,0:T(8,128)(2,1)S(1)}, bf16[80,512]{1,0:T(8,128)(2,1)S(1)}, u32[]{:S(2)}, u32[]{:S(2)}) collective-permute-start(bf16[80,512]{1,0:T(8,128)(2,1)S(1)} %collective-permute-done), channel_id=1, source_target_pairs={{0,256},{1,257},{256,0},{257,1},{2,258},{3,259},{258,2},{259,3},{4... | collective-permute-start | bytes 245768 | tf_op jit(solution)/shard_map/ppermute | solution.py:201
  26.9 6.3 %collective-permute-start.2 = (f32[16,128]{1,0:T(8,128)S(1)}, f32[16,128]{1,0:T(8,128)S(1)}, u32[]{:S(2)}, u32[]{:S(2)}) collective-permute-start(f32[16,128]{1,0:T(8,128)S(1)} %get-tuple-element.33), channel_id=1, source_target_pairs={{0,16},{1,0},{16,17},{17,1},{2,18},{3,2},{18,19},{19,3},{4,20},{5,... | collective-permute-start | bytes 24584 | tf_op jit(solution)/shard_map/ppermute | solution.py:233
  34.5 144.9 %reduce-scatter.2.cloned.1.call-start = ((), (), s32[]{:S(2)}) async-start(), calls=%async_computation.2 | async-start | bytes 4718592 | tf_op jit(solution)/shard_map/reduce_scatter | solution.py:295
  34.6 6.4 %collective-permute-start.5 = (bf16[80,512]{1,0:T(8,128)(2,1)S(1)}, bf16[80,512]{1,0:T(8,128)(2,1)S(1)}, u32[]{:S(2)}, u32[]{:S(2)}) collective-permute-start(bf16[80,512]{1,0:T(8,128)(2,1)S(1)} %collective-permute-done), channel_id=1, source_target_pairs={{0,257},{1,256},{256,1},{257,0},{2,259},{3,258},{258,3},{259,2},{4... | collective-permute-start | bytes 245768 | tf_op jit(solution)/shard_map/ppermute | solution.py:201
  41.2 45.4 %collective-permute-start.12 = (bf16[2048,512]{1,0:T(8,128)(2,1)S(1)}, bf16[2048,512]{1,0:T(8,128)(2,1)}, u32[]{:S(2)}, u32[]{:S(2)}) collective-permute-start(bf16[2048,512]{1,0:T(8,128)(2,1)S(1)} %copy-done.2), channel_id=1, source_target_pairs={{0,0},{1,16},{16,1},{17,17},{2,2},{3,18},{18,3},{19,19},{4,4},{5,2... | collective-permute-start | bytes 6291464 | tf_op jit(solution)/shard_map/ppermute | solution.py:252
  47.1 17.7 %collective-permute-start.8 = (bf16[272,512]{1,0:T(8,128)(2,1)S(1)}, bf16[272,512]{1,0:T(8,128)(2,1)S(1)}, u32[]{:S(2)}, u32[]{:S(2)}) collective-permute-start(bf16[272,512]{1,0:T(8,128)(2,1)S(1)} %concatenate.7.rest_0_), channel_id=1, source_target_pairs={{0,32},{32,64},{64,96},{96,128},{128,160},{160,192},{192,224},{224... | collective-permute-start | bytes 835592 | tf_op jit(solution)/shard_map/ppermute | solution.py:30
  51.1 15.6 %collective-permute-start.6 = (bf16[272,512]{1,0:T(8,128)(2,1)S(1)}, bf16[272,512]{1,0:T(8,128)(2,1)S(1)}, u32[]{:S(2)}, u32[]{:S(2)}) collective-permute-start(bf16[272,512]{1,0:T(8,128)(2,1)S(1)} %concatenate.7.rest_0_), channel_id=1, source_target_pairs={{0,224},{32,0},{64,32},{96,64},{128,96},{160,128},{192,160},{224,1... | collective-permute-start | bytes 835592 | tf_op jit(solution)/shard_map/ppermute | solution.py:30
  64.8 10.8 %collective-permute-start.9 = (bf16[272,512]{1,0:T(8,128)(2,1)S(1)}, bf16[272,512]{1,0:T(8,128)(2,1)}, u32[]{:S(2)}, u32[]{:S(2)}) collective-permute-start(bf16[272,512]{1,0:T(8,128)(2,1)S(1)} %collective-permute-done.8.rest_4_), channel_id=1, source_target_pairs={{0,32},{32,64},{64,96},{96,128},{128,160},{160,192},{192,224},{224... | collective-permute-start | bytes 835592 | tf_op jit(solution)/shard_map/ppermute | solution.py:30
  66.7 10.8 %collective-permute-start.7 = (bf16[272,512]{1,0:T(8,128)(2,1)S(1)}, bf16[272,512]{1,0:T(8,128)(2,1)}, u32[]{:S(2)}, u32[]{:S(2)}) collective-permute-start(bf16[272,512]{1,0:T(8,128)(2,1)S(1)} %collective-permute-done.6.rest_1_), channel_id=1, source_target_pairs={{0,224},{32,0},{64,32},{96,64},{128,96},{160,128},{192,160},{224,1... | collective-permute-start | bytes 835592 | tf_op jit(solution)/shard_map/ppermute | solution.py:30
  75.6 10.1 %collective-permute-start.10 = (bf16[272,512]{1,0:T(8,128)(2,1)}, bf16[272,512]{1,0:T(8,128)(2,1)S(1)}, u32[]{:S(2)}, u32[]{:S(2)}) collective-permute-start(bf16[272,512]{1,0:T(8,128)(2,1)} %collective-permute-done.9.rest_5_), channel_id=1, source_target_pairs={{0,32},{32,64},{64,96},{96,128},{128,160},{160,192},{192,224},{224... | collective-permute-start | bytes 835592 | tf_op jit(solution)/shard_map/ppermute | solution.py:30
  77.5 9.1 %collective-permute-start.11 = (bf16[272,512]{1,0:T(8,128)(2,1)}, bf16[272,512]{1,0:T(8,128)(2,1)S(1)}, u32[]{:S(2)}, u32[]{:S(2)}) collective-permute-start(bf16[272,512]{1,0:T(8,128)(2,1)} %collective-permute-done.7.rest_2_), channel_id=1, source_target_pairs={{0,224},{32,0},{64,32},{96,64},{128,96},{160,128},{192,160},{224,1... | collective-permute-start | bytes 835592 | tf_op jit(solution)/shard_map/ppermute | solution.py:30
  86.6 10.0 %collective-permute-start.14 = (bf16[144,512]{1,0:T(8,128)(2,1)S(1)}, bf16[144,512]{1,0:T(8,128)(2,1)S(1)}, u32[]{:S(2)}, u32[]{:S(2)}) collective-permute-start(bf16[144,512]{1,0:T(8,128)(2,1)S(1)} %slice.57), channel_id=1, source_target_pairs={{0,32},{32,64},{64,96},{96,128},{128,160},{160,192},{192,224},{224... | collective-permute-start | bytes 442376 | tf_op jit(solution)/shard_map/ppermute | solution.py:30
  88.6 8.1 %collective-permute-start.13 = (bf16[128,512]{1,0:T(8,128)(2,1)S(1)}, bf16[128,512]{1,0:T(8,128)(2,1)S(1)}, u32[]{:S(2)}, u32[]{:S(2)}) collective-permute-start(bf16[128,512]{1,0:T(8,128)(2,1)S(1)} %slice.56), channel_id=1, source_target_pairs={{0,224},{32,0},{64,32},{96,64},{128,96},{160,128},{192,160},{224,1... | collective-permute-start | bytes 393224 | tf_op jit(solution)/shard_map/ppermute | solution.py:30
  99.6 12.9 %collective-permute-start.15 = (bf16[1024,2176]{1,0:T(8,128)(2,1)}, bf16[1024,2176]{1,0:T(8,128)(2,1)S(1)}, u32[]{:S(2)}, u32[]{:S(2)}) collective-permute-start(bf16[1024,2176]{1,0:T(8,128)(2,1)} %all-gather.2.cloned.1.call-done), channel_id=1, source_target_pairs={{0,16},{16,0},{1,17},{17,1},{2,18},{18,2},{3,19},{19,3},{4,20},{20... | collective-permute-start | bytes 13369352 | tf_op jit(solution)/shard_map/ppermute | solution.py:26
  134.8 8.6 %collective-permute-start.19 = (f32[24,128]{1,0:T(8,128)S(1)}, f32[24,128]{1,0:T(8,128)S(1)}, u32[]{:S(2)}, u32[]{:S(2)}) collective-permute-start(f32[24,128]{1,0:T(8,128)S(1)} %add.54), channel_id=1, source_target_pairs={{0,128},{32,160},{64,192},{96,224},{128,0},{160,32},{192,64},{224,... | collective-permute-start | bytes 36872 | tf_op jit(solution)/shard_map/ppermute | solution.py:26
  148.2 5.7 %collective-permute-start.21 = (f32[24,128]{1,0:T(8,128)S(1)}, f32[24,128]{1,0:T(8,128)S(1)}, u32[]{:S(2)}, u32[]{:S(2)}) collective-permute-start(f32[24,128]{1,0:T(8,128)S(1)} %add.56), channel_id=1, source_target_pairs={{0,4},{2,6},{4,0},{6,2},{8,12},{10,14},{12,8},{14,10},{1,5},{3,7},... | collective-permute-start | bytes 36872 | tf_op jit(solution)/shard_map/ppermute | solution.py:26
  154.0 8.6 %collective-permute-start.22 = (f32[24,128]{1,0:T(8,128)S(1)}, f32[24,128]{1,0:T(8,128)S(1)}, u32[]{:S(2)}, u32[]{:S(2)}) collective-permute-start(f32[24,128]{1,0:T(8,128)S(1)} %add.57), channel_id=1, source_target_pairs={{0,8},{2,10},{4,12},{6,14},{8,0},{10,2},{12,4},{14,6},{1,9},{3,11}... | collective-permute-start | bytes 36872 | tf_op jit(solution)/shard_map/ppermute | solution.py:26
  167.5 5.9 %collective-permute-start.24 = (f32[24,128]{1,0:T(8,128)S(1)}, f32[24,128]{1,0:T(8,128)S(1)}, u32[]{:S(2)}, u32[]{:S(2)}) collective-permute-start(f32[24,128]{1,0:T(8,128)S(1)} %add.59), channel_id=1, source_target_pairs={{0,1},{1,0},{2,3},{3,2},{4,5},{5,4},{6,7},{7,6},{8,9},{9,8},{10,11... | collective-permute-start | bytes 36872 | tf_op jit(solution)/shard_map/ppermute | solution.py:26
  180.5 12.8 %collective-permute-start.25 = (f32[128,512]{1,0:T(8,128)S(1)}, f32[128,512]{1,0:T(8,128)S(1)}, u32[]{:S(2)}, u32[]{:S(2)}) collective-permute-start(f32[128,512]{1,0:T(8,128)S(1)} %get-tuple-element.58), channel_id=1, source_target_pairs={{0,0},{1,16},{16,1},{17,17},{256,256},{257,272},{272,257},{273,273... | collective-permute-start | bytes 786440 | tf_op jit(solution)/shard_map/ppermute | solution.py:313
  186.6 9.3 %collective-permute-start.26 = (f32[128,512]{1,0:T(8,128)S(1)}, f32[128,512]{1,0:T(8,128)S(1)}, u32[]{:S(2)}, u32[]{:S(2)}) collective-permute-start(f32[128,512]{1,0:T(8,128)S(1)} %get-tuple-element.57), channel_id=1, source_target_pairs={{0,256},{1,272},{16,257},{17,273},{256,0},{257,16},{272,1},{273,17... | collective-permute-start | bytes 786440 | tf_op jit(solution)/shard_map/ppermute | solution.py:313
  (14 other events, 153.3 us)
Sparse Core Ops, SparseCore 0:
  34.6 64.9 all-gather.1
  122.1 57.2 reduce-scatter.1
